TPU v7x, 128 devices: a whole 4x4x4 slice. The times are simulated.
128 devices in a mesh: blk: 32 (over y, z, x_lo), rep: 4 (over x_hi, core).
Axes of the slice: x: 4 (x_hi: 2, x_lo: 2; x = x_hi * 2 + x_lo), y: 4, z: 4, core: 2. Of those that a mesh axis runs over, the one named last changes fastest.
Arguments:
- features: bfloat16 [65536, 128], P('blk'), may hold values from -6 to 6
- node_order: int32 [32, 2048], P('blk'), may hold values from 0 to 2047, each once within a row
- adj_values: bfloat16 [32, 4, 8, 80, 128, 128], P('blk', 'rep'), may hold values from -0.0625 to 0.0625
- adj_rows: int32 [32, 4, 8, 80], P('blk', 'rep'), may hold values from 0 to 15, as said below
- adj_cols: int32 [32, 4, 8, 80], P('blk', 'rep'), may hold values from 0 to 15
- tile_count: int32 [32, 4, 8], P('blk', 'rep'), may hold values from 1 to 80, as said below
- weight: bfloat16 [128, 256], replicated, may hold values from -0.5 to 0.5
- upstream: bfloat16 [65536, 256], P(('blk', 'rep')), may hold values from -6 to 6
Outputs:
- activations: bfloat16 [65536, 256], P(('blk', 'rep'))
- grad_weight: float32 [128, 256], replicated
- grad_features: bfloat16 [65536, 128], P(('blk', 'rep'))
Inputs may be any that keep to these rules, and one draw needn't show every extreme that they name: Within each slot of a device the pairs (adj_rows, adj_cols) are all different. `tile_count`: tiles at positions at or beyond the count are absent. On some devices every slot holds 80 live tiles; on the others slots hold at most half of that.
All inputs are finite; a program needn't handle non-finite values.
Results may differ from a plain program's by a relative error of at most 0.025.
Values may be sent and summed in bfloat16 or wider, within the bound.
No kernel may reach another device: no remote copies, remote signals or barrier semaphores. Data moves between devices by JAX's collectives and lax.ppermute only.
A program may use at most 128 MiB of HBM per device.

v0:
```python
import jax
import jax.numpy as jnp
from jax import lax
from jax.sharding import PartitionSpec as P


def passed_along(value, axis, steps):
    count = lax.axis_size(axis)
    pairs = [(source, (source + steps) % count) for source in range(count)]
    return lax.ppermute(value, axis, pairs)


def rotate(values, direction):
    offset = lax.axis_index("rep")
    rep_count = lax.axis_size("rep")
    for bit_index in range(rep_count.bit_length() - 1):
        shifted = passed_along(values, "blk", direction * (1 << bit_index))
        values = jnp.where(offset // (1 << bit_index) % 2 == 1, shifted, values)
    return values


def replica_total(values):
    return lax.psum_scatter(
        values.astype(jnp.bfloat16), "rep", scatter_dimension=0, tiled=True
    ).astype(jnp.float32)


def per_device(features, node_order, adj_values, adj_rows, adj_cols, tile_count, weight, upstream):
    rep_count = lax.axis_size("rep")
    step_count = lax.axis_size("blk") // rep_count
    rows_dev, feat_in = features.shape
    tile_size = adj_values.shape[-1]
    block_count = rows_dev // tile_size
    per_slot = adj_values.shape[3]
    node_perm = node_order[0]
    tile_values = adj_values[0, 0]
    row_ids = adj_rows[0, 0]
    col_ids = adj_cols[0, 0]
    counts = tile_count[0, 0]
    slot_ids = jnp.arange(per_slot, dtype=jnp.int32)

    def live_part(product, slot_index):
        live_mask = (slot_ids < counts[slot_index]).astype(jnp.float32)
        return product * live_mask[:, None, None]

    blocked = jnp.take(features, node_perm, axis=0)
    current = rotate(blocked, -1)
    summed = jnp.zeros((block_count, tile_size, feat_in), jnp.float32)
    for slot_index in range(step_count):
        spread_picked = jnp.take(
            current.reshape(block_count, tile_size, feat_in), col_ids[slot_index], axis=0
        )
        spread_product = jnp.einsum(
            "ptk,pkf->ptf",
            tile_values[slot_index],
            spread_picked,
            preferred_element_type=jnp.float32,
        )
        spread_empty = jnp.zeros((block_count, tile_size, feat_in), jnp.float32)
        summed = summed + spread_empty.at[row_ids[slot_index]].add(
            live_part(spread_product, slot_index)
        )
        if slot_index + 1 < step_count:
            current = passed_along(current, "blk", -rep_count)
    shared = replica_total(summed.reshape(rows_dev, feat_in))
    aggregated = shared.astype(jnp.bfloat16)
    pre_sum = jnp.dot(aggregated, weight, preferred_element_type=jnp.float32)
    sigmoid_gate = jax.nn.sigmoid(pre_sum)
    activations = (pre_sum * sigmoid_gate).astype(jnp.bfloat16)
    grad_pre = (
        upstream.astype(jnp.float32) * sigmoid_gate * (1.0 + pre_sum * (1.0 - sigmoid_gate))
    ).astype(jnp.bfloat16)
    grad_local = lax.dot_general(
        aggregated, grad_pre, (((0,), (0,)), ((), ())), preferred_element_type=jnp.float32
    )
    grad_weight = lax.psum(grad_local, ("blk", "rep"))
    back_proj = lax.dot_general(
        grad_pre, weight, (((1,), (1,)), ((), ())), preferred_element_type=jnp.float32
    ).astype(jnp.bfloat16)
    own_rows = lax.all_gather(back_proj, "rep", axis=0, tiled=True).reshape(
        block_count, tile_size, feat_in
    )
    result = jnp.zeros((block_count, tile_size, feat_in), jnp.float32)
    for slot_index in reversed(range(step_count)):
        picked = jnp.take(own_rows, row_ids[slot_index], axis=0)
        gather_product = jnp.einsum(
            "ptk,ptf->pkf", tile_values[slot_index], picked, preferred_element_type=jnp.float32
        )
        empty = jnp.zeros((block_count, tile_size, feat_in), jnp.float32)
        result = result + empty.at[col_ids[slot_index]].add(live_part(gather_product, slot_index))
        if slot_index > 0:
            result = passed_along(result.astype(jnp.bfloat16), "blk", rep_count).astype(
                result.dtype
            )
    partial_value = result.reshape(rows_dev, feat_in).astype(jnp.bfloat16)
    partial_value = rotate(partial_value, 1)
    restored = jnp.zeros_like(partial_value).at[node_perm].set(partial_value)
    grad_features = replica_total(restored.astype(jnp.float32)).astype(jnp.bfloat16)
    return (activations, grad_weight, grad_features)


def solution(mesh):
    placed = (
        P("blk", None),
        P("blk", None),
        P("blk", "rep", None, None, None, None),
        P("blk", "rep", None, None),
        P("blk", "rep", None, None),
        P("blk", "rep", None),
        P(),
        P(("blk", "rep"), None),
    )
    return jax.shard_map(
        per_device,
        mesh=mesh,
        in_specs=placed,
        out_specs=(P(("blk", "rep"), None), P(), P(("blk", "rep"), None)),
        check_vma=False,
    )
```

profile of v0, /device:TPU:1, one launch (start us, length us, event | category | flops | bytes accessed | tf_op | source)
XLA Modules:
  0.0 799.7 jit_solution(15016416489853641191)
XLA Ops:
  9.3 6.2 gather_fusion
  15.9 8.0 %collective-permute-start = (bf16[2048,128]{1,0:T(8,128)(2,1)S(1)}, bf16[2048,128]{1,0:T(8,128)(2,1)S(1)}, u32[]{:S(2)}, u32[]{:S(2)}) collective-permute-start(bf16[2048,128]{1,0:T(8,128)(2,1)S(1)} %broadcast_select_fusion), channel_id=1, source_target_pairs={{0,124},{4,0},{8,4},{12,8},{16,12},{20,16},{24,20},{28,24},{32,28}... | collective-permute-start | bytes 1572872 | tf_op jit(solution)/shard_map/ppermute | solution.py:10
  23.9 10.6 %collective-permute-done = bf16[2048,128]{1,0:T(8,128)(2,1)S(1)} collective-permute-done((bf16[2048,128]{1,0:T(8,128)(2,1)S(1)}, bf16[2048,128]{1,0:T(8,128)(2,1)S(1)}, u32[]{:S(2)}, u32[]{:S(2)}) %collective-permute-start) | collective-permute-done | bytes 524320 | tf_op jit(solution)/shard_map/ppermute | solution.py:10
  39.3 7.4 collective-permute-done.1
  48.8 10.6 %collective-permute-done.2 = bf16[2048,128]{1,0:T(8,128)(2,1)S(1)} collective-permute-done((bf16[2048,128]{1,0:T(8,128)(2,1)S(1)}, bf16[2048,128]{1,0:T(8,128)(2,1)S(1)}, u32[]{:S(2)}, u32[]{:S(2)}) %collective-permute-start.2) | collective-permute-done | bytes 524320 | tf_op jit(solution)/shard_map/ppermute | solution.py:10
  63.3 7.6 collective-permute-done.3
  70.9 5.3 collective-permute-start.4
  76.9 6.2 collective-permute-done.4
  83.1 5.8 collective-permute-start.5
  92.1 6.9 multiply_bitcast_fusion.15
  99.1 6.0 copy.28
  105.1 10.9 %scatter_fusion = f32[16,128,128]{2,1,0:T(8,128)S(1)} fusion(f32[16,128,128]{2,1,0:T(8,128)S(1)} %broadcast.315.clone, s32[80]{0:T(128)S(1)} %get-tuple-element.80, f32[80,128,128]{2,1,0:T(8,128)} %copy.28), kind=kCustom, calls=%fused_computation.17 | custom fusion | flops 1310720 | bytes 15728960 | tf_op jit(solution)/shard_map/scatter-add | solution.py:60
  118.7 7.0 multiply_bitcast_fusion.14
  125.7 5.9 copy.30
  132.7 16.4 %scatter_fusion.1 = f32[16,128,128]{2,1,0:T(8,128)} fusion(f32[16,128,128]{2,1,0:T(8,128)} %broadcast.315.clone.1, s32[80]{0:T(128)S(1)} %get-tuple-element.79, f32[80,128,128]{2,1,0:T(8,128)} %copy.30), kind=kCustom, calls=%fused_computation.18 | custom fusion | flops 1310720 | bytes 15728960 | tf_op jit(solution)/shard_map/scatter-add | solution.py:60
  153.0 6.9 multiply_bitcast_fusion.13
  159.9 6.0 copy.32
  165.9 10.8 %scatter_fusion.2 = f32[16,128,128]{2,1,0:T(8,128)S(1)} fusion(f32[16,128,128]{2,1,0:T(8,128)S(1)} %add.284, s32[80]{0:T(128)S(1)} %get-tuple-element.78, f32[80,128,128]{2,1,0:T(8,128)} %copy.32), kind=kCustom, calls=%fused_computation.19 | custom fusion | flops 1310720 | bytes 15728960 | tf_op jit(solution)/shard_map/scatter-add | solution.py:60
  179.6 7.0 multiply_bitcast_fusion.12
  186.5 5.9 copy.34
  193.6 16.4 %scatter_fusion.3 = f32[16,128,128]{2,1,0:T(8,128)} fusion(f32[16,128,128]{2,1,0:T(8,128)} %broadcast.315.clone.2, s32[80]{0:T(128)S(1)} %get-tuple-element.77, f32[80,128,128]{2,1,0:T(8,128)} %copy.34), kind=kCustom, calls=%fused_computation.20 | custom fusion | flops 1310720 | bytes 15728960 | tf_op jit(solution)/shard_map/scatter-add | solution.py:60
  214.9 6.9 multiply_bitcast_fusion.11
  221.8 6.0 copy.36
  227.8 10.9 %scatter_fusion.4 = f32[16,128,128]{2,1,0:T(8,128)S(1)} fusion(f32[16,128,128]{2,1,0:T(8,128)S(1)} %add.287, s32[80]{0:T(128)S(1)} %get-tuple-element.76, f32[80,128,128]{2,1,0:T(8,128)} %copy.36), kind=kCustom, calls=%fused_computation.21 | custom fusion | flops 1310720 | bytes 15728960 | tf_op jit(solution)/shard_map/scatter-add | solution.py:60
  242.7 7.0 multiply_bitcast_fusion.10
  249.7 5.9 copy.38
  256.7 16.6 %scatter_fusion.5 = f32[16,128,128]{2,1,0:T(8,128)} fusion(f32[16,128,128]{2,1,0:T(8,128)} %broadcast.315.clone.3, s32[80]{0:T(128)S(1)} %get-tuple-element.75, f32[80,128,128]{2,1,0:T(8,128)} %copy.38), kind=kCustom, calls=%fused_computation.22 | custom fusion | flops 1310720 | bytes 15728960 | tf_op jit(solution)/shard_map/scatter-add | solution.py:60
  277.2 6.9 multiply_bitcast_fusion.9
  284.1 6.0 copy.40
  290.0 10.9 %scatter_fusion.6 = f32[16,128,128]{2,1,0:T(8,128)S(1)} fusion(f32[16,128,128]{2,1,0:T(8,128)S(1)} %add.290, s32[80]{0:T(128)S(1)} %get-tuple-element.81, f32[80,128,128]{2,1,0:T(8,128)} %copy.40), kind=kCustom, calls=%fused_computation.23 | custom fusion | flops 1310720 | bytes 15728960 | tf_op jit(solution)/shard_map/scatter-add | solution.py:60
  303.5 6.9 multiply_bitcast_fusion.8
  310.4 6.0 copy.42
  316.4 10.9 %scatter_fusion.7 = f32[16,128,128]{2,1,0:T(8,128)S(1)} fusion(f32[16,128,128]{2,1,0:T(8,128)S(1)} %broadcast.315.clone.4, s32[80]{0:T(128)S(1)} %get-tuple-element.74, f32[80,128,128]{2,1,0:T(8,128)} %copy.42), kind=kCustom, calls=%fused_computation.24 | custom fusion | flops 1310720 | bytes 15728960 | tf_op jit(solution)/shard_map/scatter-add | solution.py:60
  328.4 44.7 %reduce-scatter.3.cloned.1.call-done = bf16[512,128]{1,0:T(8,128)(2,1)} async-done(((bf16[2048,128]{1,0:T(8,128)(2,1)}), bf16[512,128]{1,0:T(8,128)(2,1)}) %reduce-scatter.3.cloned.1.call-update) | async-done | bytes 131088 | tf_op jit(solution)/shard_map/reduce_scatter | solution.py:23
  375.3 9.0 %all_gather.3 = bf16[2048,128]{1,0:T(8,128)(2,1)S(1)} all-gather(bf16[512,128]{1,0:T(8,128)(2,1)S(1)} %convolution_convert_fusion), channel_id=1, replica_groups=mesh['blk'=32,'rep'=4] {'rep'}, dimensions={0}, use_global_device_ids=true | all-gather | bytes 655360 | tf_op jit(solution)/shard_map/all_gather | solution.py:80
  385.3 5.4 multiply_bitcast_fusion.7
  390.8 6.0 copy.44
  396.8 10.9 %scatter_fusion.8 = f32[16,128,128]{2,1,0:T(8,128)S(1)} fusion(f32[16,128,128]{2,1,0:T(8,128)S(1)} %broadcast.315, s32[80]{0:T(128)S(1)} %get-tuple-element.59, f32[80,128,128]{2,1,0:T(8,128)} %copy.44), kind=kCustom, calls=%fused_computation.25 | custom fusion | flops 1310720 | bytes 15728960 | tf_op jit(solution)/shard_map/scatter-add | solution.py:90
  412.5 5.5 multiply_bitcast_fusion.6
  418.0 5.9 copy.46
  427.0 10.8 %scatter_fusion.9 = f32[16,128,128]{2,1,0:T(8,128)S(1)} fusion(f32[16,128,128]{2,1,0:T(8,128)S(1)} %convert_element_type.151, s32[80]{0:T(128)S(1)} %get-tuple-element.58, f32[80,128,128]{2,1,0:T(8,128)} %copy.46), kind=kCustom, calls=%fused_computation.26 | custom fusion | flops 1310720 | bytes 15728960 | tf_op jit(solution)/shard_map/scatter-add | solution.py:90
  440.6 5.5 multiply_bitcast_fusion.5
  446.1 5.9 copy.48
  456.3 10.9 %scatter_fusion.10 = f32[16,128,128]{2,1,0:T(8,128)S(1)} fusion(f32[16,128,128]{2,1,0:T(8,128)S(1)} %convert_element_type.153, s32[80]{0:T(128)S(1)} %get-tuple-element.57, f32[80,128,128]{2,1,0:T(8,128)} %copy.48), kind=kCustom, calls=%fused_computation.27 | custom fusion | flops 1310720 | bytes 15728960 | tf_op jit(solution)/shard_map/scatter-add | solution.py:90
  469.4 5.5 multiply_bitcast_fusion.4
  474.9 5.9 copy.50
  484.9 10.9 %scatter_fusion.11 = f32[16,128,128]{2,1,0:T(8,128)S(1)} fusion(f32[16,128,128]{2,1,0:T(8,128)S(1)} %convert_element_type.155, s32[80]{0:T(128)S(1)} %get-tuple-element.56, f32[80,128,128]{2,1,0:T(8,128)} %copy.50), kind=kCustom, calls=%fused_computation.28 | custom fusion | flops 1310720 | bytes 15728960 | tf_op jit(solution)/shard_map/scatter-add | solution.py:90
  497.8 5.5 multiply_bitcast_fusion.3
  503.2 5.9 copy.52
  512.4 10.8 %scatter_fusion.12 = f32[16,128,128]{2,1,0:T(8,128)S(1)} fusion(f32[16,128,128]{2,1,0:T(8,128)S(1)} %convert_element_type.157, s32[80]{0:T(128)S(1)} %get-tuple-element.55, f32[80,128,128]{2,1,0:T(8,128)} %copy.52), kind=kCustom, calls=%fused_computation.29 | custom fusion | flops 1310720 | bytes 15728960 | tf_op jit(solution)/shard_map/scatter-add | solution.py:90
  525.2 5.5 multiply_bitcast_fusion.2
  530.7 5.9 copy.54
  538.9 10.9 %scatter_fusion.13 = f32[16,128,128]{2,1,0:T(8,128)S(1)} fusion(f32[16,128,128]{2,1,0:T(8,128)S(1)} %convert_element_type.159, s32[80]{0:T(128)S(1)} %get-tuple-element.54, f32[80,128,128]{2,1,0:T(8,128)} %copy.54), kind=kCustom, calls=%fused_computation.30 | custom fusion | flops 1310720 | bytes 15728960 | tf_op jit(solution)/shard_map/scatter-add | solution.py:90
  552.0 5.5 multiply_bitcast_fusion.1
  557.5 5.9 copy.56
  564.7 10.9 %scatter_fusion.14 = f32[16,128,128]{2,1,0:T(8,128)S(1)} fusion(f32[16,128,128]{2,1,0:T(8,128)S(1)} %convert_element_type.161, s32[80]{0:T(128)S(1)} %get-tuple-element.53, f32[80,128,128]{2,1,0:T(8,128)} %copy.56), kind=kCustom, calls=%fused_computation.31 | custom fusion | flops 1310720 | bytes 15728960 | tf_op jit(solution)/shard_map/scatter-add | solution.py:90
  578.3 5.5 multiply_bitcast_fusion
  583.8 5.9 copy.58
  590.9 10.9 %scatter_fusion.15 = f32[16,128,128]{2,1,0:T(8,128)S(1)} fusion(f32[16,128,128]{2,1,0:T(8,128)S(1)} %convert_element_type.163, s32[80]{0:T(128)S(1)} %get-tuple-element.52, f32[80,128,128]{2,1,0:T(8,128)} %copy.58), kind=kCustom, calls=%fused_computation.32 | custom fusion | flops 1310720 | bytes 15728960 | tf_op jit(solution)/shard_map/scatter-add | solution.py:90
  602.2 12.0 %collective-permute-done.16 = bf16[2048,128]{1,0:T(8,128)(2,1)S(1)} collective-permute-done((bf16[2048,128]{1,0:T(8,128)(2,1)S(1)}, bf16[2048,128]{1,0:T(8,128)(2,1)S(1)}, u32[]{:S(2)}, u32[]{:S(2)}) %collective-permute-start.16) | collective-permute-done | bytes 524320 | tf_op jit(solution)/shard_map/ppermute | solution.py:10
  615.3 10.4 %collective-permute-done.17 = bf16[2048,128]{1,0:T(8,128)(2,1)S(1)} collective-permute-done((bf16[2048,128]{1,0:T(8,128)(2,1)S(1)}, bf16[2048,128]{1,0:T(8,128)(2,1)S(1)}, u32[]{:S(2)}, u32[]{:S(2)}) %collective-permute-start.17) | collective-permute-done | bytes 524320 | tf_op jit(solution)/shard_map/ppermute | solution.py:10
  625.7 6.6 scatter_custom_fusion.16
  632.4 129.6 %all-reduce.2.cloned.1.call-done = f32[128,256]{1,0:T(8,128)} async-done(((f32[128,256]{1,0:T(8,128)}), f32[128,256]{1,0:T(8,128)}) %all-reduce.2.cloned.1.call-update) | async-done | bytes 131088 | tf_op jit(solution)/shard_map/psum | solution.py:76
  762.0 29.1 %reduce-scatter.5.cloned.1.call-done = bf16[512,128]{1,0:T(8,128)(2,1)} async-done(((bf16[2048,128]{1,0:T(8,128)(2,1)}), bf16[512,128]{1,0:T(8,128)(2,1)}) %reduce-scatter.5.cloned.1.call-update) | async-done | bytes 131088 | tf_op jit(solution)/shard_map/reduce_scatter | solution.py:23
  (139 shorter events, 90.8 us)
Async XLA Ops:
  7.2 2.1 copy-start
  7.2 365.9 %reduce-scatter.3.cloned.1.call-start = ((), (), s32[]{:S(2)}) async-start(), calls=%async_computation.2 | async-start | bytes 655360 | tf_op jit(solution)/shard_map/reduce_scatter | solution.py:23
  8.0 0.6 copy-start.6
  9.3 26.9 %copy-start.7 = (s32[1,1,8]{2,1,0:T(1,128)S(1)}, s32[1,1,8]{2,1,0:T(1,128)}, u32[]{:S(2)}) copy-start(s32[1,1,8]{2,1,0:T(1,128)} %param.15) | copy-start | bytes 100
  15.5 33.2 %copy-start.9 = (s32[1,1,8,80]{3,2,1,0:T(8,128)S(1)}, s32[1,1,8,80]{3,2,1,0:T(8,128)}, u32[]{:S(2)}) copy-start(s32[1,1,8,80]{3,2,1,0:T(8,128)} %param.14) | copy-start | bytes 7684
  15.5 61.4 %copy-start.8 = (s32[1,1,8,80]{3,2,1,0:T(8,128)S(1)}, s32[1,1,8,80]{3,2,1,0:T(8,128)}, u32[]{:S(2)}) copy-start(s32[1,1,8,80]{3,2,1,0:T(8,128)} %param.13) | copy-start | bytes 7684
  15.9 18.6 %collective-permute-start = (bf16[2048,128]{1,0:T(8,128)(2,1)S(1)}, bf16[2048,128]{1,0:T(8,128)(2,1)S(1)}, u32[]{:S(2)}, u32[]{:S(2)}) collective-permute-start(bf16[2048,128]{1,0:T(8,128)(2,1)S(1)} %broadcast_select_fusion), channel_id=1, source_target_pairs={{0,124},{4,0},{8,4},{12,8},{16,12},{20,16},{24,20},{28,24},{32,28}... | collective-permute-start | bytes 1572872 | tf_op jit(solution)/shard_map/ppermute | solution.py:10
  34.8 11.9 %collective-permute-start.1 = (bf16[2048,128]{1,0:T(8,128)(2,1)S(1)}, bf16[2048,128]{1,0:T(8,128)(2,1)S(1)}, u32[]{:S(2)}, u32[]{:S(2)}) collective-permute-start(bf16[2048,128]{1,0:T(8,128)(2,1)S(1)} %broadcast_select_fusion.2), channel_id=1, source_target_pairs={{0,120},{4,124},{8,0},{12,4},{16,8},{20,12},{24,16},{28,20},{32,24... | collective-permute-start | bytes 1572872 | tf_op jit(solution)/shard_map/ppermute | solution.py:10
  37.5 81.2 %copy-start.12 = (f32[80]{0:T(128)}, f32[80]{0:T(128)S(1)}, u32[]{:S(2)}) copy-start(f32[80]{0:T(128)S(1)} %compare_convert_fusion.6) | copy-start | bytes 964
  38.1 54.0 %copy-start.10 = (f32[80]{0:T(128)}, f32[80]{0:T(128)S(1)}, u32[]{:S(2)}) copy-start(f32[80]{0:T(128)S(1)} %compare_convert_fusion.7) | copy-start | bytes 964
  46.8 12.5 %collective-permute-start.2 = (bf16[2048,128]{1,0:T(8,128)(2,1)S(1)}, bf16[2048,128]{1,0:T(8,128)(2,1)S(1)}, u32[]{:S(2)}, u32[]{:S(2)}) collective-permute-start(bf16[2048,128]{1,0:T(8,128)(2,1)S(1)} %broadcast_select_fusion.3), channel_id=1, source_target_pairs={{0,112},{4,116},{8,120},{12,124},{16,0},{20,4},{24,8},{28,12},{32,... | collective-permute-start | bytes 1572872 | tf_op jit(solution)/shard_map/ppermute | solution.py:10
  59.4 11.5 %collective-permute-start.3 = (bf16[2048,128]{1,0:T(8,128)(2,1)S(1)}, bf16[2048,128]{1,0:T(8,128)(2,1)S(1)}, u32[]{:S(2)}, u32[]{:S(2)}) collective-permute-start(bf16[2048,128]{1,0:T(8,128)(2,1)S(1)} %collective-permute-done.2), channel_id=1, source_target_pairs={{0,112},{4,116},{8,120},{12,124},{16,0},{20,4},{24,8},{28,12},{32,... | collective-permute-start | bytes 1572872 | tf_op jit(solution)/shard_map/ppermute | solution.py:10
  70.9 12.2 %collective-permute-start.4 = (bf16[2048,128]{1,0:T(8,128)(2,1)S(1)}, bf16[2048,128]{1,0:T(8,128)(2,1)S(1)}, u32[]{:S(2)}, u32[]{:S(2)}) collective-permute-start(bf16[2048,128]{1,0:T(8,128)(2,1)S(1)} %collective-permute-done.3), channel_id=1, source_target_pairs={{0,112},{4,116},{8,120},{12,124},{16,0},{20,4},{24,8},{28,12},{32,... | collective-permute-start | bytes 1572872 | tf_op jit(solution)/shard_map/ppermute | solution.py:10
  83.1 9.0 %copy-start.2 = (bf16[2048,128]{1,0:T(8,128)(2,1)}, bf16[2048,128]{1,0:T(8,128)(2,1)S(1)}, u32[]{:S(2)}) copy-start(bf16[2048,128]{1,0:T(8,128)(2,1)S(1)} %collective-permute-done.4) | copy-start | bytes 1572868
  83.1 35.4 %collective-permute-start.5 = (bf16[2048,128]{1,0:T(8,128)(2,1)S(1)}, bf16[2048,128]{1,0:T(8,128)(2,1)}, u32[]{:S(2)}, u32[]{:S(2)}) collective-permute-start(bf16[2048,128]{1,0:T(8,128)(2,1)S(1)} %collective-permute-done.4), channel_id=1, source_target_pairs={{0,112},{4,116},{8,120},{12,124},{16,0},{20,4},{24,8},{28,12},{32,... | collective-permute-start | bytes 1572872 | tf_op jit(solution)/shard_map/ppermute | solution.py:10
  118.5 60.8 %collective-permute-start.6 = (bf16[2048,128]{1,0:T(8,128)(2,1)}, bf16[2048,128]{1,0:T(8,128)(2,1)}, u32[]{:S(2)}, u32[]{:S(2)}) collective-permute-start(bf16[2048,128]{1,0:T(8,128)(2,1)} %collective-permute-done.5), channel_id=1, source_target_pairs={{0,112},{4,116},{8,120},{12,124},{16,0},{20,4},{24,8},{28,12},{32,... | collective-permute-start | bytes 1572872 | tf_op jit(solution)/shard_map/ppermute | solution.py:10
  165.9 10.9 %copy-start.3 = (bf16[2048,128]{1,0:T(8,128)(2,1)S(1)}, bf16[2048,128]{1,0:T(8,128)(2,1)}, u32[]{:S(2)}) copy-start(bf16[2048,128]{1,0:T(8,128)(2,1)} %copy-done.2) | copy-start | bytes 1572868
  179.3 62.9 %collective-permute-start.7 = (bf16[2048,128]{1,0:T(8,128)(2,1)}, bf16[2048,128]{1,0:T(8,128)(2,1)S(1)}, u32[]{:S(2)}, u32[]{:S(2)}) collective-permute-start(bf16[2048,128]{1,0:T(8,128)(2,1)} %collective-permute-done.6), channel_id=1, source_target_pairs={{0,112},{4,116},{8,120},{12,124},{16,0},{20,4},{24,8},{28,12},{32,... | collective-permute-start | bytes 1572872 | tf_op jit(solution)/shard_map/ppermute | solution.py:10
  242.2 58.7 %collective-permute-start.8 = (bf16[2048,128]{1,0:T(8,128)(2,1)S(1)}, bf16[2048,128]{1,0:T(8,128)(2,1)S(1)}, u32[]{:S(2)}, u32[]{:S(2)}) collective-permute-start(bf16[2048,128]{1,0:T(8,128)(2,1)S(1)} %collective-permute-done.7), channel_id=1, source_target_pairs={{0,112},{4,116},{8,120},{12,124},{16,0},{20,4},{24,8},{28,12},{32,... | collective-permute-start | bytes 1572872 | tf_op jit(solution)/shard_map/ppermute | solution.py:10
  327.3 45.8 %copy-start.5 = (bf16[128,256]{1,0:T(8,128)(2,1)S(1)}, bf16[128,256]{1,0:T(8,128)(2,1)}, u32[]{:S(2)}) copy-start(bf16[128,256]{1,0:T(8,128)(2,1)} %param.16) | copy-start | bytes 196612
  327.3 45.8 %copy-start.14 = (bf16[512,256]{1,0:T(8,128)(2,1)S(1)}, bf16[512,256]{1,0:T(8,128)(2,1)}, u32[]{:S(2)}) copy-start(bf16[512,256]{1,0:T(8,128)(2,1)} %param.17) | copy-start | bytes 786436
  328.3 433.7 %all-reduce.2.cloned.1.call-start = ((), (), s32[]{:S(2)}) async-start(), calls=%async_computation.3 | async-start | bytes 262144 | tf_op jit(solution)/shard_map/psum | solution.py:76
  408.6 17.3 %collective-permute-start.9 = (bf16[16,128,128]{2,1,0:T(8,128)(2,1)}, bf16[16,128,128]{2,1,0:T(8,128)(2,1)}, u32[]{:S(2)}, u32[]{:S(2)}) collective-permute-start(bf16[16,128,128]{2,1,0:T(8,128)(2,1)} %convert_element_type.150), channel_id=1, source_target_pairs={{0,16},{4,20},{8,24},{12,28},{16,32},{20,36},{24,40},{28,44},{32,4... | collective-permute-start | bytes 1572872 | tf_op jit(solution)/shard_map/ppermute | solution.py:10
  438.8 16.4 %collective-permute-start.10 = (bf16[16,128,128]{2,1,0:T(8,128)(2,1)}, bf16[16,128,128]{2,1,0:T(8,128)(2,1)}, u32[]{:S(2)}, u32[]{:S(2)}) collective-permute-start(bf16[16,128,128]{2,1,0:T(8,128)(2,1)} %convert_element_type.152), channel_id=1, source_target_pairs={{0,16},{4,20},{8,24},{12,28},{16,32},{20,36},{24,40},{28,44},{32,4... | collective-permute-start | bytes 1572872 | tf_op jit(solution)/shard_map/ppermute | solution.py:10
  468.1 15.6 %collective-permute-start.11 = (bf16[16,128,128]{2,1,0:T(8,128)(2,1)}, bf16[16,128,128]{2,1,0:T(8,128)(2,1)}, u32[]{:S(2)}, u32[]{:S(2)}) collective-permute-start(bf16[16,128,128]{2,1,0:T(8,128)(2,1)} %convert_element_type.154), channel_id=1, source_target_pairs={{0,16},{4,20},{8,24},{12,28},{16,32},{20,36},{24,40},{28,44},{32,4... | collective-permute-start | bytes 1572872 | tf_op jit(solution)/shard_map/ppermute | solution.py:10
  496.7 14.5 %collective-permute-start.12 = (bf16[16,128,128]{2,1,0:T(8,128)(2,1)}, bf16[16,128,128]{2,1,0:T(8,128)(2,1)}, u32[]{:S(2)}, u32[]{:S(2)}) collective-permute-start(bf16[16,128,128]{2,1,0:T(8,128)(2,1)} %convert_element_type.156), channel_id=1, source_target_pairs={{0,16},{4,20},{8,24},{12,28},{16,32},{20,36},{24,40},{28,44},{32,4... | collective-permute-start | bytes 1572872 | tf_op jit(solution)/shard_map/ppermute | solution.py:10
  524.1 13.6 %collective-permute-start.13 = (bf16[16,128,128]{2,1,0:T(8,128)(2,1)}, bf16[16,128,128]{2,1,0:T(8,128)(2,1)}, u32[]{:S(2)}, u32[]{:S(2)}) collective-permute-start(bf16[16,128,128]{2,1,0:T(8,128)(2,1)} %convert_element_type.158), channel_id=1, source_target_pairs={{0,16},{4,20},{8,24},{12,28},{16,32},{20,36},{24,40},{28,44},{32,4... | collective-permute-start | bytes 1572872 | tf_op jit(solution)/shard_map/ppermute | solution.py:10
  550.7 12.9 %collective-permute-start.14 = (bf16[16,128,128]{2,1,0:T(8,128)(2,1)}, bf16[16,128,128]{2,1,0:T(8,128)(2,1)}, u32[]{:S(2)}, u32[]{:S(2)}) collective-permute-start(bf16[16,128,128]{2,1,0:T(8,128)(2,1)} %convert_element_type.160), channel_id=1, source_target_pairs={{0,16},{4,20},{8,24},{12,28},{16,32},{20,36},{24,40},{28,44},{32,4... | collective-permute-start | bytes 1572872 | tf_op jit(solution)/shard_map/ppermute | solution.py:10
  550.9 1.1 copy-start.13
  576.5 13.3 %collective-permute-start.15 = (bf16[16,128,128]{2,1,0:T(8,128)(2,1)}, bf16[16,128,128]{2,1,0:T(8,128)(2,1)}, u32[]{:S(2)}, u32[]{:S(2)}) collective-permute-start(bf16[16,128,128]{2,1,0:T(8,128)(2,1)} %convert_element_type.162), channel_id=1, source_target_pairs={{0,16},{4,20},{8,24},{12,28},{16,32},{20,36},{24,40},{28,44},{32,4... | collective-permute-start | bytes 1572872 | tf_op jit(solution)/shard_map/ppermute | solution.py:10
  577.3 1.1 copy-start.11
  601.8 12.6 %copy-start.4 = (bf16[512,128]{1,0:T(8,128)(2,1)S(1)}, bf16[512,128]{1,0:T(8,128)(2,1)}, u32[]{:S(2)}) copy-start(bf16[512,128]{1,0:T(8,128)(2,1)} %reduce-scatter.3.cloned.1.call-done) | copy-start | bytes 393220
  601.8 190.9 %copy-start.1 = (bf16[2048,128]{1,0:T(8,128)(2,1)S(1)}, bf16[2048,128]{1,0:T(8,128)(2,1)}, u32[]{:S(2)}) copy-start(bf16[2048,128]{1,0:T(8,128)(2,1)} %param.10) | copy-start | bytes 1572868
  601.9 12.3 %collective-permute-start.16 = (bf16[2048,128]{1,0:T(8,128)(2,1)S(1)}, bf16[2048,128]{1,0:T(8,128)(2,1)S(1)}, u32[]{:S(2)}, u32[]{:S(2)}) collective-permute-start(bf16[2048,128]{1,0:T(8,128)(2,1)S(1)} %bitcast.261), channel_id=1, source_target_pairs={{0,4},{4,8},{8,12},{12,16},{16,20},{20,24},{24,28},{28,32},{32,36}... | collective-permute-start | bytes 1572872 | tf_op jit(solution)/shard_map/ppermute | solution.py:10
  614.3 11.5 %collective-permute-start.17 = (bf16[2048,128]{1,0:T(8,128)(2,1)S(1)}, bf16[2048,128]{1,0:T(8,128)(2,1)S(1)}, u32[]{:S(2)}, u32[]{:S(2)}) collective-permute-start(bf16[2048,128]{1,0:T(8,128)(2,1)S(1)} %broadcast_select_fusion.1), channel_id=1, source_target_pairs={{0,8},{4,12},{8,16},{12,20},{16,24},{20,28},{24,32},{28,36},{32,40... | collective-permute-start | bytes 1572872 | tf_op jit(solution)/shard_map/ppermute | solution.py:10
  615.3 175.9 %reduce-scatter.5.cloned.1.call-start = ((), (), s32[]{:S(2)}) async-start(), calls=%async_computation.4 | async-start | bytes 655360 | tf_op jit(solution)/shard_map/reduce_scatter | solution.py:23
Sparse Core Ops, SparseCore 0:
  328.4 44.6 reduce-scatter.2
  615.4 146.5 all-reduce.1
  765.2 25.9 reduce-scatter.4
where the time goes:
time: 811 us; the launch traced here: 800 us
  waiting for transfers between devices  280 us (35%)
  other arithmetic  224 us (28%)
  local copies, waits for them, and re-layouts  139 us (17%)
  matrix products  102 us (13%)
  starting transfers between devices  31.2 us (4%)
  between operations  14.9 us (2%)
  blocking collectives  8.97 us (1%)
    psum x1, waiting for transfers between devices, per_device(): grad_weight = lax.psum(grad_local, ('blk', 'rep'))  130 us
    scatter-add x8, other arithmetic, per_device(): spread_empty.at[row_ids[slot_index]]  104 us
    mul x16, local copies, waits for them, and re-layouts, live_part(): return product * live_mask[:, None, None]  94.9 us
    scatter-add x8, other arithmetic, per_device(): empty.at[col_ids[slot_index]].add(live_part(gather_product, slot_index))  86.8 us
    ppermute x18, waiting for transfers between devices, passed_along(): return lax.ppermute(value, axis, pairs)  76.2 us
    reduce_scatter x2, waiting for transfers between devices, replica_total(): lax.psum_scatter(values.astype(jnp.bfloat16), 'rep', scatter_dimension=0,...  73.8 us
    dot_general x8, matrix products, per_device(): jnp.einsum('ptk,pkf->ptf', tile_values[slot_index], spread_picked, prefer...  55.5 us
    dot_general x8, matrix products, per_device(): jnp.einsum('ptk,ptf->pkf', tile_values[slot_index], picked, preferred_ele...  43.8 us
  transfers between devices with their start and end apart: 21, of which 16 were waited for; matrix products, arithmetic and copies ran while one was open for 39% of the time, Pallas kernels for 0%

commit v1 on v0

v1 whole, which is shorter than its diff:
```python
import functools

import jax
import jax.numpy as jnp
import numpy as np
from jax import lax
from jax.experimental import pallas as pl
from jax.experimental.pallas import tpu as pltpu
from jax.sharding import PartitionSpec as P

TILE = 128
FORWARD_TURN = 4
BACKWARD_TURN = 8
FORWARD_WIDTH = 8
BACKWARD_WIDTH = 4
FORWARD_WAVES = ((0, 1, 3, 2), (4, 5, 7, 6))
BACKWARD_WAVES = ((4, 5, 6, 7), (0, 1, 2, 3))
PAIR = 2
CODE = 256
VMEM_LIMIT = 12 * 1024 * 1024
HOLD_LIMIT = 32 * 1024 * 1024


def spots():
    return [(x, y, z, c) for x in range(4) for y in range(4) for z in range(4) for c in range(2)]


def coords(x, y, z, c):
    return 8 * y + 2 * z + x % 2, x // 2 * 2 + c


def device(x, y, z, c):
    blk, rep = coords(x % 4, y % 4, z % 4, c)
    return 4 * blk + rep


def levels(x, y, z, c):
    kind = sum(coords(x, y, z, c)) % 4
    level = z if kind // 2 == z % 2 else z + 1
    return kind % 2, (level + 2 * c) % 4, (level + 2 - 2 * c) % 4


def slot_table():
    table = np.zeros((128, 8), np.int32)
    for spot in spots():
        low, near, far = levels(*spot)
        base = sum(coords(*spot))
        for item in range(8):
            row = (spot[1] + item) % 4
            wanted = 8 * row + 2 * (near if item < 4 else far) + low
            table[device(*spot), item] = (wanted - base) % 32 // 4
    return table


def fetch_pairs():
    listed = []
    for x, y, z, c in spots():
        near = levels(x, y, z, c)[1]
        listed.append((device(x - c, y, near, c), device(x, y, z, c)))
    return listed


def partner_pairs():
    return [(device(x, y, z, c), device(x + 2 * c - 1, y, z, 1 - c)) for x, y, z, c in spots()]


def blk_steps():
    near, across = (1, 0, 3, 2), (3, 2, 1, 0)
    return [
        [(device(x, y, z, c), device(x, ring[y], z, c)) for x, y, z, c in spots()]
        for ring in (near, across)
    ] + [
        [(device(x, y, z, c), device(x, y, ring[z], c)) for x, y, z, c in spots()]
        for ring in (near, across)
    ] + [
        [(device(x, y, z, c), device(near[x], y, z, c)) for x, y, z, c in spots()]
    ]


def ring_pairs(step):
    return [(device(x, y, z, c), device(x, y + step, z, c)) for x, y, z, c in spots()]


def params(limit=VMEM_LIMIT):
    return pltpu.CompilerParams(vmem_limit_bytes=limit)


def whole():
    return pl.BlockSpec(memory_space=pltpu.VMEM)


def order_kernel(order_ref, feat_ref, out_ref):
    rows = feat_ref.shape[0]
    step = 512
    feats = feat_ref[...]
    for start in range(0, rows, step):
        parts = []
        for inner in range(start, start + step, TILE):
            line = order_ref[0:1, inner : inner + TILE]
            parts.append(jnp.broadcast_to(line, (TILE, TILE)).T)
        column = jnp.concatenate(parts, axis=0)
        pieces = []
        for col in range(0, rows, TILE):
            level = lax.broadcasted_iota(jnp.int32, (step, TILE), 1) + col
            pieces.append((column == level).astype(jnp.float32).astype(jnp.bfloat16))
        pick = jnp.concatenate(pieces, axis=1)
        out_ref[start : start + step, :] = jnp.dot(
            pick, feats, preferred_element_type=jnp.float32
        ).astype(jnp.bfloat16)


def order_rows(order, features):
    return pl.pallas_call(
        order_kernel,
        out_shape=jax.ShapeDtypeStruct(features.shape, jnp.bfloat16),
        in_specs=[whole(), whole()],
        out_specs=whole(),
        compiler_params=params(),
    )(order, features)


def hold_kernel(items, place_ref, tiles_ref, out_ref, sems):
    per_slot = out_ref.shape[0] // len(items)
    copies = []
    for number, item in enumerate(items):
        copies.append(
            pltpu.make_async_copy(
                tiles_ref.at[pl.ds(place_ref[1 + item] * per_slot, per_slot)],
                out_ref.at[pl.ds(number * per_slot, per_slot)],
                sems.at[number],
            )
        )
        copies[-1].start()
    for copy in copies:
        copy.wait()


def hold(items, place, tiles, per_slot):
    size = len(items) * per_slot
    return pl.pallas_call(
        functools.partial(hold_kernel, items),
        out_shape=jax.ShapeDtypeStruct((size, TILE, TILE), tiles.dtype),
        grid_spec=pltpu.PrefetchScalarGridSpec(
            num_scalar_prefetch=1,
            grid=(),
            in_specs=[pl.BlockSpec(memory_space=pltpu.HBM)],
            out_specs=whole(),
            scratch_shapes=[pltpu.SemaphoreType.DMA((len(items),))],
        ),
        compiler_params=params(HOLD_LIMIT),
        cost_estimate=pl.CostEstimate(
            flops=0, bytes_accessed=4 * size * TILE * TILE, transcendentals=0
        ),
    )(place, tiles)


def tile_lists(key, source, target_count, zero, width, turn):
    lists, size = key.shape
    capacity = (size + target_count * (width - 1)) // width
    capacity = -(-capacity // turn) * turn
    ids = jnp.arange(size, dtype=jnp.int32)
    levels = jnp.arange(target_count, dtype=jnp.int32)
    earlier = (key[:, None, :] == key[:, :, None]) & (ids[None, :] < ids[:, None])
    rank = jnp.sum(earlier.astype(jnp.int32), axis=2)
    held = jnp.sum((key[:, None, :] == levels[:, None]).astype(jnp.int32), axis=2)
    needed = (held + width - 1) // width
    upto = levels[None, :] <= levels[:, None]
    ends = jnp.sum(jnp.where(upto, needed[:, None, :], 0), axis=2)
    base = jnp.sum(jnp.where(levels < key[:, :, None], needed[:, None, :], 0), axis=2)
    place = jnp.where(key < target_count, base * width + rank, -1)
    cells = jnp.arange(capacity * width, dtype=jnp.int32)
    hit = (place[:, None, :] == cells[:, None]).astype(jnp.int32)
    tile = jnp.sum(hit * ids, axis=2)
    origin = zero + jnp.sum(hit * (source - zero)[:, None, :], axis=2)
    groups = jnp.arange(capacity, dtype=jnp.int32)
    target = jnp.sum((ends[:, None, :] <= groups[:, None]).astype(jnp.int32), axis=2)
    code = tile * CODE + origin
    packed = jnp.concatenate([code.reshape(-1), target.reshape(-1), jnp.max(ends, axis=1)])
    return packed, capacity


def group_turns(groups, length, target_of, store, product):
    def turn(index, total):
        for lane in range(length):
            group = index * length + lane
            target = target_of(group)
            new = (group == 0) | (target != target_of(jnp.maximum(group - 1, 0)))
            fresh = product(group)
            total = jnp.where(new, fresh, total + fresh)
            store(pl.ds(pl.multiple_of(target * TILE, TILE), TILE), total)
        return total

    turns = (groups + length - 1) // length
    lax.fori_loop(0, turns, turn, jnp.zeros((TILE, TILE), jnp.float32))


def forward_kernel(pieces, lists, wave, capacity, list_ref, hold_ref, *refs):
    first = wave == 0
    x_refs, refs = refs[:pieces], refs[pieces:]
    if first:
        total_ref, x_ref = refs
        total_ref[...] = jnp.zeros_like(total_ref)
    else:
        before_ref, out_refs, (total_ref, x_ref) = refs[0], refs[1:-2], refs[-2:]
        total_ref[...] = before_ref[...].astype(jnp.bfloat16)
    start = 0
    for piece_ref in x_refs:
        x_ref[start : start + piece_ref.shape[0], :] = piece_ref[...]
        start += piece_ref.shape[0]
    x_ref[start:, :] = jnp.zeros((TILE, TILE), jnp.bfloat16)

    def product(group):
        begin = (wave * capacity + group) * FORWARD_WIDTH
        codes = [list_ref[begin + item] for item in range(FORWARD_WIDTH)]
        left = jnp.concatenate([hold_ref[code // CODE] for code in codes], axis=1)
        starts = [pl.multiple_of(code % CODE * TILE, TILE) for code in codes]
        right = jnp.concatenate([x_ref[pl.ds(start, TILE), :] for start in starts], axis=0)
        return jnp.dot(left, right, preferred_element_type=jnp.float32)

    def store(span, total):
        if first:
            total_ref[span, :] = total
        else:
            total_ref[span, :] = (total + before_ref[span, :]).astype(jnp.bfloat16)

    codes = lists * capacity * FORWARD_WIDTH
    ends = codes + lists * capacity
    group_turns(
        list_ref[ends + wave],
        FORWARD_TURN,
        lambda group: list_ref[codes + wave * capacity + group],
        store,
        product,
    )
    if not first:
        reps = len(out_refs)
        own = out_refs[0].shape[0]
        here = list_ref[ends + lists]
        for shift, out_ref in enumerate(out_refs):
            start = pl.multiple_of((here + shift) % reps * own, own)
            out_ref[...] = total_ref[pl.ds(start, own), :]


def estimate(tiles):
    return pl.CostEstimate(
        flops=8 * tiles * TILE**3, bytes_accessed=tiles * TILE * TILE * 2, transcendentals=0
    )


def forward_product(rows, lists, wave, packed, capacity, held, xs, before, reps):
    first = wave == 0
    total_shape = (rows + TILE, TILE)
    x_rows = sum(x.shape[0] for x in xs)
    x_scratch = pltpu.VMEM((x_rows + TILE, TILE), jnp.bfloat16)
    if first:
        operands = [held, *xs]
        out_shape = jax.ShapeDtypeStruct(total_shape, jnp.float32)
        out_specs = whole()
        scratch = [x_scratch]
    else:
        operands = [held, *xs, before]
        out_shape = [jax.ShapeDtypeStruct((rows // reps, TILE), jnp.bfloat16)] * reps
        out_specs = [whole()] * reps
        scratch = [pltpu.VMEM(total_shape, jnp.bfloat16), x_scratch]
    return pl.pallas_call(
        functools.partial(forward_kernel, len(xs), lists, wave, capacity),
        out_shape=out_shape,
        grid_spec=pltpu.PrefetchScalarGridSpec(
            num_scalar_prefetch=1,
            grid=(),
            in_specs=[whole()] * len(operands),
            out_specs=out_specs,
            scratch_shapes=scratch,
        ),
        compiler_params=params(),
        cost_estimate=estimate(held.shape[0]),
    )(packed, *operands)


def dense_kernel(*refs):
    part_refs, (weight_ref, upstream_ref, act_ref, pay_ref) = refs[:-4], refs[-4:]
    rows = upstream_ref.shape[0]
    total = part_refs[0][...].astype(jnp.float32)
    for part_ref in part_refs[1:]:
        total = total + part_ref[...].astype(jnp.float32)
    aggregated = total.astype(jnp.bfloat16)
    weight = weight_ref[...]
    pre = jnp.dot(aggregated, weight, preferred_element_type=jnp.float32)
    gate = jax.nn.sigmoid(pre)
    act_ref[...] = (pre * gate).astype(jnp.bfloat16)
    grad_pre = (
        upstream_ref[...].astype(jnp.float32) * gate * (1.0 + pre * (1.0 - gate))
    ).astype(jnp.bfloat16)
    back = lax.dot_general(
        weight, grad_pre, (((1,), (1,)), ((), ())), preferred_element_type=jnp.float32
    ).astype(jnp.bfloat16)
    for block in range(rows // TILE):
        pay_ref[block * TILE : (block + 1) * TILE, :] = back[:, block * TILE : (block + 1) * TILE]
    local = lax.dot_general(
        aggregated, grad_pre, (((0,), (0,)), ((), ())), preferred_element_type=jnp.float32
    ).astype(jnp.bfloat16)
    for half in range(weight.shape[1] // TILE):
        pay_ref[rows + half * TILE : rows + (half + 1) * TILE, :] = local[
            :, half * TILE : (half + 1) * TILE
        ]


def dense_layer(parts, weight, upstream):
    rows, hidden = upstream.shape
    pay_rows = rows + hidden // TILE * weight.shape[0]
    return pl.pallas_call(
        dense_kernel,
        out_shape=(
            jax.ShapeDtypeStruct((rows, hidden), jnp.bfloat16),
            jax.ShapeDtypeStruct((pay_rows, TILE), jnp.bfloat16),
        ),
        in_specs=[whole()] * (len(parts) + 2),
        out_specs=(whole(), whole()),
        compiler_params=params(),
    )(*parts, weight, upstream)


def backward_kernel(count, lists, first, capacity, list_ref, hold_ref, *refs):
    pay_refs, out_refs = refs[: -2 - count], refs[-2 - count : -2]
    total_ref, back_ref = refs[-2:]
    reps = len(pay_refs)
    rows = out_refs[0].shape[0]
    own = rows // reps
    per_slot = hold_ref.shape[0] // count
    codes = lists * capacity * BACKWARD_WIDTH
    ends = codes + lists * capacity
    place = ends + lists
    here = list_ref[place]
    for shift, pay_ref in enumerate(pay_refs):
        start = pl.multiple_of((here + reps - shift) % reps * own, own)
        back_ref[pl.ds(start, own), :] = pay_ref[:own, :]
    back_ref[rows:, :] = jnp.zeros((TILE, TILE), jnp.bfloat16)
    total_ref[...] = jnp.zeros_like(total_ref)
    for number in range(0, count, PAIR):
        listed = first + number // PAIR

        def product(group, listed=listed, number=number):
            begin = (listed * capacity + group) * BACKWARD_WIDTH
            items = [list_ref[begin + item] for item in range(BACKWARD_WIDTH)]
            starts = [pl.multiple_of(code % CODE * TILE, TILE) for code in items]
            left = jnp.concatenate([back_ref[pl.ds(start, TILE), :] for start in starts], axis=1)
            right = jnp.concatenate(
                [hold_ref[number * per_slot + code // CODE] for code in items], axis=0
            )
            return jnp.dot(left, right, preferred_element_type=jnp.float32)

        def target_of(group, listed=listed):
            return list_ref[codes + listed * capacity + group]

        def store(span, total):
            total_ref[span, :] = total.astype(jnp.bfloat16)

        group_turns(list_ref[ends + listed], BACKWARD_TURN, target_of, store, product)
        for item in range(PAIR):
            out_refs[number + item][...] = total_ref[item * rows : (item + 1) * rows, :]
        if number + PAIR < count:
            total_ref[...] = jnp.zeros_like(total_ref)


def backward_product(count, rows, lists, first, packed, capacity, held, pays):
    out_shape = jax.ShapeDtypeStruct((rows, TILE), jnp.bfloat16)
    return pl.pallas_call(
        functools.partial(backward_kernel, count, lists, first, capacity),
        out_shape=[out_shape] * count,
        grid_spec=pltpu.PrefetchScalarGridSpec(
            num_scalar_prefetch=1,
            grid=(),
            in_specs=[whole()] * (1 + len(pays)),
            out_specs=[whole()] * count,
            scratch_shapes=[
                pltpu.VMEM((PAIR * rows + TILE, TILE), jnp.bfloat16),
                pltpu.VMEM((rows + TILE, TILE), jnp.bfloat16),
            ],
        ),
        compiler_params=params(),
        cost_estimate=estimate(held.shape[0]),
    )(packed, held, *pays)


def restore_kernel(place_ref, order_ref, home_ref, *refs):
    out_refs, part_ref = refs[:-1], refs[-1]
    rows = order_ref.shape[1]
    reps = len(out_refs)
    own = rows // reps
    for block in range(rows // TILE):
        span = slice(block * TILE, (block + 1) * TILE)
        part_ref[span, :] = home_ref[span, :].astype(jnp.float32).T.astype(jnp.bfloat16)
    order = order_ref[...]
    part = part_ref[...]
    for shift, out_ref in enumerate(out_refs):
        start = (place_ref[0] + shift) % reps * own
        level = lax.broadcasted_iota(jnp.int32, (own, rows), 0) + start
        pick = (jnp.broadcast_to(order, (own, rows)) == level).astype(jnp.float32)
        out_ref[...] = jnp.dot(
            pick.astype(jnp.bfloat16), part, preferred_element_type=jnp.float32
        ).astype(jnp.bfloat16)


def restore(place, order, home, reps):
    rows = order.shape[1]
    out_shape = jax.ShapeDtypeStruct((rows // reps, TILE), jnp.bfloat16)
    return pl.pallas_call(
        restore_kernel,
        out_shape=[out_shape] * reps,
        grid_spec=pltpu.PrefetchScalarGridSpec(
            num_scalar_prefetch=1,
            grid=(),
            in_specs=[whole()] * 2,
            out_specs=[whole()] * reps,
            scratch_shapes=[pltpu.VMEM((rows, TILE), jnp.bfloat16)],
        ),
        compiler_params=params(),
    )(place, order, home)


def added(*values):
    return sum(value.astype(jnp.float32) for value in values).astype(jnp.bfloat16)


def per_device(features, node_order, adj_values, adj_rows, adj_cols, tile_count, weight, upstream):
    reps = lax.axis_size("rep")
    slices = lax.axis_size("blk")
    steps = slices // reps
    rows_dev = features.shape[0]
    blocks = rows_dev // TILE
    both = ("blk", "rep")
    row_ids, col_ids, counts = adj_rows[0, 0], adj_cols[0, 0], tile_count[0, 0]
    per_slot = row_ids.shape[1]
    tiles = adj_values.reshape((-1, TILE, TILE))
    own_rep = lax.axis_index("rep").astype(jnp.int32).reshape(1)

    here = lax.axis_index("blk") * reps + lax.axis_index("rep")
    slots = lax.dynamic_index_in_dim(jnp.asarray(slot_table()), here, 0, keepdims=False)
    place = jnp.concatenate([own_rep, slots])
    half = rows_dev // 2

    def moved(value, listed):
        return lax.ppermute(value, both, listed)

    def up(value):
        return moved(value, ring_pairs(1))

    def down(value):
        return moved(value, ring_pairs(-1))

    def swapped(value):
        return moved(value, partner_pairs())

    def to_reps(values):
        received = [values[0]]
        for shift in range(1, reps):
            along = [(rep, (rep + shift) % reps) for rep in range(reps)]
            received.append(lax.ppermute(values[shift], "rep", along))
        return received

    blocked = order_rows(node_order, features)
    near = moved(blocked, fetch_pairs())
    above, below = down(near), up(near)
    far = swapped(near)
    above, far = lax.optimization_barrier((above, far))
    middle = [down(above[:half]), up(below[half:])]
    arrived = {0: [near], 1: [above], 2: middle, 3: [below], 4: [far], 5: [swapped(above)]}
    arrived[6] = [swapped(value) for value in middle]
    arrived[7] = [swapped(below)]
    alive = jnp.arange(per_slot, dtype=jnp.int32)[None, :] < counts[:, None]
    cells = jnp.take(jnp.where(alive, row_ids * CODE + col_ids, -1), slots, axis=0)

    def split(cells, items):
        chosen = jnp.concatenate([cells[item : item + 1] for item in items])
        return chosen >= 0, chosen // CODE, chosen % CODE

    waves = len(FORWARD_WAVES)
    alive, rows_of, cols_of = split(cells, sum(FORWARD_WAVES, ()))
    offsets = jnp.arange(steps, dtype=jnp.int32)[:, None] % (steps // waves) * blocks
    packed, capacity = tile_lists(
        jnp.where(alive, rows_of, blocks).reshape(waves, -1),
        (cols_of + offsets).reshape(waves, -1),
        blocks,
        steps // waves * blocks,
        FORWARD_WIDTH,
        FORWARD_TURN,
    )
    packed = jnp.concatenate([packed, own_rep])
    places = []
    for item in (0, 1):
        known, arrived[item][0] = lax.optimization_barrier((place, arrived[item][0]))
        places.append(known)
    total = None
    for wave, items in enumerate(FORWARD_WAVES):
        xs = sum([arrived[item] for item in items], [])
        held = hold(items, places[wave], tiles, per_slot)
        total = forward_product(
            rows_dev, waves, wave, packed, capacity, held, xs, total, reps
        )
    total = list(total)
    last_cells, total[0] = lax.optimization_barrier((cells, total[0]))
    shared = to_reps(total)
    lists = steps // PAIR
    alive, rows_of, cols_of = split(last_cells, sum(BACKWARD_WAVES, ()))
    offsets = jnp.arange(steps, dtype=jnp.int32)[:, None] % PAIR * blocks
    packed, capacity = tile_lists(
        jnp.where(alive, cols_of + offsets, PAIR * blocks).reshape(lists, -1),
        rows_of.reshape(lists, -1),
        PAIR * blocks,
        blocks,
        BACKWARD_WIDTH,
        BACKWARD_TURN,
    )
    packed = jnp.concatenate([packed, own_rep])
    shared[1], packed = lax.optimization_barrier((shared[1], packed))
    activations, pay = dense_layer(shared, weight, upstream)
    late_place, pay = lax.optimization_barrier((place, pay))
    pays = to_reps([pay] * reps)
    holds = [hold(items, late_place, tiles, per_slot) for items in BACKWARD_WAVES]
    packed, holds = lax.optimization_barrier((packed, holds))

    def products(wave, packed):
        count = len(BACKWARD_WAVES[wave])
        first = wave * count // PAIR
        return list(
            backward_product(count, rows_dev, lists, first, packed, capacity, holds[wave], pays)
        )

    grad_weight = sum(pay[-weight.size // TILE :].astype(jnp.float32) for pay in pays)
    todo = blk_steps()

    def next_after(total, value):
        total, value = lax.optimization_barrier((total, value))
        return total + moved(total, todo.pop(0)), value

    step = moved(grad_weight, todo.pop(0))
    others = products(0, packed)
    step, packed, others[0] = lax.optimization_barrier((step, packed, others[0]))
    grad_weight = grad_weight + step
    returned = {item: swapped(others[item]) for item in (2, 1, 3, 0)}
    mine = products(1, packed)
    two = added(mine[2], returned[2])
    from_below, from_above = up(two[:half]), down(two[half:])
    grad_weight, returned[1] = next_after(grad_weight, returned[1])
    one = jnp.concatenate(
        [added(mine[1][:half], returned[1][:half], from_below), added(mine[1][half:], returned[1][half:])]
    )
    three = jnp.concatenate(
        [added(mine[3][:half], returned[3][:half]), added(mine[3][half:], returned[3][half:], from_above)]
    )
    onward = [up(one), down(three)]
    grad_weight, returned[0] = next_after(grad_weight, returned[0])
    ended = added(mine[0], returned[0], *onward)
    grad_weight, ended = next_after(grad_weight, ended)
    home = moved(ended, [(user, owner) for owner, user in fetch_pairs()])
    grad_weight, home = next_after(grad_weight, home)
    terms = to_reps(restore(own_rep, node_order, home, reps))
    grad_features = added(*terms)
    stacked = grad_weight.reshape(weight.shape[1] // TILE, weight.shape[0], TILE)
    grad_weight = jnp.concatenate([stacked[half] for half in range(stacked.shape[0])], axis=1)
    return (activations, grad_weight, grad_features)


def solution(mesh):
    placed = (
        P("blk", None),
        P("blk", None),
        P("blk", "rep", None, None, None, None),
        P("blk", "rep", None, None),
        P("blk", "rep", None, None),
        P("blk", "rep", None),
        P(),
        P(("blk", "rep"), None),
    )
    return jax.shard_map(
        per_device,
        mesh=mesh,
        in_specs=placed,
        out_specs=(P(("blk", "rep"), None), P(), P(("blk", "rep"), None)),
        check_vma=False,
    )
```

time: 811 us -> 177 us (0.22); the launches traced: 800 us -> 177 us
  waiting for transfers between devices: 280 us -> 53 us
  other arithmetic: 224 us -> 7.41 us
  local copies, waits for them, and re-layouts: 139 us -> 4.62 us
  matrix products: 102 us -> 0 us
  Pallas kernels: 0 us -> 54.9 us
  starting transfers between devices: 31.2 us -> 56.1 us
  between operations: 14.9 us -> 1.13 us
  blocking collectives: 8.97 us -> 0 us
    scatter-add x16 -> x0, other arithmetic: 190 us -> none  [the longest x8 104 us: per_device(): spread_empty.at[row_ids[slot_index]]]
    psum x1 -> x0, waiting for transfers between devices: 130 us -> none  [per_device(): grad_weight = lax.psum(grad_local, ('blk', 'rep'))]
    dot_general x19 -> x0, matrix products: 102 us -> none  [the longest x8 55.5 us: per_device(): jnp.einsum('ptk,pkf->ptf', tile_values[slot_index], spread_picked, prefer...]
    mul x16 -> x0, local copies, waits for them, and re-layouts: 94.9 us -> none  [live_part(): return product * live_mask[:, None, None]]
    reduce_scatter x2 -> x0, waiting for transfers between devices: 73.8 us -> none  [replica_total(): lax.psum_scatter(values.astype(jnp.bfloat16), 'rep', scatter_dimension=0,...]
    pallas_call x0 -> x11, Pallas kernels: none -> 54.9 us  [the longest x4 18.6 us: hold(): pl.pallas_call(functools.partial(hold_kernel, items), out_shape=jax.Shape...]
    gather x17 -> x1, local copies, waits for them, and re-layouts: 37 us -> 0.55 us  [per_device(): jnp.take(jnp.where(alive, row_ids * CODE + col_ids, -1), slots, axis=0)]
    ppermute x18 -> x33, starting transfers between devices: 31.1 us -> 56.1 us  [the longest x24 36.5 us: moved(): return lax.ppermute(value, both, listed)]
  transfers between devices with their start and end apart: 21 -> 33, of which waited for: 16 -> 15; matrix products, arithmetic and copies ran while one was open for 39% -> 5% of each run, Pallas kernels for 0% -> 25%
where the time goes in v1:
time: 177 us
  starting transfers between devices  56.1 us (32%)
  Pallas kernels  54.9 us (31%)
  waiting for transfers between devices  53 us (30%)
  other arithmetic  7.41 us (4%)
  local copies, waits for them, and re-layouts  4.62 us (3%)
    ppermute x24, waiting for transfers between devices, moved(): return lax.ppermute(value, both, listed)  42.5 us
    ppermute x24, starting transfers between devices, moved(): return lax.ppermute(value, both, listed)  36.5 us
    ppermute x9, starting transfers between devices, to_reps(): received.append(lax.ppermute(values[shift], 'rep', along))  19.6 us
    pallas_call x4, Pallas kernels, hold(): pl.pallas_call(functools.partial(hold_kernel, items), out_shape=jax.Shape...  18.6 us
    pallas_call x2, Pallas kernels, backward_product(): pl.pallas_call(functools.partial(backward_kernel, count, lists, first, ca...  15.9 us
    pallas_call x2, Pallas kernels, forward_product(): pl.pallas_call(functools.partial(forward_kernel, len(xs), lists, wave, ca...  14.5 us
    ppermute x9, waiting for transfers between devices, to_reps(): received.append(lax.ppermute(values[shift], 'rep', along))  10.5 us
  transfers between devices with their start and end apart: 33, of which 15 were waited for; matrix products, arithmetic and copies ran while one was open for 5% of the time, Pallas kernels for 25%

profile of v1, /device:TPU:1, one launch (start us, length us, event | category | flops | bytes accessed | tf_op | source)
XLA Modules:
  0.0 177.1 jit_solution(3377901953333941704)
XLA Ops:
  0.6 1.0 copy-done
  1.7 0.7 copy-done.3
  2.4 2.4 %shard_map.112 = bf16[2048,128]{1,0:T(8,128)(2,1)S(1)} custom-call(s32[1,2048]{1,0:T(1,128)S(1)} %copy-done.3, bf16[2048,128]{1,0:T(8,128)(2,1)S(1)} %copy-done), custom_call_target="tpu_custom_call" | custom-call | tf_op jit(solution)/shard_map/pallas_call | solution.py:113
  4.7 5.3 %collective-permute-start = (bf16[2048,128]{1,0:T(8,128)(2,1)S(1)}, bf16[2048,128]{1,0:T(8,128)(2,1)S(1)}, u32[]{:S(2)}, u32[]{:S(2)}) collective-permute-start(bf16[2048,128]{1,0:T(8,128)(2,1)S(1)} %shard_map.112), channel_id=1, source_target_pairs={{0,0},{23,1},{8,8},{31,9},{16,16},{7,17},{24,24},{15,25},{32,32},{... | collective-permute-start | bytes 1572872 | tf_op jit(solution)/shard_map/ppermute | solution.py:443
  10.1 0.7 fusion.14
  10.8 0.7 compare_and_fusion
  11.5 0.8 bitcast_select_fusion
  12.2 0.6 gather_fusion
  13.5 0.4 convert_reduce_fusion
  13.9 0.3 select_reduce_fusion.1
  14.3 5.5 %collective-permute-done.refs_0_ = bf16[2048,128]{1,0:T(8,128)(2,1)S(1)} collective-permute-done((bf16[2048,128]{1,0:T(8,128)(2,1)S(1)}, bf16[2048,128]{1,0:T(8,128)(2,1)S(1)}, u32[]{:S(2)}, u32[]{:S(2)}) %collective-permute-start) | collective-permute-done | bytes 524320 | tf_op jit(solution)/shard_map/ppermute | solution.py:443
  19.8 2.7 %collective-permute-start.1 = (bf16[2048,128]{1,0:T(8,128)(2,1)S(1)}, bf16[2048,128]{1,0:T(8,128)(2,1)S(1)}, u32[]{:S(2)}, u32[]{:S(2)}) collective-permute-start(bf16[2048,128]{1,0:T(8,128)(2,1)S(1)} %collective-permute-done.refs_0_), channel_id=1, source_target_pairs={{0,96},{1,97},{8,104},{9,105},{16,112},{17,113},{24,120},{25,121},... | collective-permute-start | bytes 1572872 | tf_op jit(solution)/shard_map/ppermute | solution.py:443
  23.1 5.6 %collective-permute-done.1.refs_1_ = bf16[2048,128]{1,0:T(8,128)(2,1)S(1)} collective-permute-done((bf16[2048,128]{1,0:T(8,128)(2,1)S(1)}, bf16[2048,128]{1,0:T(8,128)(2,1)S(1)}, u32[]{:S(2)}, u32[]{:S(2)}) %collective-permute-start.1) | collective-permute-done | bytes 524320 | tf_op jit(solution)/shard_map/ppermute | solution.py:443
  28.7 2.8 %collective-permute-done.2.refs_0_ = bf16[2048,128]{1,0:T(8,128)(2,1)S(1)} collective-permute-done((bf16[2048,128]{1,0:T(8,128)(2,1)S(1)}, bf16[2048,128]{1,0:T(8,128)(2,1)S(1)}, u32[]{:S(2)}, u32[]{:S(2)}) %collective-permute-start.2) | collective-permute-done | bytes 524320 | tf_op jit(solution)/shard_map/ppermute | solution.py:443
  31.5 0.5 collective-permute-start.6
  32.0 4.2 %collective-permute-done.4.refs_2_ = bf16[2048,128]{1,0:T(8,128)(2,1)S(1)} collective-permute-done((bf16[2048,128]{1,0:T(8,128)(2,1)S(1)}, bf16[2048,128]{1,0:T(8,128)(2,1)S(1)}, u32[]{:S(2)}, u32[]{:S(2)}) %collective-permute-start.4) | collective-permute-done | bytes 524320 | tf_op jit(solution)/shard_map/ppermute | solution.py:443
  36.3 0.7 slice.120
  37.0 0.7 dynamic-slice_bitcast_fusion
  37.7 3.4 %collective-permute-start.3 = (bf16[2048,128]{1,0:T(8,128)(2,1)S(1)}, bf16[2048,128]{1,0:T(8,128)(2,1)S(1)}, u32[]{:S(2)}, u32[]{:S(2)}) collective-permute-start(bf16[2048,128]{1,0:T(8,128)(2,1)S(1)} %collective-permute-done.1.refs_1_), channel_id=1, source_target_pairs={{0,7},{1,4},{8,15},{9,12},{16,23},{17,20},{24,31},{25,28},{32,39},... | collective-permute-start | bytes 1572872 | tf_op jit(solution)/shard_map/ppermute | solution.py:443
  41.5 4.6 %shard_map.114.hold_ref = bf16[320,128,128]{2,1,0:T(8,128)(2,1)S(1)} custom-call(s32[9]{0:T(128)S(1)} %pad_add_fusion.2.place_ref, bf16[640,128,128]{2,1,0:T(8,128)(2,1)} %bitcast.16), custom_call_target="tpu_custom_call" | custom-call | bytes 20971520 | tf_op jit(solution)/shard_map/pallas_call | solution.py:140
  46.1 4.6 %shard_map.113.hold_ref = bf16[320,128,128]{2,1,0:T(8,128)(2,1)S(1)} custom-call(s32[9]{0:T(128)S(1)} %pad_add_fusion.2.place_ref, bf16[640,128,128]{2,1,0:T(8,128)(2,1)} %bitcast.17), custom_call_target="tpu_custom_call" | custom-call | bytes 20971520 | tf_op jit(solution)/shard_map/pallas_call | solution.py:140
  50.8 1.7 collective-permute-start.7
  52.6 7.5 %shard_map.115.refs_5_ = f32[2176,128]{1,0:T(8,128)S(1)} custom-call(s32[1011]{0:T(1024)S(1)} %pad_add_fusion.list_ref, bf16[320,128,128]{2,1,0:T(8,128)(2,1)S(1)} %shard_map.114.hold_ref, bf16[2048,128]{1,0:T(8,128)(2,1)S(1)} %collective-permute-done.refs_0_, bf16[2048,128]{1,0:T(8,128)(2,1)S(1)} %collective-permute-done.1.refs_1_, ...), custom_call_target="tpu_custom_call" | custom-call | flops 5368709120 | bytes 10485760 | tf_op jit(solution)/shard_map/pallas_call | solution.py:265
  60.1 7.0 %shard_map.116 = (bf16[512,128]{1,0:T(8,128)(2,1)S(1)}, bf16[512,128]{1,0:T(8,128)(2,1)S(1)}, bf16[512,128]{1,0:T(8,128)(2,1)S(1)}, bf16[512,128]{1,0:T(8,128)(2,1)S(1)}) custom-call(s32[1011]{0:T(1024)S(1)} %pad_add_fusion.list_ref, bf16[320,128,128]{2,1,0:T(8,128)(2,1)S(1)} %shard_map.113.hold_ref, bf16[2048,128]{1,0:T(8,128)(2,1)S(1)} %collective-permute-done.2.refs_0_, ...), custom_call_target="tpu_custom_call" | custom-call | flops 5368709120 | bytes 10485760 | tf_op jit(solution)/shard_map/pallas_call | solution.py:265
  67.3 0.1 convert_reduce_fusion.2
  67.6 0.4 convert_reduce_fusion.1
  68.0 3.7 %collective-permute-start.11 = (bf16[512,128]{1,0:T(8,128)(2,1)S(1)}, bf16[512,128]{1,0:T(8,128)(2,1)S(1)}, u32[]{:S(2)}, u32[]{:S(2)}) collective-permute-start(bf16[512,128]{1,0:T(8,128)(2,1)S(1)} %get-tuple-element.58), channel_id=1, source_target_pairs={{0,2},{1,3},{2,0},{3,1},{4,6},{5,7},{6,4},{7,5},{8,10},{9,11},{10,... | collective-permute-start | bytes 393224 | tf_op jit(solution)/shard_map/ppermute | solution.py:458
  71.8 0.7 collective-permute-start.12
  72.5 0.3 select_reduce_fusion.3
  73.3 4.1 %collective-permute-done.11.refs_2_ = bf16[512,128]{1,0:T(8,128)(2,1)S(1)} collective-permute-done((bf16[512,128]{1,0:T(8,128)(2,1)S(1)}, bf16[512,128]{1,0:T(8,128)(2,1)S(1)}, u32[]{:S(2)}, u32[]{:S(2)}) %collective-permute-start.11) | collective-permute-done | bytes 131104 | tf_op jit(solution)/shard_map/ppermute | solution.py:458
  77.4 0.9 collective-permute-done.12.refs_3_
  78.3 1.0 shard_map.117
  79.3 0.8 collective-permute-start.13
  80.1 0.8 collective-permute-start.14
  81.0 0.8 collective-permute-start.15
  81.7 4.6 %shard_map.118.hold_ref = bf16[320,128,128]{2,1,0:T(8,128)(2,1)S(1)} custom-call(s32[9]{0:T(128)S(1)} %pad_add_fusion.2.place_ref, bf16[640,128,128]{2,1,0:T(8,128)(2,1)} %bitcast.18), custom_call_target="tpu_custom_call" | custom-call | bytes 20971520 | tf_op jit(solution)/shard_map/pallas_call | solution.py:140
  86.4 4.6 %shard_map.119.hold_ref = bf16[320,128,128]{2,1,0:T(8,128)(2,1)S(1)} custom-call(s32[9]{0:T(128)S(1)} %pad_add_fusion.2.place_ref, bf16[640,128,128]{2,1,0:T(8,128)(2,1)} %bitcast.19), custom_call_target="tpu_custom_call" | custom-call | bytes 20971520 | tf_op jit(solution)/shard_map/pallas_call | solution.py:140
  91.2 8.1 %shard_map.120 = (bf16[2048,128]{1,0:T(8,128)(2,1)S(1)}, bf16[2048,128]{1,0:T(8,128)(2,1)S(1)}, bf16[2048,128]{1,0:T(8,128)(2,1)S(1)}, bf16[2048,128]{1,0:T(8,128)(2,1)S(1)}) custom-call(s32[1285]{0:T(1024)S(1)} %concatenate.36.list_ref, bf16[320,128,128]{2,1,0:T(8,128)(2,1)S(1)} %shard_map.118.hold_ref, bf16[768,128]{1,0:T(8,128)(2,1)S(1)} %get-tuple-element.62.refs_0_, ...), custom_call_target="tpu_custom_call" | custom-call | flops 5368709120 | bytes 10485760 | tf_op jit(solution)/shard_map/pallas_call | solution.py:367
  99.4 1.7 collective-permute-start.17
  101.1 7.9 %shard_map.121 = (bf16[2048,128]{1,0:T(8,128)(2,1)S(1)}, bf16[2048,128]{1,0:T(8,128)(2,1)S(1)}, bf16[2048,128]{1,0:T(8,128)(2,1)S(1)}, bf16[2048,128]{1,0:T(8,128)(2,1)S(1)}) custom-call(s32[1285]{0:T(1024)S(1)} %concatenate.36.list_ref, bf16[320,128,128]{2,1,0:T(8,128)(2,1)S(1)} %shard_map.119.hold_ref, bf16[768,128]{1,0:T(8,128)(2,1)S(1)} %get-tuple-element.62.refs_0_, ...), custom_call_target="tpu_custom_call" | custom-call | flops 5368709120 | bytes 10485760 | tf_op jit(solution)/shard_map/pallas_call | solution.py:367
  109.2 1.5 collective-permute-start.22
  110.7 1.8 %collective-permute-start.19 = (bf16[2048,128]{1,0:T(8,128)(2,1)S(1)}, bf16[2048,128]{1,0:T(8,128)(2,1)S(1)}, u32[]{:S(2)}, u32[]{:S(2)}) collective-permute-start(bf16[2048,128]{1,0:T(8,128)(2,1)S(1)} %get-tuple-element.71), channel_id=1, source_target_pairs={{0,7},{1,4},{8,15},{9,12},{16,23},{17,20},{24,31},{25,28},{32,39},... | collective-permute-start | bytes 1572872 | tf_op jit(solution)/shard_map/ppermute | solution.py:443
  112.6 1.2 collective-permute-done.17
  113.8 3.8 %collective-permute-start.25 = (bf16[1024,128]{1,0:T(8,128)(2,1)S(1)}, bf16[1024,128]{1,0:T(8,128)(2,1)S(1)}, u32[]{:S(2)}, u32[]{:S(2)}) collective-permute-start(bf16[1024,128]{1,0:T(8,128)(2,1)S(1)} %get-tuple-element.100), channel_id=1, source_target_pairs={{0,96},{1,97},{8,104},{9,105},{16,112},{17,113},{24,120},{25,121},... | collective-permute-start | bytes 786440 | tf_op jit(solution)/shard_map/ppermute | solution.py:443
  117.5 0.2 add_convert_fusion.5
  117.7 1.3 collective-permute-start.23
  119.1 0.6 collective-permute-done.24
  119.6 1.2 collective-permute-done.25
  120.8 0.2 add_convert_fusion.3
  121.1 3.5 %collective-permute-start.26 = (bf16[2048,128]{1,0:T(8,128)(2,1)S(1)}, bf16[2048,128]{1,0:T(8,128)(2,1)S(1)}, u32[]{:S(2)}, u32[]{:S(2)}) collective-permute-start(bf16[2048,128]{1,0:T(8,128)(2,1)S(1)} %pad_maximum_fusion.1), channel_id=1, source_target_pairs={{0,96},{1,97},{8,104},{9,105},{16,112},{17,113},{24,120},{25,121},... | collective-permute-start | bytes 1572872 | tf_op jit(solution)/shard_map/ppermute | solution.py:443
  124.6 10.2 %collective-permute-done.18 = f32[256,128]{1,0:T(8,128)S(1)} collective-permute-done((f32[256,128]{1,0:T(8,128)S(1)}, f32[256,128]{1,0:T(8,128)S(1)}, u32[]{:S(2)}, u32[]{:S(2)}) %collective-permute-start.18) | collective-permute-done | bytes 131104 | tf_op jit(solution)/shard_map/ppermute | solution.py:443
  134.9 3.8 %collective-permute-done.20 = f32[256,128]{1,0:T(8,128)S(1)} collective-permute-done((f32[256,128]{1,0:T(8,128)S(1)}, f32[256,128]{1,0:T(8,128)S(1)}, u32[]{:S(2)}, u32[]{:S(2)}) %collective-permute-start.20) | collective-permute-done | bytes 131104 | tf_op jit(solution)/shard_map/ppermute | solution.py:443
  138.8 0.3 add_convert_fusion
  139.1 7.2 %collective-permute-start.28 = (bf16[2048,128]{1,0:T(8,128)(2,1)S(1)}, bf16[2048,128]{1,0:T(8,128)(2,1)S(1)}, u32[]{:S(2)}, u32[]{:S(2)}) collective-permute-start(bf16[2048,128]{1,0:T(8,128)(2,1)S(1)} %add_convert_fusion), channel_id=1, source_target_pairs={{0,0},{1,23},{8,8},{9,31},{16,16},{17,7},{24,24},{25,15},{32,32},{... | collective-permute-start | bytes 1572872 | tf_op jit(solution)/shard_map/ppermute | solution.py:443
  146.3 1.3 collective-permute-start.27
  147.6 7.3 %collective-permute-done.27 = f32[256,128]{1,0:T(8,128)S(1)} collective-permute-done((f32[256,128]{1,0:T(8,128)S(1)}, f32[256,128]{1,0:T(8,128)S(1)}, u32[]{:S(2)}, u32[]{:S(2)}) %collective-permute-start.27) | collective-permute-done | bytes 131104 | tf_op jit(solution)/shard_map/ppermute | solution.py:443
  155.0 2.5 %shard_map.122 = (bf16[512,128]{1,0:T(8,128)(2,1)S(1)}, bf16[512,128]{1,0:T(8,128)(2,1)S(1)}, bf16[512,128]{1,0:T(8,128)(2,1)S(1)}, bf16[512,128]{1,0:T(8,128)(2,1)S(1)}) custom-call(s32[1]{0:T(128)} %bitcast.5.place_ref, s32[1,2048]{1,0:T(1,128)S(1)} %copy-done.4, bf16[2048,128]{1,0:T(8,128)(2,1)S(1)} %collective-permute-done.28.home_ref), custom_call_target="tpu_custom_call" | custom-call | tf_op jit(solution)/shard_map/pallas_call | solution.py:407
  157.5 12.2 %collective-permute-start.30 = (bf16[512,128]{1,0:T(8,128)(2,1)S(1)}, bf16[512,128]{1,0:T(8,128)(2,1)S(1)}, u32[]{:S(2)}, u32[]{:S(2)}) collective-permute-start(bf16[512,128]{1,0:T(8,128)(2,1)S(1)} %get-tuple-element.88), channel_id=1, source_target_pairs={{0,1},{1,2},{2,3},{3,0},{4,5},{5,6},{6,7},{7,4},{8,9},{9,10},{10,1... | collective-permute-start | bytes 393224 | tf_op jit(solution)/shard_map/ppermute | solution.py:458
  169.7 0.5 collective-permute-start.32
  170.2 0.7 pad_maximum_fusion.2
  170.9 1.5 collective-permute-done.30
  172.4 3.5 %collective-permute-done.31 = bf16[512,128]{1,0:T(8,128)(2,1)S(1)} collective-permute-done((bf16[512,128]{1,0:T(8,128)(2,1)S(1)}, bf16[512,128]{1,0:T(8,128)(2,1)S(1)}, u32[]{:S(2)}, u32[]{:S(2)}) %collective-permute-start.31) | collective-permute-done | bytes 131104 | tf_op jit(solution)/shard_map/ppermute | solution.py:458
  175.9 0.6 collective-permute-done.32
  176.4 0.7 add_convert_fusion.6
  (94 shorter events, 3.4 us)
Async XLA Ops:
  0.6 1.0 copy-start
  1.7 0.7 copy-start.3
  4.7 15.1 %collective-permute-start = (bf16[2048,128]{1,0:T(8,128)(2,1)S(1)}, bf16[2048,128]{1,0:T(8,128)(2,1)S(1)}, u32[]{:S(2)}, u32[]{:S(2)}) collective-permute-start(bf16[2048,128]{1,0:T(8,128)(2,1)S(1)} %shard_map.112), channel_id=1, source_target_pairs={{0,0},{23,1},{8,8},{31,9},{16,16},{7,17},{24,24},{15,25},{32,32},{... | collective-permute-start | bytes 1572872 | tf_op jit(solution)/shard_map/ppermute | solution.py:443
  19.8 8.9 %collective-permute-start.1 = (bf16[2048,128]{1,0:T(8,128)(2,1)S(1)}, bf16[2048,128]{1,0:T(8,128)(2,1)S(1)}, u32[]{:S(2)}, u32[]{:S(2)}) collective-permute-start(bf16[2048,128]{1,0:T(8,128)(2,1)S(1)} %collective-permute-done.refs_0_), channel_id=1, source_target_pairs={{0,96},{1,97},{8,104},{9,105},{16,112},{17,113},{24,120},{25,121},... | collective-permute-start | bytes 1572872 | tf_op jit(solution)/shard_map/ppermute | solution.py:443
  22.6 8.9 %collective-permute-start.2 = (bf16[2048,128]{1,0:T(8,128)(2,1)S(1)}, bf16[2048,128]{1,0:T(8,128)(2,1)S(1)}, u32[]{:S(2)}, u32[]{:S(2)}) collective-permute-start(bf16[2048,128]{1,0:T(8,128)(2,1)S(1)} %collective-permute-done.refs_0_), channel_id=1, source_target_pairs={{0,7},{1,4},{8,15},{9,12},{16,23},{17,20},{24,31},{25,28},{32,39},... | collective-permute-start | bytes 1572872 | tf_op jit(solution)/shard_map/ppermute | solution.py:443
  22.6 13.7 %collective-permute-start.4 = (bf16[2048,128]{1,0:T(8,128)(2,1)S(1)}, bf16[2048,128]{1,0:T(8,128)(2,1)S(1)}, u32[]{:S(2)}, u32[]{:S(2)}) collective-permute-start(bf16[2048,128]{1,0:T(8,128)(2,1)S(1)} %collective-permute-done.refs_0_), channel_id=1, source_target_pairs={{0,32},{1,33},{8,40},{9,41},{16,48},{17,49},{24,56},{25,57},{32,64... | collective-permute-start | bytes 1572872 | tf_op jit(solution)/shard_map/ppermute | solution.py:443
  31.5 19.3 %collective-permute-start.6 = (bf16[1024,128]{1,0:T(8,128)(2,1)S(1)}, bf16[1024,128]{1,0:T(8,128)(2,1)}, u32[]{:S(2)}, u32[]{:S(2)}) collective-permute-start(bf16[1024,128]{1,0:T(8,128)(2,1)S(1)} %slice.98), channel_id=1, source_target_pairs={{0,96},{1,97},{8,104},{9,105},{16,112},{17,113},{24,120},{25,121},... | collective-permute-start | bytes 786440 | tf_op jit(solution)/shard_map/ppermute | solution.py:443
  37.0 15.5 %collective-permute-start.8 = (bf16[1024,128]{1,0:T(8,128)(2,1)}, bf16[1024,128]{1,0:T(8,128)(2,1)}, u32[]{:S(2)}, u32[]{:S(2)}) collective-permute-start(bf16[1024,128]{1,0:T(8,128)(2,1)} %slice.120), channel_id=1, source_target_pairs={{0,32},{1,33},{8,40},{9,41},{16,48},{17,49},{24,56},{25,57},{32,64... | collective-permute-start | bytes 786440 | tf_op jit(solution)/shard_map/ppermute | solution.py:443
  37.7 22.4 %collective-permute-start.3 = (bf16[2048,128]{1,0:T(8,128)(2,1)S(1)}, bf16[2048,128]{1,0:T(8,128)(2,1)S(1)}, u32[]{:S(2)}, u32[]{:S(2)}) collective-permute-start(bf16[2048,128]{1,0:T(8,128)(2,1)S(1)} %collective-permute-done.1.refs_1_), channel_id=1, source_target_pairs={{0,7},{1,4},{8,15},{9,12},{16,23},{17,20},{24,31},{25,28},{32,39},... | collective-permute-start | bytes 1572872 | tf_op jit(solution)/shard_map/ppermute | solution.py:443
  41.2 19.0 %collective-permute-start.5 = (bf16[2048,128]{1,0:T(8,128)(2,1)S(1)}, bf16[2048,128]{1,0:T(8,128)(2,1)S(1)}, u32[]{:S(2)}, u32[]{:S(2)}) collective-permute-start(bf16[2048,128]{1,0:T(8,128)(2,1)S(1)} %collective-permute-done.4.refs_2_), channel_id=1, source_target_pairs={{0,7},{1,4},{8,15},{9,12},{16,23},{17,20},{24,31},{25,28},{32,39},... | collective-permute-start | bytes 1572872 | tf_op jit(solution)/shard_map/ppermute | solution.py:443
  50.8 9.3 %collective-permute-start.7 = (bf16[1024,128]{1,0:T(8,128)(2,1)}, bf16[1024,128]{1,0:T(8,128)(2,1)S(1)}, u32[]{:S(2)}, u32[]{:S(2)}) collective-permute-start(bf16[1024,128]{1,0:T(8,128)(2,1)} %collective-permute-done.6.refs_3_), channel_id=1, source_target_pairs={{0,7},{1,4},{8,15},{9,12},{16,23},{17,20},{24,31},{25,28},{32,39},... | collective-permute-start | bytes 786440 | tf_op jit(solution)/shard_map/ppermute | solution.py:443
  52.5 7.6 %collective-permute-start.9 = (bf16[1024,128]{1,0:T(8,128)(2,1)}, bf16[1024,128]{1,0:T(8,128)(2,1)S(1)}, u32[]{:S(2)}, u32[]{:S(2)}) collective-permute-start(bf16[1024,128]{1,0:T(8,128)(2,1)} %collective-permute-done.8.refs_4_), channel_id=1, source_target_pairs={{0,7},{1,4},{8,15},{9,12},{16,23},{17,20},{24,31},{25,28},{32,39},... | collective-permute-start | bytes 786440 | tf_op jit(solution)/shard_map/ppermute | solution.py:443
  60.1 18.2 %copy-start.1 = (bf16[512,256]{1,0:T(8,128)(2,1)S(1)}, bf16[512,256]{1,0:T(8,128)(2,1)}, u32[]{:S(2)}) copy-start(bf16[512,256]{1,0:T(8,128)(2,1)} %refs_5_.1) | copy-start | bytes 786436
  60.1 18.2 %copy-start.2 = (bf16[128,256]{1,0:T(8,128)(2,1)S(1)}, bf16[128,256]{1,0:T(8,128)(2,1)}, u32[]{:S(2)}) copy-start(bf16[128,256]{1,0:T(8,128)(2,1)} %refs_4_.1) | copy-start | bytes 196612
  68.0 5.3 %collective-permute-start.10 = (bf16[512,128]{1,0:T(8,128)(2,1)S(1)}, bf16[512,128]{1,0:T(8,128)(2,1)S(1)}, u32[]{:S(2)}, u32[]{:S(2)}) collective-permute-start(bf16[512,128]{1,0:T(8,128)(2,1)S(1)} %get-tuple-element.55), channel_id=1, source_target_pairs={{0,1},{1,2},{2,3},{3,0},{4,5},{5,6},{6,7},{7,4},{8,9},{9,10},{10,1... | collective-permute-start | bytes 393224 | tf_op jit(solution)/shard_map/ppermute | solution.py:458
  68.0 9.3 %collective-permute-start.11 = (bf16[512,128]{1,0:T(8,128)(2,1)S(1)}, bf16[512,128]{1,0:T(8,128)(2,1)S(1)}, u32[]{:S(2)}, u32[]{:S(2)}) collective-permute-start(bf16[512,128]{1,0:T(8,128)(2,1)S(1)} %get-tuple-element.58), channel_id=1, source_target_pairs={{0,2},{1,3},{2,0},{3,1},{4,6},{5,7},{6,4},{7,5},{8,10},{9,11},{10,... | collective-permute-start | bytes 393224 | tf_op jit(solution)/shard_map/ppermute | solution.py:458
  71.8 6.5 %collective-permute-start.12 = (bf16[512,128]{1,0:T(8,128)(2,1)S(1)}, bf16[512,128]{1,0:T(8,128)(2,1)S(1)}, u32[]{:S(2)}, u32[]{:S(2)}) collective-permute-start(bf16[512,128]{1,0:T(8,128)(2,1)S(1)} %get-tuple-element.59), channel_id=1, source_target_pairs={{0,3},{1,0},{2,1},{3,2},{4,7},{5,4},{6,5},{7,6},{8,11},{9,8},{10,9... | collective-permute-start | bytes 393224 | tf_op jit(solution)/shard_map/ppermute | solution.py:458
  79.3 11.7 %collective-permute-start.13 = (bf16[768,128]{1,0:T(8,128)(2,1)S(1)}, bf16[768,128]{1,0:T(8,128)(2,1)S(1)}, u32[]{:S(2)}, u32[]{:S(2)}) collective-permute-start(bf16[768,128]{1,0:T(8,128)(2,1)S(1)} %get-tuple-element.62.refs_0_), channel_id=1, source_target_pairs={{0,1},{1,2},{2,3},{3,0},{4,5},{5,6},{6,7},{7,4},{8,9},{9,10},{10,1... | collective-permute-start | bytes 589832 | tf_op jit(solution)/shard_map/ppermute | solution.py:458
  80.1 10.9 %collective-permute-start.14 = (bf16[768,128]{1,0:T(8,128)(2,1)S(1)}, bf16[768,128]{1,0:T(8,128)(2,1)S(1)}, u32[]{:S(2)}, u32[]{:S(2)}) collective-permute-start(bf16[768,128]{1,0:T(8,128)(2,1)S(1)} %get-tuple-element.62.refs_0_), channel_id=1, source_target_pairs={{0,2},{1,3},{2,0},{3,1},{4,6},{5,7},{6,4},{7,5},{8,10},{9,11},{10,... | collective-permute-start | bytes 589832 | tf_op jit(solution)/shard_map/ppermute | solution.py:458
  81.0 10.1 %collective-permute-start.15 = (bf16[768,128]{1,0:T(8,128)(2,1)S(1)}, bf16[768,128]{1,0:T(8,128)(2,1)S(1)}, u32[]{:S(2)}, u32[]{:S(2)}) collective-permute-start(bf16[768,128]{1,0:T(8,128)(2,1)S(1)} %get-tuple-element.62.refs_0_), channel_id=1, source_target_pairs={{0,3},{1,0},{2,1},{3,2},{4,7},{5,4},{6,5},{7,6},{8,11},{9,8},{10,9... | collective-permute-start | bytes 589832 | tf_op jit(solution)/shard_map/ppermute | solution.py:458
  91.1 10.0 %collective-permute-start.16 = (f32[256,128]{1,0:T(8,128)S(1)}, f32[256,128]{1,0:T(8,128)S(1)}, u32[]{:S(2)}, u32[]{:S(2)}) collective-permute-start(f32[256,128]{1,0:T(8,128)S(1)} %convert_add_fusion), channel_id=1, source_target_pairs={{0,32},{1,33},{8,40},{9,41},{16,48},{17,49},{24,56},{25,57},{32,0}... | collective-permute-start | bytes 393224 | tf_op jit(solution)/shard_map/ppermute | solution.py:443
  99.3 9.7 %collective-permute-start.21 = (bf16[2048,128]{1,0:T(8,128)(2,1)S(1)}, bf16[2048,128]{1,0:T(8,128)(2,1)S(1)}, u32[]{:S(2)}, u32[]{:S(2)}) collective-permute-start(bf16[2048,128]{1,0:T(8,128)(2,1)S(1)} %get-tuple-element.80), channel_id=1, source_target_pairs={{0,7},{1,4},{8,15},{9,12},{16,23},{17,20},{24,31},{25,28},{32,39},... | collective-permute-start | bytes 1572872 | tf_op jit(solution)/shard_map/ppermute | solution.py:443
  99.4 14.4 %collective-permute-start.17 = (bf16[2048,128]{1,0:T(8,128)(2,1)S(1)}, bf16[2048,128]{1,0:T(8,128)(2,1)S(1)}, u32[]{:S(2)}, u32[]{:S(2)}) collective-permute-start(bf16[2048,128]{1,0:T(8,128)(2,1)S(1)} %get-tuple-element.69), channel_id=1, source_target_pairs={{0,7},{1,4},{8,15},{9,12},{16,23},{17,20},{24,31},{25,28},{32,39},... | collective-permute-start | bytes 1572872 | tf_op jit(solution)/shard_map/ppermute | solution.py:443
  109.2 8.3 %collective-permute-start.22 = (bf16[1024,128]{1,0:T(8,128)(2,1)S(1)}, bf16[1024,128]{1,0:T(8,128)(2,1)S(1)}, u32[]{:S(2)}, u32[]{:S(2)}) collective-permute-start(bf16[1024,128]{1,0:T(8,128)(2,1)S(1)} %get-tuple-element.99), channel_id=1, source_target_pairs={{0,32},{1,33},{8,40},{9,41},{16,48},{17,49},{24,56},{25,57},{32,64... | collective-permute-start | bytes 786440 | tf_op jit(solution)/shard_map/ppermute | solution.py:443
  110.7 8.9 %collective-permute-start.24 = (bf16[2048,128]{1,0:T(8,128)(2,1)S(1)}, bf16[2048,128]{1,0:T(8,128)(2,1)S(1)}, u32[]{:S(2)}, u32[]{:S(2)}) collective-permute-start(bf16[2048,128]{1,0:T(8,128)(2,1)S(1)} %get-tuple-element.82), channel_id=1, source_target_pairs={{0,7},{1,4},{8,15},{9,12},{16,23},{17,20},{24,31},{25,28},{32,39},... | collective-permute-start | bytes 1572872 | tf_op jit(solution)/shard_map/ppermute | solution.py:443
  110.7 24.1 %collective-permute-start.19 = (bf16[2048,128]{1,0:T(8,128)(2,1)S(1)}, bf16[2048,128]{1,0:T(8,128)(2,1)S(1)}, u32[]{:S(2)}, u32[]{:S(2)}) collective-permute-start(bf16[2048,128]{1,0:T(8,128)(2,1)S(1)} %get-tuple-element.71), channel_id=1, source_target_pairs={{0,7},{1,4},{8,15},{9,12},{16,23},{17,20},{24,31},{25,28},{32,39},... | collective-permute-start | bytes 1572872 | tf_op jit(solution)/shard_map/ppermute | solution.py:443
  113.8 7.1 %collective-permute-start.25 = (bf16[1024,128]{1,0:T(8,128)(2,1)S(1)}, bf16[1024,128]{1,0:T(8,128)(2,1)S(1)}, u32[]{:S(2)}, u32[]{:S(2)}) collective-permute-start(bf16[1024,128]{1,0:T(8,128)(2,1)S(1)} %get-tuple-element.100), channel_id=1, source_target_pairs={{0,96},{1,97},{8,104},{9,105},{16,112},{17,113},{24,120},{25,121},... | collective-permute-start | bytes 786440 | tf_op jit(solution)/shard_map/ppermute | solution.py:443
  117.7 21.0 %collective-permute-start.23 = (bf16[2048,128]{1,0:T(8,128)(2,1)S(1)}, bf16[2048,128]{1,0:T(8,128)(2,1)S(1)}, u32[]{:S(2)}, u32[]{:S(2)}) collective-permute-start(bf16[2048,128]{1,0:T(8,128)(2,1)S(1)} %pad_maximum_fusion), channel_id=1, source_target_pairs={{0,32},{1,33},{8,40},{9,41},{16,48},{17,49},{24,56},{25,57},{32,64... | collective-permute-start | bytes 1572872 | tf_op jit(solution)/shard_map/ppermute | solution.py:443
  121.1 17.7 %collective-permute-start.26 = (bf16[2048,128]{1,0:T(8,128)(2,1)S(1)}, bf16[2048,128]{1,0:T(8,128)(2,1)S(1)}, u32[]{:S(2)}, u32[]{:S(2)}) collective-permute-start(bf16[2048,128]{1,0:T(8,128)(2,1)S(1)} %pad_maximum_fusion.1), channel_id=1, source_target_pairs={{0,96},{1,97},{8,104},{9,105},{16,112},{17,113},{24,120},{25,121},... | collective-permute-start | bytes 1572872 | tf_op jit(solution)/shard_map/ppermute | solution.py:443
  124.5 10.3 %collective-permute-start.18 = (f32[256,128]{1,0:T(8,128)S(1)}, f32[256,128]{1,0:T(8,128)S(1)}, u32[]{:S(2)}, u32[]{:S(2)}) collective-permute-start(f32[256,128]{1,0:T(8,128)S(1)} %add.310), channel_id=1, source_target_pairs={{0,96},{1,97},{8,104},{9,105},{16,112},{17,113},{24,120},{25,121},... | collective-permute-start | bytes 393224 | tf_op jit(solution)/shard_map/ppermute | solution.py:443
  134.8 3.9 %collective-permute-start.20 = (f32[256,128]{1,0:T(8,128)S(1)}, f32[256,128]{1,0:T(8,128)S(1)}, u32[]{:S(2)}, u32[]{:S(2)}) collective-permute-start(f32[256,128]{1,0:T(8,128)S(1)} %add.311), channel_id=1, source_target_pairs={{0,8},{1,9},{8,0},{9,1},{16,24},{17,25},{24,16},{25,17},{32,40},{3... | collective-permute-start | bytes 393224 | tf_op jit(solution)/shard_map/ppermute | solution.py:443
  138.8 16.2 %copy-start.4 = (s32[1,2048]{1,0:T(1,128)S(1)}, s32[1,2048]{1,0:T(1,128)}, u32[]{:S(2)}) copy-start(s32[1,2048]{1,0:T(1,128)} %order_ref.3) | copy-start | bytes 24580
  139.1 15.9 %collective-permute-start.28 = (bf16[2048,128]{1,0:T(8,128)(2,1)S(1)}, bf16[2048,128]{1,0:T(8,128)(2,1)S(1)}, u32[]{:S(2)}, u32[]{:S(2)}) collective-permute-start(bf16[2048,128]{1,0:T(8,128)(2,1)S(1)} %add_convert_fusion), channel_id=1, source_target_pairs={{0,0},{1,23},{8,8},{9,31},{16,16},{17,7},{24,24},{25,15},{32,32},{... | collective-permute-start | bytes 1572872 | tf_op jit(solution)/shard_map/ppermute | solution.py:443
  146.3 8.6 %collective-permute-start.27 = (f32[256,128]{1,0:T(8,128)S(1)}, f32[256,128]{1,0:T(8,128)S(1)}, u32[]{:S(2)}, u32[]{:S(2)}) collective-permute-start(f32[256,128]{1,0:T(8,128)S(1)} %add.312), channel_id=1, source_target_pairs={{0,24},{1,25},{8,16},{9,17},{16,8},{17,9},{24,0},{25,1},{32,56},{3... | collective-permute-start | bytes 393224 | tf_op jit(solution)/shard_map/ppermute | solution.py:443
  154.9 15.2 %collective-permute-start.29 = (f32[256,128]{1,0:T(8,128)S(1)}, f32[256,128]{1,0:T(8,128)S(1)}, u32[]{:S(2)}, u32[]{:S(2)}) collective-permute-start(f32[256,128]{1,0:T(8,128)S(1)} %add.323), channel_id=1, source_target_pairs={{0,4},{1,5},{8,12},{9,13},{16,20},{17,21},{24,28},{25,29},{32,36},... | collective-permute-start | bytes 393224 | tf_op jit(solution)/shard_map/ppermute | solution.py:443
  157.5 14.9 %collective-permute-start.30 = (bf16[512,128]{1,0:T(8,128)(2,1)S(1)}, bf16[512,128]{1,0:T(8,128)(2,1)S(1)}, u32[]{:S(2)}, u32[]{:S(2)}) collective-permute-start(bf16[512,128]{1,0:T(8,128)(2,1)S(1)} %get-tuple-element.88), channel_id=1, source_target_pairs={{0,1},{1,2},{2,3},{3,0},{4,5},{5,6},{6,7},{7,4},{8,9},{9,10},{10,1... | collective-permute-start | bytes 393224 | tf_op jit(solution)/shard_map/ppermute | solution.py:458
  169.7 6.2 %collective-permute-start.31 = (bf16[512,128]{1,0:T(8,128)(2,1)S(1)}, bf16[512,128]{1,0:T(8,128)(2,1)S(1)}, u32[]{:S(2)}, u32[]{:S(2)}) collective-permute-start(bf16[512,128]{1,0:T(8,128)(2,1)S(1)} %get-tuple-element.89), channel_id=1, source_target_pairs={{0,2},{1,3},{2,0},{3,1},{4,6},{5,7},{6,4},{7,5},{8,10},{9,11},{10,... | collective-permute-start | bytes 393224 | tf_op jit(solution)/shard_map/ppermute | solution.py:458
  169.7 6.7 %collective-permute-start.32 = (bf16[512,128]{1,0:T(8,128)(2,1)S(1)}, bf16[512,128]{1,0:T(8,128)(2,1)S(1)}, u32[]{:S(2)}, u32[]{:S(2)}) collective-permute-start(bf16[512,128]{1,0:T(8,128)(2,1)S(1)} %get-tuple-element.90), channel_id=1, source_target_pairs={{0,3},{1,0},{2,1},{3,2},{4,7},{5,4},{6,5},{7,6},{8,11},{9,8},{10,9... | collective-permute-start | bytes 393224 | tf_op jit(solution)/shard_map/ppermute | solution.py:458

commit v2 on v1

--- a/solution.py
+++ b/solution.py
@@ -16,6 +16,7 @@
 FORWARD_WAVES = ((0, 1, 3, 2), (4, 5, 7, 6))
 BACKWARD_WAVES = ((4, 5, 6, 7), (0, 1, 2, 3))
 PAIR = 2
+PARTS = 4
 CODE = 256
 VMEM_LIMIT = 12 * 1024 * 1024
 HOLD_LIMIT = 32 * 1024 * 1024
@@ -121,16 +122,20 @@
 
 def hold_kernel(items, place_ref, tiles_ref, out_ref, sems):
     per_slot = out_ref.shape[0] // len(items)
+    part = per_slot // PARTS
     copies = []
     for number, item in enumerate(items):
-        copies.append(
-            pltpu.make_async_copy(
-                tiles_ref.at[pl.ds(place_ref[1 + item] * per_slot, per_slot)],
-                out_ref.at[pl.ds(number * per_slot, per_slot)],
-                sems.at[number],
+        for piece in range(PARTS):
+            source = place_ref[1 + item] * per_slot + piece * part
+            target = number * per_slot + piece * part
+            copies.append(
+                pltpu.make_async_copy(
+                    tiles_ref.at[pl.ds(source, part)],
+                    out_ref.at[pl.ds(target, part)],
+                    sems.at[number * PARTS + piece],
+                )
             )
-        )
-        copies[-1].start()
+            copies[-1].start()
     for copy in copies:
         copy.wait()
 
@@ -145,7 +150,7 @@
             grid=(),
             in_specs=[pl.BlockSpec(memory_space=pltpu.HBM)],
             out_specs=whole(),
-            scratch_shapes=[pltpu.SemaphoreType.DMA((len(items),))],
+            scratch_shapes=[pltpu.SemaphoreType.DMA((len(items) * PARTS,))],
         ),
         compiler_params=params(HOLD_LIMIT),
         cost_estimate=pl.CostEstimate(
@@ -462,8 +467,12 @@
     near = moved(blocked, fetch_pairs())
     above, below = down(near), up(near)
     far = swapped(near)
-    above, far = lax.optimization_barrier((above, far))
+    known, near = lax.optimization_barrier((place, near))
+    held = [hold(FORWARD_WAVES[0], known, tiles, per_slot)]
+    above, below, far, held[0] = lax.optimization_barrier((above, below, far, held[0]))
     middle = [down(above[:half]), up(below[half:])]
+    known, far = lax.optimization_barrier((place, far))
+    held.append(hold(FORWARD_WAVES[1], known, tiles, per_slot))
     arrived = {0: [near], 1: [above], 2: middle, 3: [below], 4: [far], 5: [swapped(above)]}
     arrived[6] = [swapped(value) for value in middle]
     arrived[7] = [swapped(below)]
@@ -486,16 +495,11 @@
         FORWARD_TURN,
     )
     packed = jnp.concatenate([packed, own_rep])
-    places = []
-    for item in (0, 1):
-        known, arrived[item][0] = lax.optimization_barrier((place, arrived[item][0]))
-        places.append(known)
     total = None
     for wave, items in enumerate(FORWARD_WAVES):
         xs = sum([arrived[item] for item in items], [])
-        held = hold(items, places[wave], tiles, per_slot)
         total = forward_product(
-            rows_dev, waves, wave, packed, capacity, held, xs, total, reps
+            rows_dev, waves, wave, packed, capacity, held[wave], xs, total, reps
         )
     total = list(total)
     last_cells, total[0] = lax.optimization_barrier((cells, total[0]))
@@ -540,7 +544,7 @@
     returned = {item: swapped(others[item]) for item in (2, 1, 3, 0)}
     mine = products(1, packed)
     two = added(mine[2], returned[2])
-    from_below, from_above = up(two[:half]), down(two[half:])
+    from_below, from_above = lax.optimization_barrier((up(two[:half]), down(two[half:])))
     grad_weight, returned[1] = next_after(grad_weight, returned[1])
     one = jnp.concatenate(
         [added(mine[1][:half], returned[1][:half], from_below), added(mine[1][half:], returned[1][half:])]
@@ -549,11 +553,11 @@
         [added(mine[3][:half], returned[3][:half]), added(mine[3][half:], returned[3][half:], from_above)]
     )
     onward = [up(one), down(three)]
-    grad_weight, returned[0] = next_after(grad_weight, returned[0])
     ended = added(mine[0], returned[0], *onward)
     grad_weight, ended = next_after(grad_weight, ended)
     home = moved(ended, [(user, owner) for owner, user in fetch_pairs()])
     grad_weight, home = next_after(grad_weight, home)
+    grad_weight = grad_weight + moved(grad_weight, todo.pop(0))
     terms = to_reps(restore(own_rep, node_order, home, reps))
     grad_features = added(*terms)
     stacked = grad_weight.reshape(weight.shape[1] // TILE, weight.shape[0], TILE)

time: 177 us -> 174 us (0.983)
  waiting for transfers between devices: 53 us -> 44.4 us
  local copies, waits for them, and re-layouts: 4.62 us -> 9.53 us
  starting transfers between devices: 56.1 us -> 54.2 us
  Pallas kernels: 54.9 us -> 56.7 us
    ppermute x9, starting transfers between devices: 19.6 us -> 13.2 us  [to_reps(): received.append(lax.ppermute(values[shift], 'rep', along))]
    ppermute x24, waiting for transfers between devices: 42.5 us -> 36.3 us  [moved(): return lax.ppermute(value, both, listed)]
    ppermute x24, starting transfers between devices: 36.5 us -> 41 us  [moved(): return lax.ppermute(value, both, listed)]
    unnamed x11 -> x27, local copies, waits for them, and re-layouts: 1.75 us -> 5.88 us
    ppermute x9, waiting for transfers between devices: 10.5 us -> 8.02 us  [to_reps(): received.append(lax.ppermute(values[shift], 'rep', along))]
  transfers between devices with their start and end apart: 33 -> 33, of which waited for: 15 -> 12; matrix products, arithmetic and copies ran while one was open for 5% -> 5% of each run, Pallas kernels for 25% -> 25%
where the time goes in v2:
time: 174 us; the launch traced here: 173 us
  Pallas kernels  56.7 us (33%)
  starting transfers between devices  54.2 us (31%)
  waiting for transfers between devices  44.4 us (26%)
  local copies, waits for them, and re-layouts  9.53 us (5%)
  other arithmetic  7.41 us (4%)
    ppermute x24, starting transfers between devices, moved(): return lax.ppermute(value, both, listed)  41 us
    ppermute x24, waiting for transfers between devices, moved(): return lax.ppermute(value, both, listed)  36.3 us
    pallas_call x4, Pallas kernels, hold(): pl.pallas_call(functools.partial(hold_kernel, items), out_shape=jax.Shape...  18.9 us
    pallas_call x2, Pallas kernels, forward_product(): pl.pallas_call(functools.partial(forward_kernel, len(xs), lists, wave, ca...  16 us
    pallas_call x2, Pallas kernels, backward_product(): pl.pallas_call(functools.partial(backward_kernel, count, lists, first, ca...  15.9 us
    ppermute x9, starting transfers between devices, to_reps(): received.append(lax.ppermute(values[shift], 'rep', along))  13.2 us
    ppermute x9, waiting for transfers between devices, to_reps(): received.append(lax.ppermute(values[shift], 'rep', along))  8.02 us
    unnamed x27, local copies, waits for them, and re-layouts  5.88 us
  transfers between devices with their start and end apart: 33, of which 12 were waited for; matrix products, arithmetic and copies ran while one was open for 5% of the time, Pallas kernels for 25%

profile of v2, /device:TPU:1, one launch (start us, length us, event | category | flops | bytes accessed | tf_op | source)
XLA Modules:
  0.0 173.4 jit_solution(11610209998685316582)
XLA Ops:
  0.6 1.0 copy-done.1
  1.7 0.7 copy-done.4
  2.4 2.4 %shard_map.112 = bf16[2048,128]{1,0:T(8,128)(2,1)S(1)} custom-call(s32[1,2048]{1,0:T(1,128)S(1)} %copy-done.4, bf16[2048,128]{1,0:T(8,128)(2,1)S(1)} %copy-done.1), custom_call_target="tpu_custom_call" | custom-call | tf_op jit(solution)/shard_map/pallas_call | solution.py:114
  4.7 5.3 %collective-permute-start = (bf16[2048,128]{1,0:T(8,128)(2,1)S(1)}, bf16[2048,128]{1,0:T(8,128)(2,1)S(1)}, u32[]{:S(2)}, u32[]{:S(2)}) collective-permute-start(bf16[2048,128]{1,0:T(8,128)(2,1)S(1)} %shard_map.112), channel_id=1, source_target_pairs={{0,0},{23,1},{8,8},{31,9},{16,16},{7,17},{24,24},{15,25},{32,32},{... | collective-permute-start | bytes 1572872 | tf_op jit(solution)/shard_map/ppermute | solution.py:448
  10.1 0.7 fusion.14
  10.8 0.7 compare_and_fusion
  11.5 0.8 bitcast_select_fusion
  12.2 0.6 gather_fusion
  13.5 0.4 convert_reduce_fusion
  13.9 0.3 select_reduce_fusion.1
  14.3 5.5 %collective-permute-done.refs_0_ = bf16[2048,128]{1,0:T(8,128)(2,1)S(1)} collective-permute-done((bf16[2048,128]{1,0:T(8,128)(2,1)S(1)}, bf16[2048,128]{1,0:T(8,128)(2,1)S(1)}, u32[]{:S(2)}, u32[]{:S(2)}) %collective-permute-start) | collective-permute-done | bytes 524320 | tf_op jit(solution)/shard_map/ppermute | solution.py:448
  19.8 2.7 %collective-permute-start.1 = (bf16[2048,128]{1,0:T(8,128)(2,1)S(1)}, bf16[2048,128]{1,0:T(8,128)(2,1)S(1)}, u32[]{:S(2)}, u32[]{:S(2)}) collective-permute-start(bf16[2048,128]{1,0:T(8,128)(2,1)S(1)} %collective-permute-done.refs_0_), channel_id=1, source_target_pairs={{0,96},{1,97},{8,104},{9,105},{16,112},{17,113},{24,120},{25,121},... | collective-permute-start | bytes 1572872 | tf_op jit(solution)/shard_map/ppermute | solution.py:448
  23.0 0.7 dynamic-slice_bitcast_fusion
  23.8 4.7 %shard_map.113.hold_ref = bf16[320,128,128]{2,1,0:T(8,128)(2,1)S(1)} custom-call(s32[9]{0:T(128)S(1)} %pad_add_fusion.2.place_ref, bf16[640,128,128]{2,1,0:T(8,128)(2,1)} %bitcast.18), custom_call_target="tpu_custom_call" | custom-call | bytes 20971520 | tf_op jit(solution)/shard_map/pallas_call | solution.py:145
  28.5 4.0 %copy-done = bf16[320,128,128]{2,1,0:T(8,128)(2,1)} copy-done((bf16[320,128,128]{2,1,0:T(8,128)(2,1)}, bf16[320,128,128]{2,1,0:T(8,128)(2,1)S(1)}, u32[]{:S(2)}) %copy-start) | copy-done | bytes 10485784
  32.5 0.8 slice.98
  33.4 2.7 %collective-permute-start.6 = (bf16[1024,128]{1,0:T(8,128)(2,1)}, bf16[1024,128]{1,0:T(8,128)(2,1)S(1)}, u32[]{:S(2)}, u32[]{:S(2)}) collective-permute-start(bf16[1024,128]{1,0:T(8,128)(2,1)} %slice.98), channel_id=1, source_target_pairs={{0,96},{1,97},{8,104},{9,105},{16,112},{17,113},{24,120},{25,121},... | collective-permute-start | bytes 786440 | tf_op jit(solution)/shard_map/ppermute | solution.py:448
  36.0 0.7 slice.99
  36.9 2.1 %collective-permute-start.4 = (bf16[2048,128]{1,0:T(8,128)(2,1)S(1)}, bf16[2048,128]{1,0:T(8,128)(2,1)}, u32[]{:S(2)}, u32[]{:S(2)}) collective-permute-start(bf16[2048,128]{1,0:T(8,128)(2,1)S(1)} %collective-permute-done.1.refs_1_), channel_id=1, source_target_pairs={{0,7},{1,4},{8,15},{9,12},{16,23},{17,20},{24,31},{25,28},{32,39},... | collective-permute-start | bytes 1572872 | tf_op jit(solution)/shard_map/ppermute | solution.py:448
  39.2 4.9 %shard_map.114.hold_ref = bf16[320,128,128]{2,1,0:T(8,128)(2,1)S(1)} custom-call(s32[9]{0:T(128)S(1)} %pad_add_fusion.2.place_ref, bf16[640,128,128]{2,1,0:T(8,128)(2,1)} %bitcast.19), custom_call_target="tpu_custom_call" | custom-call | bytes 20971520 | tf_op jit(solution)/shard_map/pallas_call | solution.py:145
  44.2 1.7 collective-permute-start.7
  45.9 2.9 %collective-permute-start.9 = (bf16[1024,128]{1,0:T(8,128)(2,1)}, bf16[1024,128]{1,0:T(8,128)(2,1)S(1)}, u32[]{:S(2)}, u32[]{:S(2)}) collective-permute-start(bf16[1024,128]{1,0:T(8,128)(2,1)} %collective-permute-done.8.refs_4_), channel_id=1, source_target_pairs={{0,7},{1,4},{8,15},{9,12},{16,23},{17,20},{24,31},{25,28},{32,39},... | collective-permute-start | bytes 786440 | tf_op jit(solution)/shard_map/ppermute | solution.py:448
  48.8 7.8 %shard_map.115.refs_5_ = f32[2176,128]{1,0:T(8,128)S(1)} custom-call(s32[1011]{0:T(1024)S(1)} %pad_add_fusion.list_ref, bf16[320,128,128]{2,1,0:T(8,128)(2,1)S(1)} %bitcast.17, bf16[2048,128]{1,0:T(8,128)(2,1)S(1)} %copy-done.7, bf16[2048,128]{1,0:T(8,128)(2,1)S(1)} %collective-permute-done.1.refs_1_, bf16[2048,128]{1,0:T(8,128)(2,1)S(1)} %collective-permute-done.2.refs_2_, ...), custom_call_target="tpu_custom_call" | custom-call | flops 5368709120 | bytes 10485760 | tf_op jit(solution)/shard_map/pallas_call | solution.py:270
  56.7 0.7 collective-permute-done.9.refs_4_
  57.4 8.2 %shard_map.116 = (bf16[512,128]{1,0:T(8,128)(2,1)S(1)}, bf16[512,128]{1,0:T(8,128)(2,1)S(1)}, bf16[512,128]{1,0:T(8,128)(2,1)S(1)}, bf16[512,128]{1,0:T(8,128)(2,1)S(1)}) custom-call(s32[1011]{0:T(1024)S(1)} %pad_add_fusion.list_ref, bf16[320,128,128]{2,1,0:T(8,128)(2,1)S(1)} %shard_map.114.hold_ref, bf16[2048,128]{1,0:T(8,128)(2,1)S(1)} %copy-done.9, ...), custom_call_target="tpu_custom_call" | custom-call | flops 5368709120 | bytes 10485760 | tf_op jit(solution)/shard_map/pallas_call | solution.py:270
  66.0 0.4 convert_reduce_fusion.1
  66.4 1.8 %collective-permute-start.10 = (bf16[512,128]{1,0:T(8,128)(2,1)S(1)}, bf16[512,128]{1,0:T(8,128)(2,1)S(1)}, u32[]{:S(2)}, u32[]{:S(2)}) collective-permute-start(bf16[512,128]{1,0:T(8,128)(2,1)S(1)} %get-tuple-element.59), channel_id=1, source_target_pairs={{0,1},{1,2},{2,3},{3,0},{4,5},{5,6},{6,7},{7,4},{8,9},{9,10},{10,1... | collective-permute-start | bytes 393224 | tf_op jit(solution)/shard_map/ppermute | solution.py:463
  68.2 3.2 %collective-permute-start.11 = (bf16[512,128]{1,0:T(8,128)(2,1)S(1)}, bf16[512,128]{1,0:T(8,128)(2,1)S(1)}, u32[]{:S(2)}, u32[]{:S(2)}) collective-permute-start(bf16[512,128]{1,0:T(8,128)(2,1)S(1)} %get-tuple-element.62), channel_id=1, source_target_pairs={{0,2},{1,3},{2,0},{3,1},{4,6},{5,7},{6,4},{7,5},{8,10},{9,11},{10,... | collective-permute-start | bytes 393224 | tf_op jit(solution)/shard_map/ppermute | solution.py:463
  71.4 0.7 collective-permute-start.12
  72.1 0.3 select_reduce_fusion.3
  72.9 4.1 %collective-permute-done.11.refs_2_ = bf16[512,128]{1,0:T(8,128)(2,1)S(1)} collective-permute-done((bf16[512,128]{1,0:T(8,128)(2,1)S(1)}, bf16[512,128]{1,0:T(8,128)(2,1)S(1)}, u32[]{:S(2)}, u32[]{:S(2)}) %collective-permute-start.11) | collective-permute-done | bytes 131104 | tf_op jit(solution)/shard_map/ppermute | solution.py:463
  77.0 0.9 collective-permute-done.12.refs_3_
  77.9 1.0 shard_map.117
  78.9 0.8 collective-permute-start.13
  79.7 0.8 collective-permute-start.14
  80.6 0.8 collective-permute-start.15
  81.3 4.7 %shard_map.118.hold_ref = bf16[320,128,128]{2,1,0:T(8,128)(2,1)S(1)} custom-call(s32[9]{0:T(128)S(1)} %pad_add_fusion.2.place_ref, bf16[640,128,128]{2,1,0:T(8,128)(2,1)} %bitcast.20), custom_call_target="tpu_custom_call" | custom-call | bytes 20971520 | tf_op jit(solution)/shard_map/pallas_call | solution.py:145
  86.0 4.7 %shard_map.119.hold_ref = bf16[320,128,128]{2,1,0:T(8,128)(2,1)S(1)} custom-call(s32[9]{0:T(128)S(1)} %pad_add_fusion.2.place_ref, bf16[640,128,128]{2,1,0:T(8,128)(2,1)} %bitcast.21), custom_call_target="tpu_custom_call" | custom-call | bytes 20971520 | tf_op jit(solution)/shard_map/pallas_call | solution.py:145
  90.9 8.1 %shard_map.120 = (bf16[2048,128]{1,0:T(8,128)(2,1)S(1)}, bf16[2048,128]{1,0:T(8,128)(2,1)S(1)}, bf16[2048,128]{1,0:T(8,128)(2,1)S(1)}, bf16[2048,128]{1,0:T(8,128)(2,1)S(1)}) custom-call(s32[1285]{0:T(1024)S(1)} %concatenate.36.list_ref, bf16[320,128,128]{2,1,0:T(8,128)(2,1)S(1)} %shard_map.118.hold_ref, bf16[768,128]{1,0:T(8,128)(2,1)S(1)} %get-tuple-element.66.refs_0_, ...), custom_call_target="tpu_custom_call" | custom-call | flops 5368709120 | bytes 10485760 | tf_op jit(solution)/shard_map/pallas_call | solution.py:372
  99.0 1.7 collective-permute-start.17
  100.7 7.9 %shard_map.121 = (bf16[2048,128]{1,0:T(8,128)(2,1)S(1)}, bf16[2048,128]{1,0:T(8,128)(2,1)S(1)}, bf16[2048,128]{1,0:T(8,128)(2,1)S(1)}, bf16[2048,128]{1,0:T(8,128)(2,1)S(1)}) custom-call(s32[1285]{0:T(1024)S(1)} %concatenate.36.list_ref, bf16[320,128,128]{2,1,0:T(8,128)(2,1)S(1)} %shard_map.119.hold_ref, bf16[768,128]{1,0:T(8,128)(2,1)S(1)} %get-tuple-element.66.refs_0_, ...), custom_call_target="tpu_custom_call" | custom-call | flops 5368709120 | bytes 10485760 | tf_op jit(solution)/shard_map/pallas_call | solution.py:372
  108.9 2.7 %collective-permute-start.22 = (bf16[1024,128]{1,0:T(8,128)(2,1)S(1)}, bf16[1024,128]{1,0:T(8,128)(2,1)S(1)}, u32[]{:S(2)}, u32[]{:S(2)}) collective-permute-start(bf16[1024,128]{1,0:T(8,128)(2,1)S(1)} %get-tuple-element.103), channel_id=1, source_target_pairs={{0,96},{1,97},{8,104},{9,105},{16,112},{17,113},{24,120},{25,121},... | collective-permute-start | bytes 786440 | tf_op jit(solution)/shard_map/ppermute | solution.py:448
  111.6 1.8 %collective-permute-start.19 = (bf16[2048,128]{1,0:T(8,128)(2,1)S(1)}, bf16[2048,128]{1,0:T(8,128)(2,1)S(1)}, u32[]{:S(2)}, u32[]{:S(2)}) collective-permute-start(bf16[2048,128]{1,0:T(8,128)(2,1)S(1)} %get-tuple-element.78), channel_id=1, source_target_pairs={{0,7},{1,4},{8,15},{9,12},{16,23},{17,20},{24,31},{25,28},{32,39},... | collective-permute-start | bytes 1572872 | tf_op jit(solution)/shard_map/ppermute | solution.py:448
  113.5 4.4 %collective-permute-done.21 = bf16[1024,128]{1,0:T(8,128)(2,1)S(1)} collective-permute-done((bf16[1024,128]{1,0:T(8,128)(2,1)S(1)}, bf16[1024,128]{1,0:T(8,128)(2,1)S(1)}, u32[]{:S(2)}, u32[]{:S(2)}) %collective-permute-start.21) | collective-permute-done | bytes 262176 | tf_op jit(solution)/shard_map/ppermute | solution.py:448
  118.0 0.2 add_convert_fusion.5
  118.3 2.2 %collective-permute-done.24 = bf16[2048,128]{1,0:T(8,128)(2,1)S(1)} collective-permute-done((bf16[2048,128]{1,0:T(8,128)(2,1)S(1)}, bf16[2048,128]{1,0:T(8,128)(2,1)S(1)}, u32[]{:S(2)}, u32[]{:S(2)}) %collective-permute-start.24) | collective-permute-done | bytes 524320 | tf_op jit(solution)/shard_map/ppermute | solution.py:448
  120.5 0.2 add_convert_fusion.3
  120.7 0.8 collective-permute-start.25
  121.5 1.4 collective-permute-start.18
  123.0 13.3 %collective-permute-done.18 = f32[256,128]{1,0:T(8,128)S(1)} collective-permute-done((f32[256,128]{1,0:T(8,128)S(1)}, f32[256,128]{1,0:T(8,128)S(1)}, u32[]{:S(2)}, u32[]{:S(2)}) %collective-permute-start.18) | collective-permute-done | bytes 131104 | tf_op jit(solution)/shard_map/ppermute | solution.py:448
  136.3 0.3 add_convert_fusion
  136.6 5.4 %collective-permute-start.27 = (bf16[2048,128]{1,0:T(8,128)(2,1)S(1)}, bf16[2048,128]{1,0:T(8,128)(2,1)S(1)}, u32[]{:S(2)}, u32[]{:S(2)}) collective-permute-start(bf16[2048,128]{1,0:T(8,128)(2,1)S(1)} %add_convert_fusion), channel_id=1, source_target_pairs={{0,0},{1,23},{8,8},{9,31},{16,16},{17,7},{24,24},{25,15},{32,32},{... | collective-permute-start | bytes 1572872 | tf_op jit(solution)/shard_map/ppermute | solution.py:448
  142.0 1.8 %collective-permute-start.26 = (f32[256,128]{1,0:T(8,128)S(1)}, f32[256,128]{1,0:T(8,128)S(1)}, u32[]{:S(2)}, u32[]{:S(2)}) collective-permute-start(f32[256,128]{1,0:T(8,128)S(1)} %add.311), channel_id=1, source_target_pairs={{0,8},{1,9},{8,0},{9,1},{16,24},{17,25},{24,16},{25,17},{32,40},{3... | collective-permute-start | bytes 393224 | tf_op jit(solution)/shard_map/ppermute | solution.py:448
  143.8 5.5 %collective-permute-done.26 = f32[256,128]{1,0:T(8,128)S(1)} collective-permute-done((f32[256,128]{1,0:T(8,128)S(1)}, f32[256,128]{1,0:T(8,128)S(1)}, u32[]{:S(2)}, u32[]{:S(2)}) %collective-permute-start.26) | collective-permute-done | bytes 131104 | tf_op jit(solution)/shard_map/ppermute | solution.py:448
  149.3 2.5 %shard_map.122 = (bf16[512,128]{1,0:T(8,128)(2,1)S(1)}, bf16[512,128]{1,0:T(8,128)(2,1)S(1)}, bf16[512,128]{1,0:T(8,128)(2,1)S(1)}, bf16[512,128]{1,0:T(8,128)(2,1)S(1)}) custom-call(s32[1]{0:T(128)} %bitcast.5.place_ref, s32[1,2048]{1,0:T(1,128)S(1)} %copy-done.5, bf16[2048,128]{1,0:T(8,128)(2,1)S(1)} %collective-permute-done.27.home_ref), custom_call_target="tpu_custom_call" | custom-call | tf_op jit(solution)/shard_map/pallas_call | solution.py:412
  151.8 4.2 %collective-permute-start.28 = (f32[256,128]{1,0:T(8,128)S(1)}, f32[256,128]{1,0:T(8,128)S(1)}, u32[]{:S(2)}, u32[]{:S(2)}) collective-permute-start(f32[256,128]{1,0:T(8,128)S(1)} %add.322), channel_id=1, source_target_pairs={{0,24},{1,25},{8,16},{9,17},{16,8},{17,9},{24,0},{25,1},{32,56},{3... | collective-permute-start | bytes 393224 | tf_op jit(solution)/shard_map/ppermute | solution.py:448
  156.1 4.6 %collective-permute-start.30 = (bf16[512,128]{1,0:T(8,128)(2,1)S(1)}, bf16[512,128]{1,0:T(8,128)(2,1)S(1)}, u32[]{:S(2)}, u32[]{:S(2)}) collective-permute-start(bf16[512,128]{1,0:T(8,128)(2,1)S(1)} %get-tuple-element.92), channel_id=1, source_target_pairs={{0,1},{1,2},{2,3},{3,0},{4,5},{5,6},{6,7},{7,4},{8,9},{9,10},{10,1... | collective-permute-start | bytes 393224 | tf_op jit(solution)/shard_map/ppermute | solution.py:463
  160.7 0.4 collective-permute-start.32
  161.1 3.2 %collective-permute-start.29 = (f32[256,128]{1,0:T(8,128)S(1)}, f32[256,128]{1,0:T(8,128)S(1)}, u32[]{:S(2)}, u32[]{:S(2)}) collective-permute-start(f32[256,128]{1,0:T(8,128)S(1)} %add.323), channel_id=1, source_target_pairs={{0,4},{1,5},{8,12},{9,13},{16,20},{17,21},{24,28},{25,29},{32,36},... | collective-permute-start | bytes 393224 | tf_op jit(solution)/shard_map/ppermute | solution.py:448
  164.3 2.5 %collective-permute-done.31 = bf16[512,128]{1,0:T(8,128)(2,1)S(1)} collective-permute-done((bf16[512,128]{1,0:T(8,128)(2,1)S(1)}, bf16[512,128]{1,0:T(8,128)(2,1)S(1)}, u32[]{:S(2)}, u32[]{:S(2)}) %collective-permute-start.31) | collective-permute-done | bytes 131104 | tf_op jit(solution)/shard_map/ppermute | solution.py:463
  166.8 0.6 collective-permute-done.32
  167.4 0.7 add_convert_fusion.6
  168.1 4.5 %collective-permute-done.29 = f32[256,128]{1,0:T(8,128)S(1)} collective-permute-done((f32[256,128]{1,0:T(8,128)S(1)}, f32[256,128]{1,0:T(8,128)S(1)}, u32[]{:S(2)}, u32[]{:S(2)}) %collective-permute-start.29) | collective-permute-done | bytes 131104 | tf_op jit(solution)/shard_map/ppermute | solution.py:448
  172.7 0.7 pad_maximum_fusion.2
  (111 shorter events, 3.5 us)
Async XLA Ops:
  0.6 1.0 copy-start.1
  1.7 0.7 copy-start.4
  4.7 15.1 %collective-permute-start = (bf16[2048,128]{1,0:T(8,128)(2,1)S(1)}, bf16[2048,128]{1,0:T(8,128)(2,1)S(1)}, u32[]{:S(2)}, u32[]{:S(2)}) collective-permute-start(bf16[2048,128]{1,0:T(8,128)(2,1)S(1)} %shard_map.112), channel_id=1, source_target_pairs={{0,0},{23,1},{8,8},{31,9},{16,16},{7,17},{24,24},{15,25},{32,32},{... | collective-permute-start | bytes 1572872 | tf_op jit(solution)/shard_map/ppermute | solution.py:448
  19.8 8.6 %copy-start.6 = (bf16[2048,128]{1,0:T(8,128)(2,1)}, bf16[2048,128]{1,0:T(8,128)(2,1)S(1)}, u32[]{:S(2)}) copy-start(bf16[2048,128]{1,0:T(8,128)(2,1)S(1)} %collective-permute-done.refs_0_) | copy-start | bytes 1572868
  19.8 12.6 %collective-permute-start.1 = (bf16[2048,128]{1,0:T(8,128)(2,1)S(1)}, bf16[2048,128]{1,0:T(8,128)(2,1)S(1)}, u32[]{:S(2)}, u32[]{:S(2)}) collective-permute-start(bf16[2048,128]{1,0:T(8,128)(2,1)S(1)} %collective-permute-done.refs_0_), channel_id=1, source_target_pairs={{0,96},{1,97},{8,104},{9,105},{16,112},{17,113},{24,120},{25,121},... | collective-permute-start | bytes 1572872 | tf_op jit(solution)/shard_map/ppermute | solution.py:448
  22.6 9.9 %collective-permute-start.2 = (bf16[2048,128]{1,0:T(8,128)(2,1)S(1)}, bf16[2048,128]{1,0:T(8,128)(2,1)S(1)}, u32[]{:S(2)}, u32[]{:S(2)}) collective-permute-start(bf16[2048,128]{1,0:T(8,128)(2,1)S(1)} %collective-permute-done.refs_0_), channel_id=1, source_target_pairs={{0,32},{1,33},{8,40},{9,41},{16,48},{17,49},{24,56},{25,57},{32,64... | collective-permute-start | bytes 1572872 | tf_op jit(solution)/shard_map/ppermute | solution.py:448
  22.6 9.9 %collective-permute-start.3 = (bf16[2048,128]{1,0:T(8,128)(2,1)S(1)}, bf16[2048,128]{1,0:T(8,128)(2,1)S(1)}, u32[]{:S(2)}, u32[]{:S(2)}) collective-permute-start(bf16[2048,128]{1,0:T(8,128)(2,1)S(1)} %collective-permute-done.refs_0_), channel_id=1, source_target_pairs={{0,7},{1,4},{8,15},{9,12},{16,23},{17,20},{24,31},{25,28},{32,39},... | collective-permute-start | bytes 1572872 | tf_op jit(solution)/shard_map/ppermute | solution.py:448
  28.5 4.0 %copy-start = (bf16[320,128,128]{2,1,0:T(8,128)(2,1)}, bf16[320,128,128]{2,1,0:T(8,128)(2,1)S(1)}, u32[]{:S(2)}) copy-start(bf16[320,128,128]{2,1,0:T(8,128)(2,1)S(1)} %shard_map.113.hold_ref) | copy-start | bytes 31457284
  32.5 0.9 copy-start.8
  33.4 10.8 %collective-permute-start.6 = (bf16[1024,128]{1,0:T(8,128)(2,1)}, bf16[1024,128]{1,0:T(8,128)(2,1)S(1)}, u32[]{:S(2)}, u32[]{:S(2)}) collective-permute-start(bf16[1024,128]{1,0:T(8,128)(2,1)} %slice.98), channel_id=1, source_target_pairs={{0,96},{1,97},{8,104},{9,105},{16,112},{17,113},{24,120},{25,121},... | collective-permute-start | bytes 786440 | tf_op jit(solution)/shard_map/ppermute | solution.py:448
  36.0 12.8 %slice-start = ((s8[10485760]{0:T(1024)(128)(4,1)}), s8[2097152]{0:T(1024)(128)(4,1)S(1)}, s32[]{:S(2)}) async-start(s8[10485760]{0:T(1024)(128)(4,1)} %bitcast.16), calls=%async_computation | async-start | bytes 4194304
  36.8 9.2 %collective-permute-start.8 = (bf16[1024,128]{1,0:T(8,128)(2,1)}, bf16[1024,128]{1,0:T(8,128)(2,1)}, u32[]{:S(2)}, u32[]{:S(2)}) collective-permute-start(bf16[1024,128]{1,0:T(8,128)(2,1)} %slice.99), channel_id=1, source_target_pairs={{0,32},{1,33},{8,40},{9,41},{16,48},{17,49},{24,56},{25,57},{32,64... | collective-permute-start | bytes 786440 | tf_op jit(solution)/shard_map/ppermute | solution.py:448
  36.9 19.8 %collective-permute-start.4 = (bf16[2048,128]{1,0:T(8,128)(2,1)S(1)}, bf16[2048,128]{1,0:T(8,128)(2,1)}, u32[]{:S(2)}, u32[]{:S(2)}) collective-permute-start(bf16[2048,128]{1,0:T(8,128)(2,1)S(1)} %collective-permute-done.1.refs_1_), channel_id=1, source_target_pairs={{0,7},{1,4},{8,15},{9,12},{16,23},{17,20},{24,31},{25,28},{32,39},... | collective-permute-start | bytes 1572872 | tf_op jit(solution)/shard_map/ppermute | solution.py:448
  39.0 17.7 %collective-permute-start.5 = (bf16[2048,128]{1,0:T(8,128)(2,1)S(1)}, bf16[2048,128]{1,0:T(8,128)(2,1)}, u32[]{:S(2)}, u32[]{:S(2)}) collective-permute-start(bf16[2048,128]{1,0:T(8,128)(2,1)S(1)} %collective-permute-done.2.refs_2_), channel_id=1, source_target_pairs={{0,7},{1,4},{8,15},{9,12},{16,23},{17,20},{24,31},{25,28},{32,39},... | collective-permute-start | bytes 1572872 | tf_op jit(solution)/shard_map/ppermute | solution.py:448
  39.2 9.6 %slice-start.1 = ((s8[10485760]{0:T(1024)(128)(4,1)}), s8[4194304]{0:T(1024)(128)(4,1)S(1)}, s32[]{:S(2)}) async-start(s8[10485760]{0:T(1024)(128)(4,1)} %bitcast.16), calls=%async_computation.1 | async-start | bytes 8388608
  39.2 9.6 %slice-start.2 = ((s8[10485760]{0:T(1024)(128)(4,1)}), s8[4194304]{0:T(1024)(128)(4,1)S(1)}, s32[]{:S(2)}) async-start(s8[10485760]{0:T(1024)(128)(4,1)} %bitcast.16), calls=%async_computation.2 | async-start | bytes 8388608
  39.2 9.6 %copy-start.7 = (bf16[2048,128]{1,0:T(8,128)(2,1)S(1)}, bf16[2048,128]{1,0:T(8,128)(2,1)}, u32[]{:S(2)}) copy-start(bf16[2048,128]{1,0:T(8,128)(2,1)} %copy-done.6) | copy-start | bytes 1572868
  44.2 13.2 %copy-start.9 = (bf16[2048,128]{1,0:T(8,128)(2,1)S(1)}, bf16[2048,128]{1,0:T(8,128)(2,1)}, u32[]{:S(2)}) copy-start(bf16[2048,128]{1,0:T(8,128)(2,1)} %copy-done.8) | copy-start | bytes 1572868
  44.2 12.5 %collective-permute-start.7 = (bf16[1024,128]{1,0:T(8,128)(2,1)S(1)}, bf16[1024,128]{1,0:T(8,128)(2,1)S(1)}, u32[]{:S(2)}, u32[]{:S(2)}) collective-permute-start(bf16[1024,128]{1,0:T(8,128)(2,1)S(1)} %collective-permute-done.6.refs_3_), channel_id=1, source_target_pairs={{0,7},{1,4},{8,15},{9,12},{16,23},{17,20},{24,31},{25,28},{32,39},... | collective-permute-start | bytes 786440 | tf_op jit(solution)/shard_map/ppermute | solution.py:448
  45.9 11.4 %collective-permute-start.9 = (bf16[1024,128]{1,0:T(8,128)(2,1)}, bf16[1024,128]{1,0:T(8,128)(2,1)S(1)}, u32[]{:S(2)}, u32[]{:S(2)}) collective-permute-start(bf16[1024,128]{1,0:T(8,128)(2,1)} %collective-permute-done.8.refs_4_), channel_id=1, source_target_pairs={{0,7},{1,4},{8,15},{9,12},{16,23},{17,20},{24,31},{25,28},{32,39},... | collective-permute-start | bytes 786440 | tf_op jit(solution)/shard_map/ppermute | solution.py:448
  56.6 21.3 %copy-start.2 = (bf16[512,256]{1,0:T(8,128)(2,1)S(1)}, bf16[512,256]{1,0:T(8,128)(2,1)}, u32[]{:S(2)}) copy-start(bf16[512,256]{1,0:T(8,128)(2,1)} %refs_5_.1) | copy-start | bytes 786436
  56.6 21.2 %copy-start.3 = (bf16[128,256]{1,0:T(8,128)(2,1)S(1)}, bf16[128,256]{1,0:T(8,128)(2,1)}, u32[]{:S(2)}) copy-start(bf16[128,256]{1,0:T(8,128)(2,1)} %refs_4_.1) | copy-start | bytes 196612
  66.4 6.5 %collective-permute-start.10 = (bf16[512,128]{1,0:T(8,128)(2,1)S(1)}, bf16[512,128]{1,0:T(8,128)(2,1)S(1)}, u32[]{:S(2)}, u32[]{:S(2)}) collective-permute-start(bf16[512,128]{1,0:T(8,128)(2,1)S(1)} %get-tuple-element.59), channel_id=1, source_target_pairs={{0,1},{1,2},{2,3},{3,0},{4,5},{5,6},{6,7},{7,4},{8,9},{9,10},{10,1... | collective-permute-start | bytes 393224 | tf_op jit(solution)/shard_map/ppermute | solution.py:463
  68.2 8.8 %collective-permute-start.11 = (bf16[512,128]{1,0:T(8,128)(2,1)S(1)}, bf16[512,128]{1,0:T(8,128)(2,1)S(1)}, u32[]{:S(2)}, u32[]{:S(2)}) collective-permute-start(bf16[512,128]{1,0:T(8,128)(2,1)S(1)} %get-tuple-element.62), channel_id=1, source_target_pairs={{0,2},{1,3},{2,0},{3,1},{4,6},{5,7},{6,4},{7,5},{8,10},{9,11},{10,... | collective-permute-start | bytes 393224 | tf_op jit(solution)/shard_map/ppermute | solution.py:463
  71.4 6.5 %collective-permute-start.12 = (bf16[512,128]{1,0:T(8,128)(2,1)S(1)}, bf16[512,128]{1,0:T(8,128)(2,1)S(1)}, u32[]{:S(2)}, u32[]{:S(2)}) collective-permute-start(bf16[512,128]{1,0:T(8,128)(2,1)S(1)} %get-tuple-element.63), channel_id=1, source_target_pairs={{0,3},{1,0},{2,1},{3,2},{4,7},{5,4},{6,5},{7,6},{8,11},{9,8},{10,9... | collective-permute-start | bytes 393224 | tf_op jit(solution)/shard_map/ppermute | solution.py:463
  78.9 11.8 %collective-permute-start.13 = (bf16[768,128]{1,0:T(8,128)(2,1)S(1)}, bf16[768,128]{1,0:T(8,128)(2,1)S(1)}, u32[]{:S(2)}, u32[]{:S(2)}) collective-permute-start(bf16[768,128]{1,0:T(8,128)(2,1)S(1)} %get-tuple-element.66.refs_0_), channel_id=1, source_target_pairs={{0,1},{1,2},{2,3},{3,0},{4,5},{5,6},{6,7},{7,4},{8,9},{9,10},{10,1... | collective-permute-start | bytes 589832 | tf_op jit(solution)/shard_map/ppermute | solution.py:463
  79.7 11.0 %collective-permute-start.14 = (bf16[768,128]{1,0:T(8,128)(2,1)S(1)}, bf16[768,128]{1,0:T(8,128)(2,1)S(1)}, u32[]{:S(2)}, u32[]{:S(2)}) collective-permute-start(bf16[768,128]{1,0:T(8,128)(2,1)S(1)} %get-tuple-element.66.refs_0_), channel_id=1, source_target_pairs={{0,2},{1,3},{2,0},{3,1},{4,6},{5,7},{6,4},{7,5},{8,10},{9,11},{10,... | collective-permute-start | bytes 589832 | tf_op jit(solution)/shard_map/ppermute | solution.py:463
  80.6 10.2 %collective-permute-start.15 = (bf16[768,128]{1,0:T(8,128)(2,1)S(1)}, bf16[768,128]{1,0:T(8,128)(2,1)S(1)}, u32[]{:S(2)}, u32[]{:S(2)}) collective-permute-start(bf16[768,128]{1,0:T(8,128)(2,1)S(1)} %get-tuple-element.66.refs_0_), channel_id=1, source_target_pairs={{0,3},{1,0},{2,1},{3,2},{4,7},{5,4},{6,5},{7,6},{8,11},{9,8},{10,9... | collective-permute-start | bytes 589832 | tf_op jit(solution)/shard_map/ppermute | solution.py:463
  90.8 10.0 %collective-permute-start.16 = (f32[256,128]{1,0:T(8,128)S(1)}, f32[256,128]{1,0:T(8,128)S(1)}, u32[]{:S(2)}, u32[]{:S(2)}) collective-permute-start(f32[256,128]{1,0:T(8,128)S(1)} %convert_add_fusion), channel_id=1, source_target_pairs={{0,32},{1,33},{8,40},{9,41},{16,48},{17,49},{24,56},{25,57},{32,0}... | collective-permute-start | bytes 393224 | tf_op jit(solution)/shard_map/ppermute | solution.py:448
  98.9 9.7 %collective-permute-start.20 = (bf16[2048,128]{1,0:T(8,128)(2,1)S(1)}, bf16[2048,128]{1,0:T(8,128)(2,1)S(1)}, u32[]{:S(2)}, u32[]{:S(2)}) collective-permute-start(bf16[2048,128]{1,0:T(8,128)(2,1)S(1)} %get-tuple-element.82), channel_id=1, source_target_pairs={{0,7},{1,4},{8,15},{9,12},{16,23},{17,20},{24,31},{25,28},{32,39},... | collective-permute-start | bytes 1572872 | tf_op jit(solution)/shard_map/ppermute | solution.py:448
  99.0 14.5 %collective-permute-start.17 = (bf16[2048,128]{1,0:T(8,128)(2,1)S(1)}, bf16[2048,128]{1,0:T(8,128)(2,1)S(1)}, u32[]{:S(2)}, u32[]{:S(2)}) collective-permute-start(bf16[2048,128]{1,0:T(8,128)(2,1)S(1)} %get-tuple-element.73), channel_id=1, source_target_pairs={{0,7},{1,4},{8,15},{9,12},{16,23},{17,20},{24,31},{25,28},{32,39},... | collective-permute-start | bytes 1572872 | tf_op jit(solution)/shard_map/ppermute | solution.py:448
  108.8 9.1 %collective-permute-start.21 = (bf16[1024,128]{1,0:T(8,128)(2,1)S(1)}, bf16[1024,128]{1,0:T(8,128)(2,1)S(1)}, u32[]{:S(2)}, u32[]{:S(2)}) collective-permute-start(bf16[1024,128]{1,0:T(8,128)(2,1)S(1)} %get-tuple-element.104), channel_id=1, source_target_pairs={{0,32},{1,33},{8,40},{9,41},{16,48},{17,49},{24,56},{25,57},{32,64... | collective-permute-start | bytes 786440 | tf_op jit(solution)/shard_map/ppermute | solution.py:448
  108.9 9.0 %collective-permute-start.22 = (bf16[1024,128]{1,0:T(8,128)(2,1)S(1)}, bf16[1024,128]{1,0:T(8,128)(2,1)S(1)}, u32[]{:S(2)}, u32[]{:S(2)}) collective-permute-start(bf16[1024,128]{1,0:T(8,128)(2,1)S(1)} %get-tuple-element.103), channel_id=1, source_target_pairs={{0,96},{1,97},{8,104},{9,105},{16,112},{17,113},{24,120},{25,121},... | collective-permute-start | bytes 786440 | tf_op jit(solution)/shard_map/ppermute | solution.py:448
  111.6 8.9 %collective-permute-start.24 = (bf16[2048,128]{1,0:T(8,128)(2,1)S(1)}, bf16[2048,128]{1,0:T(8,128)(2,1)S(1)}, u32[]{:S(2)}, u32[]{:S(2)}) collective-permute-start(bf16[2048,128]{1,0:T(8,128)(2,1)S(1)} %get-tuple-element.85), channel_id=1, source_target_pairs={{0,7},{1,4},{8,15},{9,12},{16,23},{17,20},{24,31},{25,28},{32,39},... | collective-permute-start | bytes 1572872 | tf_op jit(solution)/shard_map/ppermute | solution.py:448
  111.6 24.6 %collective-permute-start.19 = (bf16[2048,128]{1,0:T(8,128)(2,1)S(1)}, bf16[2048,128]{1,0:T(8,128)(2,1)S(1)}, u32[]{:S(2)}, u32[]{:S(2)}) collective-permute-start(bf16[2048,128]{1,0:T(8,128)(2,1)S(1)} %get-tuple-element.78), channel_id=1, source_target_pairs={{0,7},{1,4},{8,15},{9,12},{16,23},{17,20},{24,31},{25,28},{32,39},... | collective-permute-start | bytes 1572872 | tf_op jit(solution)/shard_map/ppermute | solution.py:448
  118.2 18.1 %collective-permute-start.23 = (bf16[2048,128]{1,0:T(8,128)(2,1)S(1)}, bf16[2048,128]{1,0:T(8,128)(2,1)S(1)}, u32[]{:S(2)}, u32[]{:S(2)}) collective-permute-start(bf16[2048,128]{1,0:T(8,128)(2,1)S(1)} %pad_maximum_fusion), channel_id=1, source_target_pairs={{0,32},{1,33},{8,40},{9,41},{16,48},{17,49},{24,56},{25,57},{32,64... | collective-permute-start | bytes 1572872 | tf_op jit(solution)/shard_map/ppermute | solution.py:448
  120.7 15.6 %collective-permute-start.25 = (bf16[2048,128]{1,0:T(8,128)(2,1)S(1)}, bf16[2048,128]{1,0:T(8,128)(2,1)S(1)}, u32[]{:S(2)}, u32[]{:S(2)}) collective-permute-start(bf16[2048,128]{1,0:T(8,128)(2,1)S(1)} %pad_maximum_fusion.1), channel_id=1, source_target_pairs={{0,96},{1,97},{8,104},{9,105},{16,112},{17,113},{24,120},{25,121},... | collective-permute-start | bytes 1572872 | tf_op jit(solution)/shard_map/ppermute | solution.py:448
  121.5 14.7 %collective-permute-start.18 = (f32[256,128]{1,0:T(8,128)S(1)}, f32[256,128]{1,0:T(8,128)S(1)}, u32[]{:S(2)}, u32[]{:S(2)}) collective-permute-start(f32[256,128]{1,0:T(8,128)S(1)} %add.310), channel_id=1, source_target_pairs={{0,96},{1,97},{8,104},{9,105},{16,112},{17,113},{24,120},{25,121},... | collective-permute-start | bytes 393224 | tf_op jit(solution)/shard_map/ppermute | solution.py:448
  136.3 13.1 %copy-start.5 = (s32[1,2048]{1,0:T(1,128)S(1)}, s32[1,2048]{1,0:T(1,128)}, u32[]{:S(2)}) copy-start(s32[1,2048]{1,0:T(1,128)} %order_ref.3) | copy-start | bytes 24580
  136.6 12.8 %collective-permute-start.27 = (bf16[2048,128]{1,0:T(8,128)(2,1)S(1)}, bf16[2048,128]{1,0:T(8,128)(2,1)S(1)}, u32[]{:S(2)}, u32[]{:S(2)}) collective-permute-start(bf16[2048,128]{1,0:T(8,128)(2,1)S(1)} %add_convert_fusion), channel_id=1, source_target_pairs={{0,0},{1,23},{8,8},{9,31},{16,16},{17,7},{24,24},{25,15},{32,32},{... | collective-permute-start | bytes 1572872 | tf_op jit(solution)/shard_map/ppermute | solution.py:448
  142.0 7.3 %collective-permute-start.26 = (f32[256,128]{1,0:T(8,128)S(1)}, f32[256,128]{1,0:T(8,128)S(1)}, u32[]{:S(2)}, u32[]{:S(2)}) collective-permute-start(f32[256,128]{1,0:T(8,128)S(1)} %add.311), channel_id=1, source_target_pairs={{0,8},{1,9},{8,0},{9,1},{16,24},{17,25},{24,16},{25,17},{32,40},{3... | collective-permute-start | bytes 393224 | tf_op jit(solution)/shard_map/ppermute | solution.py:448
  151.8 9.3 %collective-permute-start.28 = (f32[256,128]{1,0:T(8,128)S(1)}, f32[256,128]{1,0:T(8,128)S(1)}, u32[]{:S(2)}, u32[]{:S(2)}) collective-permute-start(f32[256,128]{1,0:T(8,128)S(1)} %add.322), channel_id=1, source_target_pairs={{0,24},{1,25},{8,16},{9,17},{16,8},{17,9},{24,0},{25,1},{32,56},{3... | collective-permute-start | bytes 393224 | tf_op jit(solution)/shard_map/ppermute | solution.py:448
  156.1 8.3 %collective-permute-start.30 = (bf16[512,128]{1,0:T(8,128)(2,1)S(1)}, bf16[512,128]{1,0:T(8,128)(2,1)S(1)}, u32[]{:S(2)}, u32[]{:S(2)}) collective-permute-start(bf16[512,128]{1,0:T(8,128)(2,1)S(1)} %get-tuple-element.92), channel_id=1, source_target_pairs={{0,1},{1,2},{2,3},{3,0},{4,5},{5,6},{6,7},{7,4},{8,9},{9,10},{10,1... | collective-permute-start | bytes 393224 | tf_op jit(solution)/shard_map/ppermute | solution.py:463
  160.7 6.2 %collective-permute-start.31 = (bf16[512,128]{1,0:T(8,128)(2,1)S(1)}, bf16[512,128]{1,0:T(8,128)(2,1)S(1)}, u32[]{:S(2)}, u32[]{:S(2)}) collective-permute-start(bf16[512,128]{1,0:T(8,128)(2,1)S(1)} %get-tuple-element.93), channel_id=1, source_target_pairs={{0,2},{1,3},{2,0},{3,1},{4,6},{5,7},{6,4},{7,5},{8,10},{9,11},{10,... | collective-permute-start | bytes 393224 | tf_op jit(solution)/shard_map/ppermute | solution.py:463
  160.7 6.7 %collective-permute-start.32 = (bf16[512,128]{1,0:T(8,128)(2,1)S(1)}, bf16[512,128]{1,0:T(8,128)(2,1)S(1)}, u32[]{:S(2)}, u32[]{:S(2)}) collective-permute-start(bf16[512,128]{1,0:T(8,128)(2,1)S(1)} %get-tuple-element.94), channel_id=1, source_target_pairs={{0,3},{1,0},{2,1},{3,2},{4,7},{5,4},{6,5},{7,6},{8,11},{9,8},{10,9... | collective-permute-start | bytes 393224 | tf_op jit(solution)/shard_map/ppermute | solution.py:463
  161.1 11.6 %collective-permute-start.29 = (f32[256,128]{1,0:T(8,128)S(1)}, f32[256,128]{1,0:T(8,128)S(1)}, u32[]{:S(2)}, u32[]{:S(2)}) collective-permute-start(f32[256,128]{1,0:T(8,128)S(1)} %add.323), channel_id=1, source_target_pairs={{0,4},{1,5},{8,12},{9,13},{16,20},{17,21},{24,28},{25,29},{32,36},... | collective-permute-start | bytes 393224 | tf_op jit(solution)/shard_map/ppermute | solution.py:448

commit v3 on v2

--- a/solution.py
+++ b/solution.py
@@ -14,12 +14,14 @@
 FORWARD_WIDTH = 8
 BACKWARD_WIDTH = 4
 FORWARD_WAVES = ((0, 1, 3, 2), (4, 5, 7, 6))
-BACKWARD_WAVES = ((4, 5, 6, 7), (0, 1, 2, 3))
+BACKWARD_WAVES = ((6, 5, 7, 4), (0, 1, 2, 3))
+BACKWARD_OUTPUTS = ((1, 2, 1), (1, 1, 1, 1))
 PAIR = 2
 PARTS = 4
 CODE = 256
 VMEM_LIMIT = 12 * 1024 * 1024
 HOLD_LIMIT = 32 * 1024 * 1024
+STREAM_LIMIT = 40 * 1024 * 1024
 
 
 def spots():
@@ -63,19 +65,6 @@
 
 def partner_pairs():
     return [(device(x, y, z, c), device(x + 2 * c - 1, y, z, 1 - c)) for x, y, z, c in spots()]
-
-
-def blk_steps():
-    near, across = (1, 0, 3, 2), (3, 2, 1, 0)
-    return [
-        [(device(x, y, z, c), device(x, ring[y], z, c)) for x, y, z, c in spots()]
-        for ring in (near, across)
-    ] + [
-        [(device(x, y, z, c), device(x, y, ring[z], c)) for x, y, z, c in spots()]
-        for ring in (near, across)
-    ] + [
-        [(device(x, y, z, c), device(near[x], y, z, c)) for x, y, z, c in spots()]
-    ]
 
 
 def ring_pairs(step):
@@ -120,22 +109,28 @@
     )(order, features)
 
 
-def hold_kernel(items, place_ref, tiles_ref, out_ref, sems):
-    per_slot = out_ref.shape[0] // len(items)
+def tile_copies(slots, tiles_ref, out_ref, sems):
+    per_slot = out_ref.shape[0] // len(slots)
     part = per_slot // PARTS
     copies = []
-    for number, item in enumerate(items):
+    for number, slot in enumerate(slots):
         for piece in range(PARTS):
-            source = place_ref[1 + item] * per_slot + piece * part
             target = number * per_slot + piece * part
             copies.append(
                 pltpu.make_async_copy(
-                    tiles_ref.at[pl.ds(source, part)],
+                    tiles_ref.at[pl.ds(slot * per_slot + piece * part, part)],
                     out_ref.at[pl.ds(target, part)],
                     sems.at[number * PARTS + piece],
                 )
             )
-            copies[-1].start()
+    return copies
+
+
+def hold_kernel(items, place_ref, tiles_ref, out_ref, sems):
+    slots = [place_ref[1 + item] for item in items]
+    copies = tile_copies(slots, tiles_ref, out_ref, sems)
+    for copy in copies:
+        copy.start()
     for copy in copies:
         copy.wait()
 
@@ -202,8 +197,16 @@
 def forward_kernel(pieces, lists, wave, capacity, list_ref, hold_ref, *refs):
     first = wave == 0
     x_refs, refs = refs[:pieces], refs[pieces:]
+    codes = lists * capacity * FORWARD_WIDTH
+    ends = codes + lists * capacity
+    copies = []
     if first:
-        total_ref, x_ref = refs
+        tiles_ref = hold_ref
+        total_ref, x_ref, hold_ref, sems = refs
+        slots = [list_ref[ends + lists + 1 + item] for item in FORWARD_WAVES[0]]
+        copies = tile_copies(slots, tiles_ref, hold_ref, sems)
+        for copy in copies:
+            copy.start()
         total_ref[...] = jnp.zeros_like(total_ref)
     else:
         before_ref, out_refs, (total_ref, x_ref) = refs[0], refs[1:-2], refs[-2:]
@@ -213,6 +216,8 @@
         x_ref[start : start + piece_ref.shape[0], :] = piece_ref[...]
         start += piece_ref.shape[0]
     x_ref[start:, :] = jnp.zeros((TILE, TILE), jnp.bfloat16)
+    for copy in copies:
+        copy.wait()
 
     def product(group):
         begin = (wave * capacity + group) * FORWARD_WIDTH
@@ -228,8 +233,6 @@
         else:
             total_ref[span, :] = (total + before_ref[span, :]).astype(jnp.bfloat16)
 
-    codes = lists * capacity * FORWARD_WIDTH
-    ends = codes + lists * capacity
     group_turns(
         list_ref[ends + wave],
         FORWARD_TURN,
@@ -252,18 +255,27 @@
     )
 
 
-def forward_product(rows, lists, wave, packed, capacity, held, xs, before, reps):
+def forward_product(rows, lists, wave, packed, capacity, tiles, xs, before, reps):
     first = wave == 0
     total_shape = (rows + TILE, TILE)
     x_rows = sum(x.shape[0] for x in xs)
     x_scratch = pltpu.VMEM((x_rows + TILE, TILE), jnp.bfloat16)
+    in_specs = [whole()] * (1 + len(xs))
     if first:
-        operands = [held, *xs]
+        operands = [tiles, *xs]
+        in_specs[0] = pl.BlockSpec(memory_space=pltpu.HBM)
         out_shape = jax.ShapeDtypeStruct(total_shape, jnp.float32)
         out_specs = whole()
-        scratch = [x_scratch]
+        count = len(FORWARD_WAVES[0])
+        held = (tiles.shape[0] // (lists * count) * count, TILE, TILE)
+        scratch = [
+            x_scratch,
+            pltpu.VMEM(held, jnp.bfloat16),
+            pltpu.SemaphoreType.DMA((count * PARTS,)),
+        ]
     else:
-        operands = [held, *xs, before]
+        operands = [tiles, *xs, before]
+        in_specs.append(whole())
         out_shape = [jax.ShapeDtypeStruct((rows // reps, TILE), jnp.bfloat16)] * reps
         out_specs = [whole()] * reps
         scratch = [pltpu.VMEM(total_shape, jnp.bfloat16), x_scratch]
@@ -273,12 +285,12 @@
         grid_spec=pltpu.PrefetchScalarGridSpec(
             num_scalar_prefetch=1,
             grid=(),
-            in_specs=[whole()] * len(operands),
+            in_specs=in_specs,
             out_specs=out_specs,
             scratch_shapes=scratch,
         ),
-        compiler_params=params(),
-        cost_estimate=estimate(held.shape[0]),
+        compiler_params=params(STREAM_LIMIT if first else VMEM_LIMIT),
+        cost_estimate=estimate(x_rows // rows * 80),
     )(packed, *operands)
 
 
@@ -325,11 +337,12 @@
     )(*parts, weight, upstream)
 
 
-def backward_kernel(count, lists, first, capacity, list_ref, hold_ref, *refs):
-    pay_refs, out_refs = refs[: -2 - count], refs[-2 - count : -2]
+def backward_kernel(sizes, rows, lists, first, capacity, list_ref, hold_ref, *refs):
+    pay_refs, out_refs = refs[: -2 - len(sizes)], refs[-2 - len(sizes) : -2]
+    count = sum(sizes)
+    spots_of = [(number, item) for number, size in enumerate(sizes) for item in range(size)]
     total_ref, back_ref = refs[-2:]
     reps = len(pay_refs)
-    rows = out_refs[0].shape[0]
     own = rows // reps
     per_slot = hold_ref.shape[0] // count
     codes = lists * capacity * BACKWARD_WIDTH
@@ -341,6 +354,11 @@
         back_ref[pl.ds(start, own), :] = pay_ref[:own, :]
     back_ref[rows:, :] = jnp.zeros((TILE, TILE), jnp.bfloat16)
     total_ref[...] = jnp.zeros_like(total_ref)
+    if out_refs[0].shape[0] > sizes[0] * rows:
+        ride = pay_refs[0][own:, :].astype(jnp.float32)
+        for pay_ref in pay_refs[1:]:
+            ride = ride + pay_ref[own:, :].astype(jnp.float32)
+        out_refs[0][sizes[0] * rows :, :] = ride.astype(jnp.bfloat16)
     for number in range(0, count, PAIR):
         listed = first + number // PAIR
 
@@ -362,21 +380,26 @@
 
         group_turns(list_ref[ends + listed], BACKWARD_TURN, target_of, store, product)
         for item in range(PAIR):
-            out_refs[number + item][...] = total_ref[item * rows : (item + 1) * rows, :]
+            target, spot = spots_of[number + item]
+            out_refs[target][spot * rows : (spot + 1) * rows, :] = total_ref[
+                item * rows : (item + 1) * rows, :
+            ]
         if number + PAIR < count:
             total_ref[...] = jnp.zeros_like(total_ref)
 
 
-def backward_product(count, rows, lists, first, packed, capacity, held, pays):
-    out_shape = jax.ShapeDtypeStruct((rows, TILE), jnp.bfloat16)
+def backward_product(sizes, rows, lists, first, packed, capacity, held, pays):
+    out_rows = [size * rows for size in sizes]
+    if first == 0:
+        out_rows[0] += pays[0].shape[0] - rows // len(pays)
     return pl.pallas_call(
-        functools.partial(backward_kernel, count, lists, first, capacity),
-        out_shape=[out_shape] * count,
+        functools.partial(backward_kernel, sizes, rows, lists, first, capacity),
+        out_shape=[jax.ShapeDtypeStruct((size, TILE), jnp.bfloat16) for size in out_rows],
         grid_spec=pltpu.PrefetchScalarGridSpec(
             num_scalar_prefetch=1,
             grid=(),
             in_specs=[whole()] * (1 + len(pays)),
-            out_specs=[whole()] * count,
+            out_specs=[whole()] * len(sizes),
             scratch_shapes=[
                 pltpu.VMEM((PAIR * rows + TILE, TILE), jnp.bfloat16),
                 pltpu.VMEM((rows + TILE, TILE), jnp.bfloat16),
@@ -401,14 +424,16 @@
         start = (place_ref[0] + shift) % reps * own
         level = lax.broadcasted_iota(jnp.int32, (own, rows), 0) + start
         pick = (jnp.broadcast_to(order, (own, rows)) == level).astype(jnp.float32)
-        out_ref[...] = jnp.dot(
+        out_ref[:own, :] = jnp.dot(
             pick.astype(jnp.bfloat16), part, preferred_element_type=jnp.float32
         ).astype(jnp.bfloat16)
+        out_ref[own:, :] = home_ref[rows:, :]
 
 
 def restore(place, order, home, reps):
     rows = order.shape[1]
-    out_shape = jax.ShapeDtypeStruct((rows // reps, TILE), jnp.bfloat16)
+    out_rows = rows // reps + home.shape[0] - rows
+    out_shape = jax.ShapeDtypeStruct((out_rows, TILE), jnp.bfloat16)
     return pl.pallas_call(
         restore_kernel,
         out_shape=[out_shape] * reps,
@@ -465,17 +490,6 @@
 
     blocked = order_rows(node_order, features)
     near = moved(blocked, fetch_pairs())
-    above, below = down(near), up(near)
-    far = swapped(near)
-    known, near = lax.optimization_barrier((place, near))
-    held = [hold(FORWARD_WAVES[0], known, tiles, per_slot)]
-    above, below, far, held[0] = lax.optimization_barrier((above, below, far, held[0]))
-    middle = [down(above[:half]), up(below[half:])]
-    known, far = lax.optimization_barrier((place, far))
-    held.append(hold(FORWARD_WAVES[1], known, tiles, per_slot))
-    arrived = {0: [near], 1: [above], 2: middle, 3: [below], 4: [far], 5: [swapped(above)]}
-    arrived[6] = [swapped(value) for value in middle]
-    arrived[7] = [swapped(below)]
     alive = jnp.arange(per_slot, dtype=jnp.int32)[None, :] < counts[:, None]
     cells = jnp.take(jnp.where(alive, row_ids * CODE + col_ids, -1), slots, axis=0)
 
@@ -486,7 +500,7 @@
     waves = len(FORWARD_WAVES)
     alive, rows_of, cols_of = split(cells, sum(FORWARD_WAVES, ()))
     offsets = jnp.arange(steps, dtype=jnp.int32)[:, None] % (steps // waves) * blocks
-    packed, capacity = tile_lists(
+    forward_list, forward_capacity = tile_lists(
         jnp.where(alive, rows_of, blocks).reshape(waves, -1),
         (cols_of + offsets).reshape(waves, -1),
         blocks,
@@ -494,18 +508,10 @@
         FORWARD_WIDTH,
         FORWARD_TURN,
     )
-    packed = jnp.concatenate([packed, own_rep])
-    total = None
-    for wave, items in enumerate(FORWARD_WAVES):
-        xs = sum([arrived[item] for item in items], [])
-        total = forward_product(
-            rows_dev, waves, wave, packed, capacity, held[wave], xs, total, reps
-        )
-    total = list(total)
-    last_cells, total[0] = lax.optimization_barrier((cells, total[0]))
-    shared = to_reps(total)
+    forward_list = jnp.concatenate([forward_list, place])
+    late_cells, near = lax.optimization_barrier((cells, near))
     lists = steps // PAIR
-    alive, rows_of, cols_of = split(last_cells, sum(BACKWARD_WAVES, ()))
+    alive, rows_of, cols_of = split(late_cells, sum(BACKWARD_WAVES, ()))
     offsets = jnp.arange(steps, dtype=jnp.int32)[:, None] % PAIR * blocks
     packed, capacity = tile_lists(
         jnp.where(alive, cols_of + offsets, PAIR * blocks).reshape(lists, -1),
@@ -516,50 +522,77 @@
         BACKWARD_TURN,
     )
     packed = jnp.concatenate([packed, own_rep])
-    shared[1], packed = lax.optimization_barrier((shared[1], packed))
+    above, below = down(near), up(near)
+    far = swapped(near)
+    above, below, far, forward_list, packed = lax.optimization_barrier(
+        (above, below, far, forward_list, packed)
+    )
+    middle = [down(above[:half]), up(below[half:])]
+    known, far = lax.optimization_barrier((place, far))
+    held = hold(FORWARD_WAVES[1], known, tiles, per_slot)
+    xs = [near, above, below, *middle]
+    total = forward_product(
+        rows_dev, waves, 0, forward_list, forward_capacity, tiles, xs, None, reps
+    )
+    xs = [far, swapped(above), swapped(below), *[swapped(value) for value in middle]]
+    total = list(
+        forward_product(
+            rows_dev, waves, 1, forward_list, forward_capacity, held, xs, total, reps
+        )
+    )
+    known, total[0] = lax.optimization_barrier((place, total[0]))
+    shared = to_reps(total)
+    holds = [hold(BACKWARD_WAVES[0], known, tiles, per_slot)]
+    shared[1], holds[0] = lax.optimization_barrier((shared[1], holds[0]))
     activations, pay = dense_layer(shared, weight, upstream)
-    late_place, pay = lax.optimization_barrier((place, pay))
+    known, pay = lax.optimization_barrier((place, pay))
     pays = to_reps([pay] * reps)
-    holds = [hold(items, late_place, tiles, per_slot) for items in BACKWARD_WAVES]
+    holds.append(hold(BACKWARD_WAVES[1], known, tiles, per_slot))
     packed, holds = lax.optimization_barrier((packed, holds))
 
     def products(wave, packed):
-        count = len(BACKWARD_WAVES[wave])
-        first = wave * count // PAIR
+        sizes = BACKWARD_OUTPUTS[wave]
+        first = wave * sum(sizes) // PAIR
         return list(
-            backward_product(count, rows_dev, lists, first, packed, capacity, holds[wave], pays)
+            backward_product(sizes, rows_dev, lists, first, packed, capacity, holds[wave], pays)
         )
 
-    grad_weight = sum(pay[-weight.size // TILE :].astype(jnp.float32) for pay in pays)
-    todo = blk_steps()
-
-    def next_after(total, value):
-        total, value = lax.optimization_barrier((total, value))
-        return total + moved(total, todo.pop(0)), value
-
-    step = moved(grad_weight, todo.pop(0))
     others = products(0, packed)
-    step, packed, others[0] = lax.optimization_barrier((step, packed, others[0]))
-    grad_weight = grad_weight + step
-    returned = {item: swapped(others[item]) for item in (2, 1, 3, 0)}
+    packed, others[2] = lax.optimization_barrier((packed, others[2]))
+    returned = swapped(others[0])
+    sides = swapped(others[1])
+    last = swapped(others[2])
     mine = products(1, packed)
-    two = added(mine[2], returned[2])
-    from_below, from_above = lax.optimization_barrier((up(two[:half]), down(two[half:])))
-    grad_weight, returned[1] = next_after(grad_weight, returned[1])
+    two = added(mine[2], returned[:rows_dev])
+    ride = added(others[0][rows_dev:], returned[rows_dev:])
+    from_below, from_above = lax.optimization_barrier(
+        (up(jnp.concatenate([two[:half], ride])), down(jnp.concatenate([two[half:], ride])))
+    )
     one = jnp.concatenate(
-        [added(mine[1][:half], returned[1][:half], from_below), added(mine[1][half:], returned[1][half:])]
+        [
+            added(mine[1][:half], sides[:half], from_below[:half]),
+            added(mine[1][half:], sides[half:rows_dev]),
+            from_below[half:],
+        ]
     )
     three = jnp.concatenate(
-        [added(mine[3][:half], returned[3][:half]), added(mine[3][half:], returned[3][half:], from_above)]
-    )
-    onward = [up(one), down(three)]
-    ended = added(mine[0], returned[0], *onward)
-    grad_weight, ended = next_after(grad_weight, ended)
+        [
+            added(mine[3][:half], sides[rows_dev : rows_dev + half]),
+            added(mine[3][half:], sides[rows_dev + half :], from_above[:half]),
+        ]
+    )
+    below_sum, above_sum = up(one), down(three)
+    ended = jnp.concatenate(
+        [
+            added(mine[0], last, below_sum[:rows_dev], above_sum),
+            added(ride, from_below[half:], from_above[half:], below_sum[rows_dev:]),
+        ]
+    )
     home = moved(ended, [(user, owner) for owner, user in fetch_pairs()])
-    grad_weight, home = next_after(grad_weight, home)
-    grad_weight = grad_weight + moved(grad_weight, todo.pop(0))
     terms = to_reps(restore(own_rep, node_order, home, reps))
-    grad_features = added(*terms)
+    own = rows_dev // reps
+    grad_features = added(*[term[:own] for term in terms])
+    grad_weight = sum(term[own:].astype(jnp.float32) for term in terms)
     stacked = grad_weight.reshape(weight.shape[1] // TILE, weight.shape[0], TILE)
     grad_weight = jnp.concatenate([stacked[half] for half in range(stacked.shape[0])], axis=1)
     return (activations, grad_weight, grad_features)

time: 174 us -> 170 us (0.977); the launches traced: 173 us -> 167 us
  Pallas kernels: 56.7 us -> 41.3 us
  waiting for transfers between devices: 44.4 us -> 57.2 us
  local copies, waits for them, and re-layouts: 9.53 us -> 4.02 us
  starting transfers between devices: 54.2 us -> 56.3 us
    ppermute x24 -> x18, waiting for transfers between devices: 36.3 us -> 47.9 us  [moved(): return lax.ppermute(value, both, listed)]
    ppermute x9, starting transfers between devices: 13.2 us -> 21.5 us  [to_reps(): received.append(lax.ppermute(values[shift], 'rep', along))]
    ppermute x24 -> x18, starting transfers between devices: 41 us -> 34.8 us  [moved(): return lax.ppermute(value, both, listed)]
    pallas_call x2, Pallas kernels: 15.9 us -> 10.2 us  [backward_product(): pl.pallas_call(functools.partial(backward_kernel, sizes, rows, lists, fir...]
    pallas_call x4 -> x3, Pallas kernels: 18.9 us -> 14 us  [hold(): pl.pallas_call(functools.partial(hold_kernel, items), out_shape=jax.Shape...]
    pallas_call x2, Pallas kernels: 16 us -> 11.3 us  [forward_product(): pl.pallas_call(functools.partial(forward_kernel, len(xs), lists, wave, ca...]
    unnamed x27 -> x11, local copies, waits for them, and re-layouts: 5.88 us -> 1.75 us
  transfers between devices with their start and end apart: 33 -> 27, of which waited for: 12 -> 17; matrix products, arithmetic and copies ran while one was open for 5% -> 4% of each run, Pallas kernels for 25% -> 16%
where the time goes in v3:
time: 170 us; the launch traced here: 167 us
  waiting for transfers between devices  57.2 us (34%)
  starting transfers between devices  56.3 us (33%)
  Pallas kernels  41.3 us (24%)
  other arithmetic  7.4 us (4%)
  local copies, waits for them, and re-layouts  4.02 us (2%)
    ppermute x18, waiting for transfers between devices, moved(): return lax.ppermute(value, both, listed)  47.9 us
    ppermute x18, starting transfers between devices, moved(): return lax.ppermute(value, both, listed)  34.8 us
    ppermute x9, starting transfers between devices, to_reps(): received.append(lax.ppermute(values[shift], 'rep', along))  21.5 us
    pallas_call x3, Pallas kernels, hold(): pl.pallas_call(functools.partial(hold_kernel, items), out_shape=jax.Shape...  14 us
    pallas_call x2, Pallas kernels, forward_product(): pl.pallas_call(functools.partial(forward_kernel, len(xs), lists, wave, ca...  11.3 us
    pallas_call x2, Pallas kernels, backward_product(): pl.pallas_call(functools.partial(backward_kernel, sizes, rows, lists, fir...  10.2 us
    ppermute x9, waiting for transfers between devices, to_reps(): received.append(lax.ppermute(values[shift], 'rep', along))  9.2 us
  transfers between devices with their start and end apart: 27, of which 17 were waited for; matrix products, arithmetic and copies ran while one was open for 4% of the time, Pallas kernels for 16%

profile of v3, /device:TPU:1, one launch (start us, length us, event | category | flops | bytes accessed | tf_op | source)
XLA Modules:
  0.0 167.2 jit_solution(9662898711739100786)
XLA Ops:
  0.6 1.0 copy-done
  1.7 0.7 copy-done.3
  2.4 2.4 %shard_map.112 = bf16[2048,128]{1,0:T(8,128)(2,1)S(1)} custom-call(s32[1,2048]{1,0:T(1,128)S(1)} %copy-done.3, bf16[2048,128]{1,0:T(8,128)(2,1)S(1)} %copy-done), custom_call_target="tpu_custom_call" | custom-call | tf_op jit(solution)/shard_map/pallas_call | solution.py:103
  4.7 5.3 %collective-permute-start = (bf16[2048,128]{1,0:T(8,128)(2,1)S(1)}, bf16[2048,128]{1,0:T(8,128)(2,1)S(1)}, u32[]{:S(2)}, u32[]{:S(2)}) collective-permute-start(bf16[2048,128]{1,0:T(8,128)(2,1)S(1)} %shard_map.112), channel_id=1, source_target_pairs={{0,0},{23,1},{8,8},{31,9},{16,16},{7,17},{24,24},{15,25},{32,32},{... | collective-permute-start | bytes 1572872 | tf_op jit(solution)/shard_map/ppermute | solution.py:473
  10.1 0.7 compare_and_fusion
  10.8 0.7 fusion.14
  11.5 0.8 bitcast_select_fusion
  12.3 0.6 gather_fusion
  14.1 0.4 convert_reduce_fusion
  14.5 0.3 select_reduce_fusion.1
  14.9 0.7 dynamic-slice_bitcast_fusion
  15.7 4.1 %collective-permute-done.refs_0_ = bf16[2048,128]{1,0:T(8,128)(2,1)S(1)} collective-permute-done((bf16[2048,128]{1,0:T(8,128)(2,1)S(1)}, bf16[2048,128]{1,0:T(8,128)(2,1)S(1)}, u32[]{:S(2)}, u32[]{:S(2)}) %collective-permute-start) | collective-permute-done | bytes 524320 | tf_op jit(solution)/shard_map/ppermute | solution.py:473
  20.0 0.1 convert_reduce_fusion.2
  20.1 0.1 select_reduce_fusion.5
  20.3 0.1 reduce_max.19
  20.7 1.4 collective-permute-start.2
  22.1 1.5 collective-permute-start.1
  23.6 0.4 convert_reduce_fusion.1
  24.0 0.3 select_reduce_fusion.3
  24.4 5.2 %collective-permute-done.3.refs_0_ = bf16[2048,128]{1,0:T(8,128)(2,1)S(1)} collective-permute-done((bf16[2048,128]{1,0:T(8,128)(2,1)S(1)}, bf16[2048,128]{1,0:T(8,128)(2,1)S(1)}, u32[]{:S(2)}, u32[]{:S(2)}) %collective-permute-start.3) | collective-permute-done | bytes 524320 | tf_op jit(solution)/shard_map/ppermute | solution.py:473
  29.6 5.1 %collective-permute-done.2.refs_2_ = bf16[2048,128]{1,0:T(8,128)(2,1)S(1)} collective-permute-done((bf16[2048,128]{1,0:T(8,128)(2,1)S(1)}, bf16[2048,128]{1,0:T(8,128)(2,1)S(1)}, u32[]{:S(2)}, u32[]{:S(2)}) %collective-permute-start.2) | collective-permute-done | bytes 524320 | tf_op jit(solution)/shard_map/ppermute | solution.py:473
  34.7 1.0 collective-permute-start.8
  35.8 1.8 %collective-permute-start.6 = (bf16[1024,128]{1,0:T(8,128)(2,1)S(1)}, bf16[1024,128]{1,0:T(8,128)(2,1)S(1)}, u32[]{:S(2)}, u32[]{:S(2)}) collective-permute-start(bf16[1024,128]{1,0:T(8,128)(2,1)S(1)} %slice.148), channel_id=1, source_target_pairs={{0,96},{1,97},{8,104},{9,105},{16,112},{17,113},{24,120},{25,121},... | collective-permute-start | bytes 786440 | tf_op jit(solution)/shard_map/ppermute | solution.py:473
  37.6 3.4 %collective-permute-start.4 = (bf16[2048,128]{1,0:T(8,128)(2,1)S(1)}, bf16[2048,128]{1,0:T(8,128)(2,1)S(1)}, u32[]{:S(2)}, u32[]{:S(2)}) collective-permute-start(bf16[2048,128]{1,0:T(8,128)(2,1)S(1)} %collective-permute-done.1.refs_1_), channel_id=1, source_target_pairs={{0,7},{1,4},{8,15},{9,12},{16,23},{17,20},{24,31},{25,28},{32,39},... | collective-permute-start | bytes 1572872 | tf_op jit(solution)/shard_map/ppermute | solution.py:473
  41.1 4.7 %shard_map.113.hold_ref = bf16[320,128,128]{2,1,0:T(8,128)(2,1)S(1)} custom-call(s32[9]{0:T(128)S(1)} %pad_add_fusion.place_ref, bf16[640,128,128]{2,1,0:T(8,128)(2,1)} %bitcast.16), custom_call_target="tpu_custom_call" | custom-call | bytes 20971520 | tf_op jit(solution)/shard_map/pallas_call | solution.py:140
  45.8 1.8 %collective-permute-start.9 = (bf16[1024,128]{1,0:T(8,128)(2,1)S(1)}, bf16[1024,128]{1,0:T(8,128)(2,1)S(1)}, u32[]{:S(2)}, u32[]{:S(2)}) collective-permute-start(bf16[1024,128]{1,0:T(8,128)(2,1)S(1)} %collective-permute-done.8.refs_4_), channel_id=1, source_target_pairs={{0,7},{1,4},{8,15},{9,12},{16,23},{17,20},{24,31},{25,28},{32,39},... | collective-permute-start | bytes 786440 | tf_op jit(solution)/shard_map/ppermute | solution.py:473
  47.7 7.6 %shard_map.114.refs_5_ = f32[2176,128]{1,0:T(8,128)S(1)} custom-call(s32[1019]{0:T(1024)S(1)} %concatenate.43.list_ref, bf16[640,128,128]{2,1,0:T(8,128)(2,1)} %bitcast.17, bf16[2048,128]{1,0:T(8,128)(2,1)S(1)} %collective-permute-done.refs_0_, bf16[2048,128]{1,0:T(8,128)(2,1)S(1)} %collective-permute-done.1.refs_1_, ...), custom_call_target="tpu_custom_call" | custom-call | flops 5368709120 | bytes 10485760 | tf_op jit(solution)/shard_map/pallas_call | solution.py:282
  55.3 1.3 collective-permute-done.9.refs_4_
  56.6 2.8 %collective-permute-done.7.refs_3_ = bf16[1024,128]{1,0:T(8,128)(2,1)S(1)} collective-permute-done((bf16[1024,128]{1,0:T(8,128)(2,1)S(1)}, bf16[1024,128]{1,0:T(8,128)(2,1)S(1)}, u32[]{:S(2)}, u32[]{:S(2)}) %collective-permute-start.7) | collective-permute-done | bytes 262176 | tf_op jit(solution)/shard_map/ppermute | solution.py:473
  59.4 3.7 %shard_map.115 = (bf16[512,128]{1,0:T(8,128)(2,1)S(1)}, bf16[512,128]{1,0:T(8,128)(2,1)S(1)}, bf16[512,128]{1,0:T(8,128)(2,1)S(1)}, bf16[512,128]{1,0:T(8,128)(2,1)S(1)}) custom-call(s32[1019]{0:T(1024)S(1)} %concatenate.43.list_ref, bf16[320,128,128]{2,1,0:T(8,128)(2,1)S(1)} %shard_map.113.hold_ref, bf16[2048,128]{1,0:T(8,128)(2,1)S(1)} %collective-permute-done.3.refs_0_, ...), custom_call_target="tpu_custom_call" | custom-call | flops 5368709120 | bytes 10485760 | tf_op jit(solution)/shard_map/pallas_call | solution.py:282
  63.2 4.8 %collective-permute-start.11 = (bf16[512,128]{1,0:T(8,128)(2,1)S(1)}, bf16[512,128]{1,0:T(8,128)(2,1)S(1)}, u32[]{:S(2)}, u32[]{:S(2)}) collective-permute-start(bf16[512,128]{1,0:T(8,128)(2,1)S(1)} %get-tuple-element.55), channel_id=1, source_target_pairs={{0,2},{1,3},{2,0},{3,1},{4,6},{5,7},{6,4},{7,5},{8,10},{9,11},{10,... | collective-permute-start | bytes 393224 | tf_op jit(solution)/shard_map/ppermute | solution.py:488
  67.9 0.7 collective-permute-start.12
  68.6 4.7 %shard_map.116.hold_ref = bf16[320,128,128]{2,1,0:T(8,128)(2,1)S(1)} custom-call(s32[9]{0:T(128)S(1)} %pad_add_fusion.place_ref, bf16[640,128,128]{2,1,0:T(8,128)(2,1)} %bitcast.18), custom_call_target="tpu_custom_call" | custom-call | bytes 20971520 | tf_op jit(solution)/shard_map/pallas_call | solution.py:140
  73.3 0.2 collective-permute-done.11.refs_2_
  73.5 0.9 collective-permute-done.12.refs_3_
  74.4 1.0 shard_map.117
  75.5 1.7 %collective-permute-start.14 = (bf16[768,128]{1,0:T(8,128)(2,1)S(1)}, bf16[768,128]{1,0:T(8,128)(2,1)S(1)}, u32[]{:S(2)}, u32[]{:S(2)}) collective-permute-start(bf16[768,128]{1,0:T(8,128)(2,1)S(1)} %get-tuple-element.64.refs_0_), channel_id=1, source_target_pairs={{0,2},{1,3},{2,0},{3,1},{4,6},{5,7},{6,4},{7,5},{8,10},{9,11},{10,... | collective-permute-start | bytes 589832 | tf_op jit(solution)/shard_map/ppermute | solution.py:488
  77.1 3.5 %collective-permute-start.13 = (bf16[768,128]{1,0:T(8,128)(2,1)S(1)}, bf16[768,128]{1,0:T(8,128)(2,1)S(1)}, u32[]{:S(2)}, u32[]{:S(2)}) collective-permute-start(bf16[768,128]{1,0:T(8,128)(2,1)S(1)} %get-tuple-element.64.refs_0_), channel_id=1, source_target_pairs={{0,1},{1,2},{2,3},{3,0},{4,5},{5,6},{6,7},{7,4},{8,9},{9,10},{10,1... | collective-permute-start | bytes 589832 | tf_op jit(solution)/shard_map/ppermute | solution.py:488
  80.6 4.7 %shard_map.118.hold_ref = bf16[320,128,128]{2,1,0:T(8,128)(2,1)S(1)} custom-call(s32[9]{0:T(128)S(1)} %pad_add_fusion.place_ref, bf16[640,128,128]{2,1,0:T(8,128)(2,1)} %bitcast.19), custom_call_target="tpu_custom_call" | custom-call | bytes 20971520 | tf_op jit(solution)/shard_map/pallas_call | solution.py:140
  85.3 0.3 collective-permute-done.13.refs_1_
  85.6 5.2 %shard_map.119 = (bf16[2304,128]{1,0:T(8,128)(2,1)S(1)}, bf16[4096,128]{1,0:T(8,128)(2,1)S(1)}, bf16[2048,128]{1,0:T(8,128)(2,1)S(1)}) custom-call(s32[1285]{0:T(1024)S(1)} %concatenate.46.list_ref, bf16[320,128,128]{2,1,0:T(8,128)(2,1)S(1)} %shard_map.116.hold_ref, bf16[768,128]{1,0:T(8,128)(2,1)S(1)} %get-tuple-element.64.refs_0_, ...), custom_call_target="tpu_custom_call" | custom-call | flops 5368709120 | bytes 10485760 | tf_op jit(solution)/shard_map/pallas_call | solution.py:395
  90.8 4.2 %collective-permute-start.18 = (bf16[2304,128]{1,0:T(8,128)(2,1)S(1)}, bf16[2304,128]{1,0:T(8,128)(2,1)S(1)}, u32[]{:S(2)}, u32[]{:S(2)}) collective-permute-start(bf16[2304,128]{1,0:T(8,128)(2,1)S(1)} %get-tuple-element.73), channel_id=1, source_target_pairs={{0,7},{1,4},{8,15},{9,12},{16,23},{17,20},{24,31},{25,28},{32,39},... | collective-permute-start | bytes 1769480 | tf_op jit(solution)/shard_map/ppermute | solution.py:473
  95.2 5.0 %shard_map.120 = (bf16[2048,128]{1,0:T(8,128)(2,1)S(1)}, bf16[2048,128]{1,0:T(8,128)(2,1)S(1)}, bf16[2048,128]{1,0:T(8,128)(2,1)S(1)}, bf16[2048,128]{1,0:T(8,128)(2,1)S(1)}) custom-call(s32[1285]{0:T(1024)S(1)} %concatenate.46.list_ref, bf16[320,128,128]{2,1,0:T(8,128)(2,1)S(1)} %shard_map.118.hold_ref, bf16[768,128]{1,0:T(8,128)(2,1)S(1)} %get-tuple-element.64.refs_0_, ...), custom_call_target="tpu_custom_call" | custom-call | flops 5368709120 | bytes 10485760 | tf_op jit(solution)/shard_map/pallas_call | solution.py:395
  100.2 2.8 %collective-permute-done.18 = bf16[2304,128]{1,0:T(8,128)(2,1)S(1)} collective-permute-done((bf16[2304,128]{1,0:T(8,128)(2,1)S(1)}, bf16[2304,128]{1,0:T(8,128)(2,1)S(1)}, u32[]{:S(2)}, u32[]{:S(2)}) %collective-permute-start.18) | collective-permute-done | bytes 589856 | tf_op jit(solution)/shard_map/ppermute | solution.py:473
  102.9 0.1 add_convert_fusion.1
  103.2 1.9 %collective-permute-start.20 = (bf16[1280,128]{1,0:T(8,128)(2,1)S(1)}, bf16[1280,128]{1,0:T(8,128)(2,1)S(1)}, u32[]{:S(2)}, u32[]{:S(2)}) collective-permute-start(bf16[1280,128]{1,0:T(8,128)(2,1)S(1)} %get-tuple-element.95), channel_id=1, source_target_pairs={{0,96},{1,97},{8,104},{9,105},{16,112},{17,113},{24,120},{25,121},... | collective-permute-start | bytes 983048 | tf_op jit(solution)/shard_map/ppermute | solution.py:473
  105.1 6.1 %collective-permute-done.20 = bf16[1280,128]{1,0:T(8,128)(2,1)S(1)} collective-permute-done((bf16[1280,128]{1,0:T(8,128)(2,1)S(1)}, bf16[1280,128]{1,0:T(8,128)(2,1)S(1)}, u32[]{:S(2)}, u32[]{:S(2)}) %collective-permute-start.20) | collective-permute-done | bytes 327712 | tf_op jit(solution)/shard_map/ppermute | solution.py:473
  111.2 2.9 %collective-permute-done.19 = bf16[1280,128]{1,0:T(8,128)(2,1)S(1)} collective-permute-done((bf16[1280,128]{1,0:T(8,128)(2,1)S(1)}, bf16[1280,128]{1,0:T(8,128)(2,1)S(1)}, u32[]{:S(2)}, u32[]{:S(2)}) %collective-permute-start.19) | collective-permute-done | bytes 327712 | tf_op jit(solution)/shard_map/ppermute | solution.py:473
  114.2 0.3 add_convert_fusion.3
  114.5 1.1 collective-permute-start.21
  115.7 1.7 %collective-permute-start.16 = (bf16[2048,128]{1,0:T(8,128)(2,1)S(1)}, bf16[2048,128]{1,0:T(8,128)(2,1)S(1)}, u32[]{:S(2)}, u32[]{:S(2)}) collective-permute-start(bf16[2048,128]{1,0:T(8,128)(2,1)S(1)} %get-tuple-element.69), channel_id=1, source_target_pairs={{0,7},{1,4},{8,15},{9,12},{16,23},{17,20},{24,31},{25,28},{32,39},... | collective-permute-start | bytes 1572872 | tf_op jit(solution)/shard_map/ppermute | solution.py:473
  117.4 2.5 %collective-permute-start.22 = (bf16[2048,128]{1,0:T(8,128)(2,1)S(1)}, bf16[2048,128]{1,0:T(8,128)(2,1)S(1)}, u32[]{:S(2)}, u32[]{:S(2)}) collective-permute-start(bf16[2048,128]{1,0:T(8,128)(2,1)S(1)} %pad_maximum_fusion.2), channel_id=1, source_target_pairs={{0,96},{1,97},{8,104},{9,105},{16,112},{17,113},{24,120},{25,121},... | collective-permute-start | bytes 1572872 | tf_op jit(solution)/shard_map/ppermute | solution.py:473
  119.9 8.5 %collective-permute-done.21 = bf16[2304,128]{1,0:T(8,128)(2,1)S(1)} collective-permute-done((bf16[2304,128]{1,0:T(8,128)(2,1)S(1)}, bf16[2304,128]{1,0:T(8,128)(2,1)S(1)}, u32[]{:S(2)}, u32[]{:S(2)}) %collective-permute-start.21) | collective-permute-done | bytes 589856 | tf_op jit(solution)/shard_map/ppermute | solution.py:473
  128.4 2.3 %collective-permute-done.22 = bf16[2048,128]{1,0:T(8,128)(2,1)S(1)} collective-permute-done((bf16[2048,128]{1,0:T(8,128)(2,1)S(1)}, bf16[2048,128]{1,0:T(8,128)(2,1)S(1)}, u32[]{:S(2)}, u32[]{:S(2)}) %collective-permute-start.22) | collective-permute-done | bytes 524320 | tf_op jit(solution)/shard_map/ppermute | solution.py:473
  130.7 0.3 add_convert_fusion
  131.0 6.8 %collective-permute-start.23 = (bf16[2304,128]{1,0:T(8,128)(2,1)S(1)}, bf16[2304,128]{1,0:T(8,128)(2,1)S(1)}, u32[]{:S(2)}, u32[]{:S(2)}) collective-permute-start(bf16[2304,128]{1,0:T(8,128)(2,1)S(1)} %pad_maximum_fusion.1), channel_id=1, source_target_pairs={{0,0},{1,23},{8,8},{9,31},{16,16},{17,7},{24,24},{25,15},{32,32},{... | collective-permute-start | bytes 1769480 | tf_op jit(solution)/shard_map/ppermute | solution.py:473
  137.8 6.9 %collective-permute-done.23.home_ref = bf16[2304,128]{1,0:T(8,128)(2,1)S(1)} collective-permute-done((bf16[2304,128]{1,0:T(8,128)(2,1)S(1)}, bf16[2304,128]{1,0:T(8,128)(2,1)S(1)}, u32[]{:S(2)}, u32[]{:S(2)}) %collective-permute-start.23) | collective-permute-done | bytes 589856 | tf_op jit(solution)/shard_map/ppermute | solution.py:473
  144.7 2.5 %shard_map.121 = (bf16[768,128]{1,0:T(8,128)(2,1)S(1)}, bf16[768,128]{1,0:T(8,128)(2,1)S(1)}, bf16[768,128]{1,0:T(8,128)(2,1)S(1)}, bf16[768,128]{1,0:T(8,128)(2,1)S(1)}) custom-call(s32[1]{0:T(128)} %bitcast.place_ref, s32[1,2048]{1,0:T(1,128)S(1)} %copy-done.4, bf16[2304,128]{1,0:T(8,128)(2,1)S(1)} %collective-permute-done.23.home_ref), custom_call_target="tpu_custom_call" | custom-call | tf_op jit(solution)/shard_map/pallas_call | solution.py:437
  147.2 10.3 %collective-permute-start.24 = (bf16[768,128]{1,0:T(8,128)(2,1)S(1)}, bf16[768,128]{1,0:T(8,128)(2,1)S(1)}, u32[]{:S(2)}, u32[]{:S(2)}) collective-permute-start(bf16[768,128]{1,0:T(8,128)(2,1)S(1)} %get-tuple-element.78), channel_id=1, source_target_pairs={{0,1},{1,2},{2,3},{3,0},{4,5},{5,6},{6,7},{7,4},{8,9},{9,10},{10,1... | collective-permute-start | bytes 589832 | tf_op jit(solution)/shard_map/ppermute | solution.py:488
  157.5 0.5 collective-permute-start.26
  157.9 3.6 %collective-permute-done.24 = bf16[768,128]{1,0:T(8,128)(2,1)S(1)} collective-permute-done((bf16[768,128]{1,0:T(8,128)(2,1)S(1)}, bf16[768,128]{1,0:T(8,128)(2,1)S(1)}, u32[]{:S(2)}, u32[]{:S(2)}) %collective-permute-start.24) | collective-permute-done | bytes 196640 | tf_op jit(solution)/shard_map/ppermute | solution.py:488
  161.6 4.2 %collective-permute-done.25 = bf16[768,128]{1,0:T(8,128)(2,1)S(1)} collective-permute-done((bf16[768,128]{1,0:T(8,128)(2,1)S(1)}, bf16[768,128]{1,0:T(8,128)(2,1)S(1)}, u32[]{:S(2)}, u32[]{:S(2)}) %collective-permute-start.25) | collective-permute-done | bytes 196640 | tf_op jit(solution)/shard_map/ppermute | solution.py:488
  165.8 0.7 pad_maximum_fusion.5
  166.5 0.7 add_convert_fusion.6
  (81 shorter events, 2.9 us)
Async XLA Ops:
  0.6 1.0 copy-start
  1.7 0.7 copy-start.3
  4.7 15.1 %collective-permute-start = (bf16[2048,128]{1,0:T(8,128)(2,1)S(1)}, bf16[2048,128]{1,0:T(8,128)(2,1)S(1)}, u32[]{:S(2)}, u32[]{:S(2)}) collective-permute-start(bf16[2048,128]{1,0:T(8,128)(2,1)S(1)} %shard_map.112), channel_id=1, source_target_pairs={{0,0},{23,1},{8,8},{31,9},{16,16},{7,17},{24,24},{15,25},{32,32},{... | collective-permute-start | bytes 1572872 | tf_op jit(solution)/shard_map/ppermute | solution.py:473
  20.6 9.0 %collective-permute-start.3 = (bf16[2048,128]{1,0:T(8,128)(2,1)S(1)}, bf16[2048,128]{1,0:T(8,128)(2,1)S(1)}, u32[]{:S(2)}, u32[]{:S(2)}) collective-permute-start(bf16[2048,128]{1,0:T(8,128)(2,1)S(1)} %collective-permute-done.refs_0_), channel_id=1, source_target_pairs={{0,7},{1,4},{8,15},{9,12},{16,23},{17,20},{24,31},{25,28},{32,39},... | collective-permute-start | bytes 1572872 | tf_op jit(solution)/shard_map/ppermute | solution.py:473
  20.7 14.0 %collective-permute-start.2 = (bf16[2048,128]{1,0:T(8,128)(2,1)S(1)}, bf16[2048,128]{1,0:T(8,128)(2,1)S(1)}, u32[]{:S(2)}, u32[]{:S(2)}) collective-permute-start(bf16[2048,128]{1,0:T(8,128)(2,1)S(1)} %collective-permute-done.refs_0_), channel_id=1, source_target_pairs={{0,32},{1,33},{8,40},{9,41},{16,48},{17,49},{24,56},{25,57},{32,64... | collective-permute-start | bytes 1572872 | tf_op jit(solution)/shard_map/ppermute | solution.py:473
  22.1 12.6 %collective-permute-start.1 = (bf16[2048,128]{1,0:T(8,128)(2,1)S(1)}, bf16[2048,128]{1,0:T(8,128)(2,1)S(1)}, u32[]{:S(2)}, u32[]{:S(2)}) collective-permute-start(bf16[2048,128]{1,0:T(8,128)(2,1)S(1)} %collective-permute-done.refs_0_), channel_id=1, source_target_pairs={{0,96},{1,97},{8,104},{9,105},{16,112},{17,113},{24,120},{25,121},... | collective-permute-start | bytes 1572872 | tf_op jit(solution)/shard_map/ppermute | solution.py:473
  34.7 11.0 %collective-permute-start.8 = (bf16[1024,128]{1,0:T(8,128)(2,1)S(1)}, bf16[1024,128]{1,0:T(8,128)(2,1)S(1)}, u32[]{:S(2)}, u32[]{:S(2)}) collective-permute-start(bf16[1024,128]{1,0:T(8,128)(2,1)S(1)} %slice.149), channel_id=1, source_target_pairs={{0,32},{1,33},{8,40},{9,41},{16,48},{17,49},{24,56},{25,57},{32,64... | collective-permute-start | bytes 786440 | tf_op jit(solution)/shard_map/ppermute | solution.py:473
  35.8 11.8 %collective-permute-start.6 = (bf16[1024,128]{1,0:T(8,128)(2,1)S(1)}, bf16[1024,128]{1,0:T(8,128)(2,1)S(1)}, u32[]{:S(2)}, u32[]{:S(2)}) collective-permute-start(bf16[1024,128]{1,0:T(8,128)(2,1)S(1)} %slice.148), channel_id=1, source_target_pairs={{0,96},{1,97},{8,104},{9,105},{16,112},{17,113},{24,120},{25,121},... | collective-permute-start | bytes 786440 | tf_op jit(solution)/shard_map/ppermute | solution.py:473
  37.6 17.7 %collective-permute-start.4 = (bf16[2048,128]{1,0:T(8,128)(2,1)S(1)}, bf16[2048,128]{1,0:T(8,128)(2,1)S(1)}, u32[]{:S(2)}, u32[]{:S(2)}) collective-permute-start(bf16[2048,128]{1,0:T(8,128)(2,1)S(1)} %collective-permute-done.1.refs_1_), channel_id=1, source_target_pairs={{0,7},{1,4},{8,15},{9,12},{16,23},{17,20},{24,31},{25,28},{32,39},... | collective-permute-start | bytes 1572872 | tf_op jit(solution)/shard_map/ppermute | solution.py:473
  41.0 14.3 %collective-permute-start.5 = (bf16[2048,128]{1,0:T(8,128)(2,1)S(1)}, bf16[2048,128]{1,0:T(8,128)(2,1)S(1)}, u32[]{:S(2)}, u32[]{:S(2)}) collective-permute-start(bf16[2048,128]{1,0:T(8,128)(2,1)S(1)} %collective-permute-done.2.refs_2_), channel_id=1, source_target_pairs={{0,7},{1,4},{8,15},{9,12},{16,23},{17,20},{24,31},{25,28},{32,39},... | collective-permute-start | bytes 1572872 | tf_op jit(solution)/shard_map/ppermute | solution.py:473
  45.8 10.8 %collective-permute-start.9 = (bf16[1024,128]{1,0:T(8,128)(2,1)S(1)}, bf16[1024,128]{1,0:T(8,128)(2,1)S(1)}, u32[]{:S(2)}, u32[]{:S(2)}) collective-permute-start(bf16[1024,128]{1,0:T(8,128)(2,1)S(1)} %collective-permute-done.8.refs_4_), channel_id=1, source_target_pairs={{0,7},{1,4},{8,15},{9,12},{16,23},{17,20},{24,31},{25,28},{32,39},... | collective-permute-start | bytes 786440 | tf_op jit(solution)/shard_map/ppermute | solution.py:473
  47.6 11.8 %collective-permute-start.7 = (bf16[1024,128]{1,0:T(8,128)(2,1)S(1)}, bf16[1024,128]{1,0:T(8,128)(2,1)S(1)}, u32[]{:S(2)}, u32[]{:S(2)}) collective-permute-start(bf16[1024,128]{1,0:T(8,128)(2,1)S(1)} %collective-permute-done.6.refs_3_), channel_id=1, source_target_pairs={{0,7},{1,4},{8,15},{9,12},{16,23},{17,20},{24,31},{25,28},{32,39},... | collective-permute-start | bytes 786440 | tf_op jit(solution)/shard_map/ppermute | solution.py:473
  63.1 10.2 %collective-permute-start.10 = (bf16[512,128]{1,0:T(8,128)(2,1)S(1)}, bf16[512,128]{1,0:T(8,128)(2,1)S(1)}, u32[]{:S(2)}, u32[]{:S(2)}) collective-permute-start(bf16[512,128]{1,0:T(8,128)(2,1)S(1)} %get-tuple-element.52), channel_id=1, source_target_pairs={{0,1},{1,2},{2,3},{3,0},{4,5},{5,6},{6,7},{7,4},{8,9},{9,10},{10,1... | collective-permute-start | bytes 393224 | tf_op jit(solution)/shard_map/ppermute | solution.py:488
  63.2 10.4 %collective-permute-start.11 = (bf16[512,128]{1,0:T(8,128)(2,1)S(1)}, bf16[512,128]{1,0:T(8,128)(2,1)S(1)}, u32[]{:S(2)}, u32[]{:S(2)}) collective-permute-start(bf16[512,128]{1,0:T(8,128)(2,1)S(1)} %get-tuple-element.55), channel_id=1, source_target_pairs={{0,2},{1,3},{2,0},{3,1},{4,6},{5,7},{6,4},{7,5},{8,10},{9,11},{10,... | collective-permute-start | bytes 393224 | tf_op jit(solution)/shard_map/ppermute | solution.py:488
  67.9 6.5 %collective-permute-start.12 = (bf16[512,128]{1,0:T(8,128)(2,1)S(1)}, bf16[512,128]{1,0:T(8,128)(2,1)S(1)}, u32[]{:S(2)}, u32[]{:S(2)}) collective-permute-start(bf16[512,128]{1,0:T(8,128)(2,1)S(1)} %get-tuple-element.56), channel_id=1, source_target_pairs={{0,3},{1,0},{2,1},{3,2},{4,7},{5,4},{6,5},{7,6},{8,11},{9,8},{10,9... | collective-permute-start | bytes 393224 | tf_op jit(solution)/shard_map/ppermute | solution.py:488
  68.6 5.8 %copy-start.1 = (bf16[512,256]{1,0:T(8,128)(2,1)S(1)}, bf16[512,256]{1,0:T(8,128)(2,1)}, u32[]{:S(2)}) copy-start(bf16[512,256]{1,0:T(8,128)(2,1)} %refs_5_.1) | copy-start | bytes 786436
  68.6 5.8 %copy-start.2 = (bf16[128,256]{1,0:T(8,128)(2,1)S(1)}, bf16[128,256]{1,0:T(8,128)(2,1)}, u32[]{:S(2)}) copy-start(bf16[128,256]{1,0:T(8,128)(2,1)} %refs_4_.1) | copy-start | bytes 196612
  75.5 9.9 %collective-permute-start.15 = (bf16[768,128]{1,0:T(8,128)(2,1)S(1)}, bf16[768,128]{1,0:T(8,128)(2,1)S(1)}, u32[]{:S(2)}, u32[]{:S(2)}) collective-permute-start(bf16[768,128]{1,0:T(8,128)(2,1)S(1)} %get-tuple-element.64.refs_0_), channel_id=1, source_target_pairs={{0,3},{1,0},{2,1},{3,2},{4,7},{5,4},{6,5},{7,6},{8,11},{9,8},{10,9... | collective-permute-start | bytes 589832 | tf_op jit(solution)/shard_map/ppermute | solution.py:488
  75.5 9.9 %collective-permute-start.14 = (bf16[768,128]{1,0:T(8,128)(2,1)S(1)}, bf16[768,128]{1,0:T(8,128)(2,1)S(1)}, u32[]{:S(2)}, u32[]{:S(2)}) collective-permute-start(bf16[768,128]{1,0:T(8,128)(2,1)S(1)} %get-tuple-element.64.refs_0_), channel_id=1, source_target_pairs={{0,2},{1,3},{2,0},{3,1},{4,6},{5,7},{6,4},{7,5},{8,10},{9,11},{10,... | collective-permute-start | bytes 589832 | tf_op jit(solution)/shard_map/ppermute | solution.py:488
  77.1 8.5 %collective-permute-start.13 = (bf16[768,128]{1,0:T(8,128)(2,1)S(1)}, bf16[768,128]{1,0:T(8,128)(2,1)S(1)}, u32[]{:S(2)}, u32[]{:S(2)}) collective-permute-start(bf16[768,128]{1,0:T(8,128)(2,1)S(1)} %get-tuple-element.64.refs_0_), channel_id=1, source_target_pairs={{0,1},{1,2},{2,3},{3,0},{4,5},{5,6},{6,7},{7,4},{8,9},{9,10},{10,1... | collective-permute-start | bytes 589832 | tf_op jit(solution)/shard_map/ppermute | solution.py:488
  90.8 12.1 %collective-permute-start.18 = (bf16[2304,128]{1,0:T(8,128)(2,1)S(1)}, bf16[2304,128]{1,0:T(8,128)(2,1)S(1)}, u32[]{:S(2)}, u32[]{:S(2)}) collective-permute-start(bf16[2304,128]{1,0:T(8,128)(2,1)S(1)} %get-tuple-element.73), channel_id=1, source_target_pairs={{0,7},{1,4},{8,15},{9,12},{16,23},{17,20},{24,31},{25,28},{32,39},... | collective-permute-start | bytes 1769480 | tf_op jit(solution)/shard_map/ppermute | solution.py:473
  95.1 19.1 %collective-permute-start.17 = (bf16[4096,128]{1,0:T(8,128)(2,1)S(1)}, bf16[4096,128]{1,0:T(8,128)(2,1)S(1)}, u32[]{:S(2)}, u32[]{:S(2)}) collective-permute-start(bf16[4096,128]{1,0:T(8,128)(2,1)S(1)} %get-tuple-element.71), channel_id=1, source_target_pairs={{0,7},{1,4},{8,15},{9,12},{16,23},{17,20},{24,31},{25,28},{32,39},... | collective-permute-start | bytes 3145736 | tf_op jit(solution)/shard_map/ppermute | solution.py:473
  103.2 8.0 %collective-permute-start.20 = (bf16[1280,128]{1,0:T(8,128)(2,1)S(1)}, bf16[1280,128]{1,0:T(8,128)(2,1)S(1)}, u32[]{:S(2)}, u32[]{:S(2)}) collective-permute-start(bf16[1280,128]{1,0:T(8,128)(2,1)S(1)} %get-tuple-element.95), channel_id=1, source_target_pairs={{0,96},{1,97},{8,104},{9,105},{16,112},{17,113},{24,120},{25,121},... | collective-permute-start | bytes 983048 | tf_op jit(solution)/shard_map/ppermute | solution.py:473
  105.1 9.0 %collective-permute-start.19 = (bf16[1280,128]{1,0:T(8,128)(2,1)S(1)}, bf16[1280,128]{1,0:T(8,128)(2,1)S(1)}, u32[]{:S(2)}, u32[]{:S(2)}) collective-permute-start(bf16[1280,128]{1,0:T(8,128)(2,1)S(1)} %get-tuple-element.96), channel_id=1, source_target_pairs={{0,32},{1,33},{8,40},{9,41},{16,48},{17,49},{24,56},{25,57},{32,64... | collective-permute-start | bytes 983048 | tf_op jit(solution)/shard_map/ppermute | solution.py:473
  114.5 13.8 %collective-permute-start.21 = (bf16[2304,128]{1,0:T(8,128)(2,1)S(1)}, bf16[2304,128]{1,0:T(8,128)(2,1)S(1)}, u32[]{:S(2)}, u32[]{:S(2)}) collective-permute-start(bf16[2304,128]{1,0:T(8,128)(2,1)S(1)} %pad_maximum_fusion), channel_id=1, source_target_pairs={{0,32},{1,33},{8,40},{9,41},{16,48},{17,49},{24,56},{25,57},{32,64... | collective-permute-start | bytes 1769480 | tf_op jit(solution)/shard_map/ppermute | solution.py:473
  115.7 12.7 %collective-permute-start.16 = (bf16[2048,128]{1,0:T(8,128)(2,1)S(1)}, bf16[2048,128]{1,0:T(8,128)(2,1)S(1)}, u32[]{:S(2)}, u32[]{:S(2)}) collective-permute-start(bf16[2048,128]{1,0:T(8,128)(2,1)S(1)} %get-tuple-element.69), channel_id=1, source_target_pairs={{0,7},{1,4},{8,15},{9,12},{16,23},{17,20},{24,31},{25,28},{32,39},... | collective-permute-start | bytes 1572872 | tf_op jit(solution)/shard_map/ppermute | solution.py:473
  117.4 13.3 %collective-permute-start.22 = (bf16[2048,128]{1,0:T(8,128)(2,1)S(1)}, bf16[2048,128]{1,0:T(8,128)(2,1)S(1)}, u32[]{:S(2)}, u32[]{:S(2)}) collective-permute-start(bf16[2048,128]{1,0:T(8,128)(2,1)S(1)} %pad_maximum_fusion.2), channel_id=1, source_target_pairs={{0,96},{1,97},{8,104},{9,105},{16,112},{17,113},{24,120},{25,121},... | collective-permute-start | bytes 1572872 | tf_op jit(solution)/shard_map/ppermute | solution.py:473
  130.7 14.0 %copy-start.4 = (s32[1,2048]{1,0:T(1,128)S(1)}, s32[1,2048]{1,0:T(1,128)}, u32[]{:S(2)}) copy-start(s32[1,2048]{1,0:T(1,128)} %order_ref.3) | copy-start | bytes 24580
  131.0 13.7 %collective-permute-start.23 = (bf16[2304,128]{1,0:T(8,128)(2,1)S(1)}, bf16[2304,128]{1,0:T(8,128)(2,1)S(1)}, u32[]{:S(2)}, u32[]{:S(2)}) collective-permute-start(bf16[2304,128]{1,0:T(8,128)(2,1)S(1)} %pad_maximum_fusion.1), channel_id=1, source_target_pairs={{0,0},{1,23},{8,8},{9,31},{16,16},{17,7},{24,24},{25,15},{32,32},{... | collective-permute-start | bytes 1769480 | tf_op jit(solution)/shard_map/ppermute | solution.py:473
  147.2 14.4 %collective-permute-start.24 = (bf16[768,128]{1,0:T(8,128)(2,1)S(1)}, bf16[768,128]{1,0:T(8,128)(2,1)S(1)}, u32[]{:S(2)}, u32[]{:S(2)}) collective-permute-start(bf16[768,128]{1,0:T(8,128)(2,1)S(1)} %get-tuple-element.78), channel_id=1, source_target_pairs={{0,1},{1,2},{2,3},{3,0},{4,5},{5,6},{6,7},{7,4},{8,9},{9,10},{10,1... | collective-permute-start | bytes 589832 | tf_op jit(solution)/shard_map/ppermute | solution.py:488
  157.5 8.3 %collective-permute-start.25 = (bf16[768,128]{1,0:T(8,128)(2,1)S(1)}, bf16[768,128]{1,0:T(8,128)(2,1)S(1)}, u32[]{:S(2)}, u32[]{:S(2)}) collective-permute-start(bf16[768,128]{1,0:T(8,128)(2,1)S(1)} %get-tuple-element.79), channel_id=1, source_target_pairs={{0,2},{1,3},{2,0},{3,1},{4,6},{5,7},{6,4},{7,5},{8,10},{9,11},{10,... | collective-permute-start | bytes 589832 | tf_op jit(solution)/shard_map/ppermute | solution.py:488
  157.5 8.3 %collective-permute-start.26 = (bf16[768,128]{1,0:T(8,128)(2,1)S(1)}, bf16[768,128]{1,0:T(8,128)(2,1)S(1)}, u32[]{:S(2)}, u32[]{:S(2)}) collective-permute-start(bf16[768,128]{1,0:T(8,128)(2,1)S(1)} %get-tuple-element.80), channel_id=1, source_target_pairs={{0,3},{1,0},{2,1},{3,2},{4,7},{5,4},{6,5},{7,6},{8,11},{9,8},{10,9... | collective-permute-start | bytes 589832 | tf_op jit(solution)/shard_map/ppermute | solution.py:488

commit v4 on v3

--- a/solution.py
+++ b/solution.py
@@ -61,6 +61,26 @@
         near = levels(x, y, z, c)[1]
         listed.append((device(x - c, y, near, c), device(x, y, z, c)))
     return listed
+
+
+def fetched_rep(x, y, z, c):
+    return coords((x - c) % 4, y, z, c)[1]
+
+
+def quarter_pairs(shift):
+    listed = []
+    for x, y, z, c in spots():
+        near = levels(x, y, z, c)[1]
+        blk = device(x - c, y, near, c) // 4
+        listed.append((device(x, y, z, c), 4 * blk + (fetched_rep(x, y, z, c) + shift) % 4))
+    return listed
+
+
+def rep_table():
+    table = np.zeros((128, 1), np.int32)
+    for spot in spots():
+        table[device(*spot), 0] = fetched_rep(*spot)
+    return table
 
 
 def partner_pairs():
@@ -467,6 +487,7 @@
     here = lax.axis_index("blk") * reps + lax.axis_index("rep")
     slots = lax.dynamic_index_in_dim(jnp.asarray(slot_table()), here, 0, keepdims=False)
     place = jnp.concatenate([own_rep, slots])
+    home_rep = lax.dynamic_index_in_dim(jnp.asarray(rep_table()), here, 0, keepdims=False)
     half = rows_dev // 2
 
     def moved(value, listed):
@@ -490,6 +511,7 @@
 
     blocked = order_rows(node_order, features)
     near = moved(blocked, fetch_pairs())
+    near_order = moved(node_order, fetch_pairs())
     alive = jnp.arange(per_slot, dtype=jnp.int32)[None, :] < counts[:, None]
     cells = jnp.take(jnp.where(alive, row_ids * CODE + col_ids, -1), slots, axis=0)
 
@@ -523,9 +545,10 @@
     )
     packed = jnp.concatenate([packed, own_rep])
     above, below = down(near), up(near)
-    far = swapped(near)
-    above, below, far, forward_list, packed = lax.optimization_barrier(
-        (above, below, far, forward_list, packed)
+    ready, packed = lax.optimization_barrier((near, packed))
+    far = swapped(ready)
+    above, below, far, forward_list, packed, near_order = lax.optimization_barrier(
+        (above, below, far, forward_list, packed, near_order)
     )
     middle = [down(above[:half]), up(below[half:])]
     known, far = lax.optimization_barrier((place, far))
@@ -588,8 +611,8 @@
             added(ride, from_below[half:], from_above[half:], below_sum[rows_dev:]),
         ]
     )
-    home = moved(ended, [(user, owner) for owner, user in fetch_pairs()])
-    terms = to_reps(restore(own_rep, node_order, home, reps))
+    quarters = restore(home_rep, near_order, ended, reps)
+    terms = [moved(value, quarter_pairs(shift)) for shift, value in enumerate(quarters)]
     own = rows_dev // reps
     grad_features = added(*[term[:own] for term in terms])
     grad_weight = sum(term[own:].astype(jnp.float32) for term in terms)

time: 170 us -> 159 us (0.935)
  waiting for transfers between devices: 57.2 us -> 46.1 us
    ppermute x9 -> x6, starting transfers between devices: 21.5 us -> 13.5 us  [to_reps(): received.append(lax.ppermute(values[shift], 'rep', along))]
    ppermute x9 -> x6, waiting for transfers between devices: 9.2 us -> 1.57 us  [to_reps(): received.append(lax.ppermute(values[shift], 'rep', along))]
    ppermute x18 -> x22, starting transfers between devices: 34.8 us -> 42.4 us  [moved(): return lax.ppermute(value, both, listed)]
    ppermute x18 -> x22, waiting for transfers between devices: 47.9 us -> 44.6 us  [moved(): return lax.ppermute(value, both, listed)]
  transfers between devices with their start and end apart: 27 -> 28, of which waited for: 17 -> 14; matrix products, arithmetic and copies ran while one was open for 4% -> 6% of each run, Pallas kernels for 16% -> 18%
where the time goes in v4:
time: 159 us; the launch traced here: 157 us
  starting transfers between devices  55.8 us (35%)
  waiting for transfers between devices  46.1 us (29%)
  Pallas kernels  41.5 us (26%)
  other arithmetic  7.41 us (5%)
  local copies, waits for them, and re-layouts  5.23 us (3%)
    ppermute x22, waiting for transfers between devices, moved(): return lax.ppermute(value, both, listed)  44.6 us
    ppermute x22, starting transfers between devices, moved(): return lax.ppermute(value, both, listed)  42.4 us
    pallas_call x3, Pallas kernels, hold(): pl.pallas_call(functools.partial(hold_kernel, items), out_shape=jax.Shape...  14 us
    ppermute x6, starting transfers between devices, to_reps(): received.append(lax.ppermute(values[shift], 'rep', along))  13.5 us
    pallas_call x2, Pallas kernels, forward_product(): pl.pallas_call(functools.partial(forward_kernel, len(xs), lists, wave, ca...  10.8 us
    pallas_call x2, Pallas kernels, backward_product(): pl.pallas_call(functools.partial(backward_kernel, sizes, rows, lists, fir...  10.2 us
  transfers between devices with their start and end apart: 28, of which 14 were waited for; matrix products, arithmetic and copies ran while one was open for 6% of the time, Pallas kernels for 18%

profile of v4, /device:TPU:1, one launch (start us, length us, event | category | flops | bytes accessed | tf_op | source)
XLA Modules:
  0.0 157.2 jit_solution(2587903036733875529)
XLA Ops:
  0.6 5.3 %collective-permute-start.4 = (s32[1,2048]{1,0:T(1,128)}, s32[1,2048]{1,0:T(1,128)S(1)}, u32[]{:S(2)}, u32[]{:S(2)}) collective-permute-start(s32[1,2048]{1,0:T(1,128)} %order_ref.1), channel_id=1, source_target_pairs={{0,0},{23,1},{8,8},{31,9},{16,16},{7,17},{24,24},{15,25},{32,32},{... | collective-permute-start | bytes 24584 | tf_op jit(solution)/shard_map/ppermute | solution.py:494
  5.9 1.0 copy-done
  7.0 0.7 copy-done.3
  7.7 2.4 %shard_map.121 = bf16[2048,128]{1,0:T(8,128)(2,1)S(1)} custom-call(s32[1,2048]{1,0:T(1,128)S(1)} %copy-done.3, bf16[2048,128]{1,0:T(8,128)(2,1)S(1)} %copy-done), custom_call_target="tpu_custom_call" | custom-call | tf_op jit(solution)/shard_map/pallas_call | solution.py:123
  10.1 4.5 %collective-permute-start = (bf16[2048,128]{1,0:T(8,128)(2,1)S(1)}, bf16[2048,128]{1,0:T(8,128)(2,1)S(1)}, u32[]{:S(2)}, u32[]{:S(2)}) collective-permute-start(bf16[2048,128]{1,0:T(8,128)(2,1)S(1)} %shard_map.121), channel_id=1, source_target_pairs={{0,0},{23,1},{8,8},{31,9},{16,16},{7,17},{24,24},{15,25},{32,32},{... | collective-permute-start | bytes 1572872 | tf_op jit(solution)/shard_map/ppermute | solution.py:494
  14.5 0.7 compare_and_fusion
  15.2 0.7 fusion.14
  16.0 0.8 bitcast_select_fusion
  16.8 0.6 gather_fusion
  18.3 0.4 convert_reduce_fusion
  18.7 4.9 %collective-permute-done.refs_0_ = bf16[2048,128]{1,0:T(8,128)(2,1)S(1)} collective-permute-done((bf16[2048,128]{1,0:T(8,128)(2,1)S(1)}, bf16[2048,128]{1,0:T(8,128)(2,1)S(1)}, u32[]{:S(2)}, u32[]{:S(2)}) %collective-permute-start) | collective-permute-done | bytes 524320 | tf_op jit(solution)/shard_map/ppermute | solution.py:494
  23.6 1.3 collective-permute-start.2
  24.9 1.5 collective-permute-start.1
  26.5 0.1 convert_reduce_fusion.2
  26.7 0.4 convert_reduce_fusion.1
  27.2 0.1 select_reduce_fusion.5
  27.6 0.3 select_reduce_fusion.3
  28.1 0.3 select_reduce_fusion.1
  28.5 0.7 fusion.15
  29.5 7.4 %collective-permute-done.3.refs_0_ = bf16[2048,128]{1,0:T(8,128)(2,1)S(1)} collective-permute-done((bf16[2048,128]{1,0:T(8,128)(2,1)S(1)}, bf16[2048,128]{1,0:T(8,128)(2,1)S(1)}, u32[]{:S(2)}, u32[]{:S(2)}) %collective-permute-start.3) | collective-permute-done | bytes 524320 | tf_op jit(solution)/shard_map/ppermute | solution.py:494
  37.1 2.7 %collective-permute-start.7 = (bf16[1024,128]{1,0:T(8,128)(2,1)S(1)}, bf16[1024,128]{1,0:T(8,128)(2,1)S(1)}, u32[]{:S(2)}, u32[]{:S(2)}) collective-permute-start(bf16[1024,128]{1,0:T(8,128)(2,1)S(1)} %slice.148), channel_id=1, source_target_pairs={{0,96},{1,97},{8,104},{9,105},{16,112},{17,113},{24,120},{25,121},... | collective-permute-start | bytes 786440 | tf_op jit(solution)/shard_map/ppermute | solution.py:494
  39.8 0.3 collective-permute-start.5
  40.1 1.5 collective-permute-start.6
  41.6 4.7 %shard_map.122.hold_ref = bf16[320,128,128]{2,1,0:T(8,128)(2,1)S(1)} custom-call(s32[9]{0:T(128)S(1)} %pad_add_fusion.place_ref, bf16[640,128,128]{2,1,0:T(8,128)(2,1)} %bitcast.17), custom_call_target="tpu_custom_call" | custom-call | bytes 20971520 | tf_op jit(solution)/shard_map/pallas_call | solution.py:160
  46.3 0.7 collective-permute-start.10
  47.0 1.1 collective-permute-start.8
  48.1 7.6 %shard_map.123.refs_5_ = f32[2176,128]{1,0:T(8,128)S(1)} custom-call(s32[1019]{0:T(1024)S(1)} %concatenate.46.list_ref, bf16[640,128,128]{2,1,0:T(8,128)(2,1)} %bitcast.18, bf16[2048,128]{1,0:T(8,128)(2,1)S(1)} %collective-permute-done.refs_0_, bf16[2048,128]{1,0:T(8,128)(2,1)S(1)} %collective-permute-done.1.refs_1_, ...), custom_call_target="tpu_custom_call" | custom-call | flops 5368709120 | bytes 10485760 | tf_op jit(solution)/shard_map/pallas_call | solution.py:302
  55.7 1.4 collective-permute-done.10.refs_4_
  57.1 2.8 %collective-permute-done.8.refs_3_ = bf16[1024,128]{1,0:T(8,128)(2,1)S(1)} collective-permute-done((bf16[1024,128]{1,0:T(8,128)(2,1)S(1)}, bf16[1024,128]{1,0:T(8,128)(2,1)S(1)}, u32[]{:S(2)}, u32[]{:S(2)}) %collective-permute-start.8) | collective-permute-done | bytes 262176 | tf_op jit(solution)/shard_map/ppermute | solution.py:494
  59.9 3.2 %shard_map.124 = (bf16[512,128]{1,0:T(8,128)(2,1)S(1)}, bf16[512,128]{1,0:T(8,128)(2,1)S(1)}, bf16[512,128]{1,0:T(8,128)(2,1)S(1)}, bf16[512,128]{1,0:T(8,128)(2,1)S(1)}) custom-call(s32[1019]{0:T(1024)S(1)} %concatenate.46.list_ref, bf16[320,128,128]{2,1,0:T(8,128)(2,1)S(1)} %shard_map.122.hold_ref, bf16[2048,128]{1,0:T(8,128)(2,1)S(1)} %collective-permute-done.3.refs_0_, ...), custom_call_target="tpu_custom_call" | custom-call | flops 5368709120 | bytes 10485760 | tf_op jit(solution)/shard_map/pallas_call | solution.py:302
  63.1 6.4 %collective-permute-start.11 = (bf16[512,128]{1,0:T(8,128)(2,1)S(1)}, bf16[512,128]{1,0:T(8,128)(2,1)S(1)}, u32[]{:S(2)}, u32[]{:S(2)}) collective-permute-start(bf16[512,128]{1,0:T(8,128)(2,1)S(1)} %get-tuple-element.57), channel_id=1, source_target_pairs={{0,1},{1,2},{2,3},{3,0},{4,5},{5,6},{6,7},{7,4},{8,9},{9,10},{10,1... | collective-permute-start | bytes 393224 | tf_op jit(solution)/shard_map/ppermute | solution.py:509
  69.6 0.7 collective-permute-start.13
  70.3 4.7 %shard_map.125.hold_ref = bf16[320,128,128]{2,1,0:T(8,128)(2,1)S(1)} custom-call(s32[9]{0:T(128)S(1)} %pad_add_fusion.place_ref, bf16[640,128,128]{2,1,0:T(8,128)(2,1)} %bitcast.19), custom_call_target="tpu_custom_call" | custom-call | bytes 20971520 | tf_op jit(solution)/shard_map/pallas_call | solution.py:160
  75.0 0.7 collective-permute-done.12.refs_2_
  75.7 0.6 collective-permute-done.13.refs_3_
  76.3 1.0 shard_map.126
  77.3 1.4 collective-permute-start.16
  78.7 1.5 collective-permute-start.15
  80.2 3.5 %collective-permute-start.14 = (bf16[768,128]{1,0:T(8,128)(2,1)S(1)}, bf16[768,128]{1,0:T(8,128)(2,1)S(1)}, u32[]{:S(2)}, u32[]{:S(2)}) collective-permute-start(bf16[768,128]{1,0:T(8,128)(2,1)S(1)} %get-tuple-element.70.refs_0_), channel_id=1, source_target_pairs={{0,1},{1,2},{2,3},{3,0},{4,5},{5,6},{6,7},{7,4},{8,9},{9,10},{10,1... | collective-permute-start | bytes 589832 | tf_op jit(solution)/shard_map/ppermute | solution.py:509
  83.6 4.7 %shard_map.127.hold_ref = bf16[320,128,128]{2,1,0:T(8,128)(2,1)S(1)} custom-call(s32[9]{0:T(128)S(1)} %pad_add_fusion.place_ref, bf16[640,128,128]{2,1,0:T(8,128)(2,1)} %bitcast.20), custom_call_target="tpu_custom_call" | custom-call | bytes 20971520 | tf_op jit(solution)/shard_map/pallas_call | solution.py:160
  88.3 0.3 collective-permute-done.14.refs_1_
  88.6 5.2 %shard_map.128 = (bf16[2304,128]{1,0:T(8,128)(2,1)S(1)}, bf16[4096,128]{1,0:T(8,128)(2,1)S(1)}, bf16[2048,128]{1,0:T(8,128)(2,1)S(1)}) custom-call(s32[1285]{0:T(1024)S(1)} %concatenate.43.list_ref, bf16[320,128,128]{2,1,0:T(8,128)(2,1)S(1)} %shard_map.125.hold_ref, bf16[768,128]{1,0:T(8,128)(2,1)S(1)} %get-tuple-element.70.refs_0_, ...), custom_call_target="tpu_custom_call" | custom-call | flops 5368709120 | bytes 10485760 | tf_op jit(solution)/shard_map/pallas_call | solution.py:415
  93.8 4.2 %collective-permute-start.19 = (bf16[2304,128]{1,0:T(8,128)(2,1)S(1)}, bf16[2304,128]{1,0:T(8,128)(2,1)S(1)}, u32[]{:S(2)}, u32[]{:S(2)}) collective-permute-start(bf16[2304,128]{1,0:T(8,128)(2,1)S(1)} %get-tuple-element.79), channel_id=1, source_target_pairs={{0,7},{1,4},{8,15},{9,12},{16,23},{17,20},{24,31},{25,28},{32,39},... | collective-permute-start | bytes 1769480 | tf_op jit(solution)/shard_map/ppermute | solution.py:494
  98.1 5.0 %shard_map.129 = (bf16[2048,128]{1,0:T(8,128)(2,1)S(1)}, bf16[2048,128]{1,0:T(8,128)(2,1)S(1)}, bf16[2048,128]{1,0:T(8,128)(2,1)S(1)}, bf16[2048,128]{1,0:T(8,128)(2,1)S(1)}) custom-call(s32[1285]{0:T(1024)S(1)} %concatenate.43.list_ref, bf16[320,128,128]{2,1,0:T(8,128)(2,1)S(1)} %shard_map.127.hold_ref, bf16[768,128]{1,0:T(8,128)(2,1)S(1)} %get-tuple-element.70.refs_0_, ...), custom_call_target="tpu_custom_call" | custom-call | flops 5368709120 | bytes 10485760 | tf_op jit(solution)/shard_map/pallas_call | solution.py:415
  103.1 2.8 %collective-permute-done.19 = bf16[2304,128]{1,0:T(8,128)(2,1)S(1)} collective-permute-done((bf16[2304,128]{1,0:T(8,128)(2,1)S(1)}, bf16[2304,128]{1,0:T(8,128)(2,1)S(1)}, u32[]{:S(2)}, u32[]{:S(2)}) %collective-permute-start.19) | collective-permute-done | bytes 589856 | tf_op jit(solution)/shard_map/ppermute | solution.py:494
  105.9 0.1 add_convert_fusion.1
  106.2 1.5 collective-permute-start.20
  107.7 6.3 %collective-permute-done.21 = bf16[1280,128]{1,0:T(8,128)(2,1)S(1)} collective-permute-done((bf16[1280,128]{1,0:T(8,128)(2,1)S(1)}, bf16[1280,128]{1,0:T(8,128)(2,1)S(1)}, u32[]{:S(2)}, u32[]{:S(2)}) %collective-permute-start.21) | collective-permute-done | bytes 327712 | tf_op jit(solution)/shard_map/ppermute | solution.py:494
  114.0 0.6 collective-permute-done.20
  114.6 2.5 %collective-permute-done.18 = bf16[4096,128]{1,0:T(8,128)(2,1)S(1)} collective-permute-done((bf16[4096,128]{1,0:T(8,128)(2,1)S(1)}, bf16[4096,128]{1,0:T(8,128)(2,1)S(1)}, u32[]{:S(2)}, u32[]{:S(2)}) %collective-permute-start.18) | collective-permute-done | bytes 1048608 | tf_op jit(solution)/shard_map/ppermute | solution.py:494
  117.1 0.3 add_convert_fusion.3
  117.6 1.5 collective-permute-start.17
  119.2 2.9 %collective-permute-start.23 = (bf16[2048,128]{1,0:T(8,128)(2,1)S(1)}, bf16[2048,128]{1,0:T(8,128)(2,1)S(1)}, u32[]{:S(2)}, u32[]{:S(2)}) collective-permute-start(bf16[2048,128]{1,0:T(8,128)(2,1)S(1)} %pad_maximum_fusion.2), channel_id=1, source_target_pairs={{0,96},{1,97},{8,104},{9,105},{16,112},{17,113},{24,120},{25,121},... | collective-permute-start | bytes 1572872 | tf_op jit(solution)/shard_map/ppermute | solution.py:494
  122.1 1.2 constant_dynamic-slice_fusion
  123.3 8.9 %collective-permute-done.22 = bf16[2304,128]{1,0:T(8,128)(2,1)S(1)} collective-permute-done((bf16[2304,128]{1,0:T(8,128)(2,1)S(1)}, bf16[2304,128]{1,0:T(8,128)(2,1)S(1)}, u32[]{:S(2)}, u32[]{:S(2)}) %collective-permute-start.22) | collective-permute-done | bytes 589856 | tf_op jit(solution)/shard_map/ppermute | solution.py:494
  132.3 0.3 add_convert_fusion
  132.6 3.1 %shard_map.130 = (bf16[768,128]{1,0:T(8,128)(2,1)S(1)}, bf16[768,128]{1,0:T(8,128)(2,1)S(1)}, bf16[768,128]{1,0:T(8,128)(2,1)S(1)}, bf16[768,128]{1,0:T(8,128)(2,1)S(1)}) custom-call(s32[1]{0:T(128)} %bitcast.7.place_ref, s32[1,2048]{1,0:T(1,128)S(1)} %collective-permute-done.4.order_ref, bf16[2304,128]{1,0:T(8,128)(2,1)S(1)} %pad_maximum_fusion.1.home_ref), custom_call_target="tpu_custom_call" | custom-call | tf_op jit(solution)/shard_map/pallas_call | solution.py:457
  135.7 3.3 %collective-permute-start.24 = (bf16[768,128]{1,0:T(8,128)(2,1)S(1)}, bf16[768,128]{1,0:T(8,128)(2,1)S(1)}, u32[]{:S(2)}, u32[]{:S(2)}) collective-permute-start(bf16[768,128]{1,0:T(8,128)(2,1)S(1)} %get-tuple-element.83), channel_id=1, source_target_pairs={{0,0},{1,23},{8,8},{9,31},{16,16},{17,7},{24,24},{25,15},{32,32},{... | collective-permute-start | bytes 589832 | tf_op jit(solution)/shard_map/ppermute | solution.py:494
  139.2 5.8 %collective-permute-start.26 = (bf16[768,128]{1,0:T(8,128)(2,1)S(1)}, bf16[768,128]{1,0:T(8,128)(2,1)S(1)}, u32[]{:S(2)}, u32[]{:S(2)}) collective-permute-start(bf16[768,128]{1,0:T(8,128)(2,1)S(1)} %get-tuple-element.85), channel_id=1, source_target_pairs={{0,2},{1,21},{8,10},{9,29},{16,18},{17,5},{24,26},{25,13},{32,34},... | collective-permute-start | bytes 589832 | tf_op jit(solution)/shard_map/ppermute | solution.py:494
  144.9 3.9 %collective-permute-start.27 = (bf16[768,128]{1,0:T(8,128)(2,1)S(1)}, bf16[768,128]{1,0:T(8,128)(2,1)S(1)}, u32[]{:S(2)}, u32[]{:S(2)}) collective-permute-start(bf16[768,128]{1,0:T(8,128)(2,1)S(1)} %get-tuple-element.86), channel_id=1, source_target_pairs={{0,3},{1,22},{8,11},{9,30},{16,19},{17,6},{24,27},{25,14},{32,35},... | collective-permute-start | bytes 589832 | tf_op jit(solution)/shard_map/ppermute | solution.py:494
  148.8 1.9 %collective-permute-done.26 = bf16[768,128]{1,0:T(8,128)(2,1)S(1)} collective-permute-done((bf16[768,128]{1,0:T(8,128)(2,1)S(1)}, bf16[768,128]{1,0:T(8,128)(2,1)S(1)}, u32[]{:S(2)}, u32[]{:S(2)}) %collective-permute-start.26) | collective-permute-done | bytes 196640 | tf_op jit(solution)/shard_map/ppermute | solution.py:494
  150.7 5.0 %collective-permute-done.27 = bf16[768,128]{1,0:T(8,128)(2,1)S(1)} collective-permute-done((bf16[768,128]{1,0:T(8,128)(2,1)S(1)}, bf16[768,128]{1,0:T(8,128)(2,1)S(1)}, u32[]{:S(2)}, u32[]{:S(2)}) %collective-permute-start.27) | collective-permute-done | bytes 196640 | tf_op jit(solution)/shard_map/ppermute | solution.py:494
  155.8 0.7 pad_maximum_fusion.5
  156.4 0.7 add_convert_fusion.6
  (82 shorter events, 3.0 us)
Async XLA Ops:
  0.6 28.9 %collective-permute-start.4 = (s32[1,2048]{1,0:T(1,128)}, s32[1,2048]{1,0:T(1,128)S(1)}, u32[]{:S(2)}, u32[]{:S(2)}) collective-permute-start(s32[1,2048]{1,0:T(1,128)} %order_ref.1), channel_id=1, source_target_pairs={{0,0},{23,1},{8,8},{31,9},{16,16},{7,17},{24,24},{15,25},{32,32},{... | collective-permute-start | bytes 24584 | tf_op jit(solution)/shard_map/ppermute | solution.py:494
  5.9 1.0 copy-start
  7.0 0.7 copy-start.3
  10.1 13.5 %collective-permute-start = (bf16[2048,128]{1,0:T(8,128)(2,1)S(1)}, bf16[2048,128]{1,0:T(8,128)(2,1)S(1)}, u32[]{:S(2)}, u32[]{:S(2)}) collective-permute-start(bf16[2048,128]{1,0:T(8,128)(2,1)S(1)} %shard_map.121), channel_id=1, source_target_pairs={{0,0},{23,1},{8,8},{31,9},{16,16},{7,17},{24,24},{15,25},{32,32},{... | collective-permute-start | bytes 1572872 | tf_op jit(solution)/shard_map/ppermute | solution.py:494
  23.6 13.3 %collective-permute-start.2 = (bf16[2048,128]{1,0:T(8,128)(2,1)S(1)}, bf16[2048,128]{1,0:T(8,128)(2,1)S(1)}, u32[]{:S(2)}, u32[]{:S(2)}) collective-permute-start(bf16[2048,128]{1,0:T(8,128)(2,1)S(1)} %collective-permute-done.refs_0_), channel_id=1, source_target_pairs={{0,32},{1,33},{8,40},{9,41},{16,48},{17,49},{24,56},{25,57},{32,64... | collective-permute-start | bytes 1572872 | tf_op jit(solution)/shard_map/ppermute | solution.py:494
  24.9 12.0 %collective-permute-start.1 = (bf16[2048,128]{1,0:T(8,128)(2,1)S(1)}, bf16[2048,128]{1,0:T(8,128)(2,1)S(1)}, u32[]{:S(2)}, u32[]{:S(2)}) collective-permute-start(bf16[2048,128]{1,0:T(8,128)(2,1)S(1)} %collective-permute-done.refs_0_), channel_id=1, source_target_pairs={{0,96},{1,97},{8,104},{9,105},{16,112},{17,113},{24,120},{25,121},... | collective-permute-start | bytes 1572872 | tf_op jit(solution)/shard_map/ppermute | solution.py:494
  28.0 8.9 %collective-permute-start.3 = (bf16[2048,128]{1,0:T(8,128)(2,1)S(1)}, bf16[2048,128]{1,0:T(8,128)(2,1)S(1)}, u32[]{:S(2)}, u32[]{:S(2)}) collective-permute-start(bf16[2048,128]{1,0:T(8,128)(2,1)S(1)} %collective-permute-done.refs_0_), channel_id=1, source_target_pairs={{0,7},{1,4},{8,15},{9,12},{16,23},{17,20},{24,31},{25,28},{32,39},... | collective-permute-start | bytes 1572872 | tf_op jit(solution)/shard_map/ppermute | solution.py:494
  36.9 9.3 %collective-permute-start.9 = (bf16[1024,128]{1,0:T(8,128)(2,1)S(1)}, bf16[1024,128]{1,0:T(8,128)(2,1)S(1)}, u32[]{:S(2)}, u32[]{:S(2)}) collective-permute-start(bf16[1024,128]{1,0:T(8,128)(2,1)S(1)} %slice.149), channel_id=1, source_target_pairs={{0,32},{1,33},{8,40},{9,41},{16,48},{17,49},{24,56},{25,57},{32,64... | collective-permute-start | bytes 786440 | tf_op jit(solution)/shard_map/ppermute | solution.py:494
  37.1 10.0 %collective-permute-start.7 = (bf16[1024,128]{1,0:T(8,128)(2,1)S(1)}, bf16[1024,128]{1,0:T(8,128)(2,1)S(1)}, u32[]{:S(2)}, u32[]{:S(2)}) collective-permute-start(bf16[1024,128]{1,0:T(8,128)(2,1)S(1)} %slice.148), channel_id=1, source_target_pairs={{0,96},{1,97},{8,104},{9,105},{16,112},{17,113},{24,120},{25,121},... | collective-permute-start | bytes 786440 | tf_op jit(solution)/shard_map/ppermute | solution.py:494
  39.8 15.9 %collective-permute-start.5 = (bf16[2048,128]{1,0:T(8,128)(2,1)S(1)}, bf16[2048,128]{1,0:T(8,128)(2,1)S(1)}, u32[]{:S(2)}, u32[]{:S(2)}) collective-permute-start(bf16[2048,128]{1,0:T(8,128)(2,1)S(1)} %collective-permute-done.1.refs_1_), channel_id=1, source_target_pairs={{0,7},{1,4},{8,15},{9,12},{16,23},{17,20},{24,31},{25,28},{32,39},... | collective-permute-start | bytes 1572872 | tf_op jit(solution)/shard_map/ppermute | solution.py:494
  40.1 15.6 %collective-permute-start.6 = (bf16[2048,128]{1,0:T(8,128)(2,1)S(1)}, bf16[2048,128]{1,0:T(8,128)(2,1)S(1)}, u32[]{:S(2)}, u32[]{:S(2)}) collective-permute-start(bf16[2048,128]{1,0:T(8,128)(2,1)S(1)} %collective-permute-done.2.refs_2_), channel_id=1, source_target_pairs={{0,7},{1,4},{8,15},{9,12},{16,23},{17,20},{24,31},{25,28},{32,39},... | collective-permute-start | bytes 1572872 | tf_op jit(solution)/shard_map/ppermute | solution.py:494
  46.3 10.8 %collective-permute-start.10 = (bf16[1024,128]{1,0:T(8,128)(2,1)S(1)}, bf16[1024,128]{1,0:T(8,128)(2,1)S(1)}, u32[]{:S(2)}, u32[]{:S(2)}) collective-permute-start(bf16[1024,128]{1,0:T(8,128)(2,1)S(1)} %collective-permute-done.9.refs_4_), channel_id=1, source_target_pairs={{0,7},{1,4},{8,15},{9,12},{16,23},{17,20},{24,31},{25,28},{32,39},... | collective-permute-start | bytes 786440 | tf_op jit(solution)/shard_map/ppermute | solution.py:494
  47.0 12.9 %collective-permute-start.8 = (bf16[1024,128]{1,0:T(8,128)(2,1)S(1)}, bf16[1024,128]{1,0:T(8,128)(2,1)S(1)}, u32[]{:S(2)}, u32[]{:S(2)}) collective-permute-start(bf16[1024,128]{1,0:T(8,128)(2,1)S(1)} %collective-permute-done.7.refs_3_), channel_id=1, source_target_pairs={{0,7},{1,4},{8,15},{9,12},{16,23},{17,20},{24,31},{25,28},{32,39},... | collective-permute-start | bytes 786440 | tf_op jit(solution)/shard_map/ppermute | solution.py:494
  63.1 11.8 %collective-permute-start.11 = (bf16[512,128]{1,0:T(8,128)(2,1)S(1)}, bf16[512,128]{1,0:T(8,128)(2,1)S(1)}, u32[]{:S(2)}, u32[]{:S(2)}) collective-permute-start(bf16[512,128]{1,0:T(8,128)(2,1)S(1)} %get-tuple-element.57), channel_id=1, source_target_pairs={{0,1},{1,2},{2,3},{3,0},{4,5},{5,6},{6,7},{7,4},{8,9},{9,10},{10,1... | collective-permute-start | bytes 393224 | tf_op jit(solution)/shard_map/ppermute | solution.py:509
  69.5 6.2 %collective-permute-start.12 = (bf16[512,128]{1,0:T(8,128)(2,1)S(1)}, bf16[512,128]{1,0:T(8,128)(2,1)S(1)}, u32[]{:S(2)}, u32[]{:S(2)}) collective-permute-start(bf16[512,128]{1,0:T(8,128)(2,1)S(1)} %get-tuple-element.60), channel_id=1, source_target_pairs={{0,2},{1,3},{2,0},{3,1},{4,6},{5,7},{6,4},{7,5},{8,10},{9,11},{10,... | collective-permute-start | bytes 393224 | tf_op jit(solution)/shard_map/ppermute | solution.py:509
  69.6 6.7 %collective-permute-start.13 = (bf16[512,128]{1,0:T(8,128)(2,1)S(1)}, bf16[512,128]{1,0:T(8,128)(2,1)S(1)}, u32[]{:S(2)}, u32[]{:S(2)}) collective-permute-start(bf16[512,128]{1,0:T(8,128)(2,1)S(1)} %get-tuple-element.61), channel_id=1, source_target_pairs={{0,3},{1,0},{2,1},{3,2},{4,7},{5,4},{6,5},{7,6},{8,11},{9,8},{10,9... | collective-permute-start | bytes 393224 | tf_op jit(solution)/shard_map/ppermute | solution.py:509
  70.3 6.0 %copy-start.1 = (bf16[512,256]{1,0:T(8,128)(2,1)S(1)}, bf16[512,256]{1,0:T(8,128)(2,1)}, u32[]{:S(2)}) copy-start(bf16[512,256]{1,0:T(8,128)(2,1)} %refs_5_.1) | copy-start | bytes 786436
  70.3 6.0 %copy-start.2 = (bf16[128,256]{1,0:T(8,128)(2,1)S(1)}, bf16[128,256]{1,0:T(8,128)(2,1)}, u32[]{:S(2)}) copy-start(bf16[128,256]{1,0:T(8,128)(2,1)} %refs_4_.1) | copy-start | bytes 196612
  77.3 11.0 %collective-permute-start.16 = (bf16[768,128]{1,0:T(8,128)(2,1)S(1)}, bf16[768,128]{1,0:T(8,128)(2,1)S(1)}, u32[]{:S(2)}, u32[]{:S(2)}) collective-permute-start(bf16[768,128]{1,0:T(8,128)(2,1)S(1)} %get-tuple-element.70.refs_0_), channel_id=1, source_target_pairs={{0,3},{1,0},{2,1},{3,2},{4,7},{5,4},{6,5},{7,6},{8,11},{9,8},{10,9... | collective-permute-start | bytes 589832 | tf_op jit(solution)/shard_map/ppermute | solution.py:509
  78.7 9.7 %collective-permute-start.15 = (bf16[768,128]{1,0:T(8,128)(2,1)S(1)}, bf16[768,128]{1,0:T(8,128)(2,1)S(1)}, u32[]{:S(2)}, u32[]{:S(2)}) collective-permute-start(bf16[768,128]{1,0:T(8,128)(2,1)S(1)} %get-tuple-element.70.refs_0_), channel_id=1, source_target_pairs={{0,2},{1,3},{2,0},{3,1},{4,6},{5,7},{6,4},{7,5},{8,10},{9,11},{10,... | collective-permute-start | bytes 589832 | tf_op jit(solution)/shard_map/ppermute | solution.py:509
  80.2 8.5 %collective-permute-start.14 = (bf16[768,128]{1,0:T(8,128)(2,1)S(1)}, bf16[768,128]{1,0:T(8,128)(2,1)S(1)}, u32[]{:S(2)}, u32[]{:S(2)}) collective-permute-start(bf16[768,128]{1,0:T(8,128)(2,1)S(1)} %get-tuple-element.70.refs_0_), channel_id=1, source_target_pairs={{0,1},{1,2},{2,3},{3,0},{4,5},{5,6},{6,7},{7,4},{8,9},{9,10},{10,1... | collective-permute-start | bytes 589832 | tf_op jit(solution)/shard_map/ppermute | solution.py:509
  93.8 12.1 %collective-permute-start.19 = (bf16[2304,128]{1,0:T(8,128)(2,1)S(1)}, bf16[2304,128]{1,0:T(8,128)(2,1)S(1)}, u32[]{:S(2)}, u32[]{:S(2)}) collective-permute-start(bf16[2304,128]{1,0:T(8,128)(2,1)S(1)} %get-tuple-element.79), channel_id=1, source_target_pairs={{0,7},{1,4},{8,15},{9,12},{16,23},{17,20},{24,31},{25,28},{32,39},... | collective-permute-start | bytes 1769480 | tf_op jit(solution)/shard_map/ppermute | solution.py:494
  98.0 19.1 %collective-permute-start.18 = (bf16[4096,128]{1,0:T(8,128)(2,1)S(1)}, bf16[4096,128]{1,0:T(8,128)(2,1)S(1)}, u32[]{:S(2)}, u32[]{:S(2)}) collective-permute-start(bf16[4096,128]{1,0:T(8,128)(2,1)S(1)} %get-tuple-element.77), channel_id=1, source_target_pairs={{0,7},{1,4},{8,15},{9,12},{16,23},{17,20},{24,31},{25,28},{32,39},... | collective-permute-start | bytes 3145736 | tf_op jit(solution)/shard_map/ppermute | solution.py:494
  106.1 7.9 %collective-permute-start.21 = (bf16[1280,128]{1,0:T(8,128)(2,1)S(1)}, bf16[1280,128]{1,0:T(8,128)(2,1)S(1)}, u32[]{:S(2)}, u32[]{:S(2)}) collective-permute-start(bf16[1280,128]{1,0:T(8,128)(2,1)S(1)} %get-tuple-element.101), channel_id=1, source_target_pairs={{0,96},{1,97},{8,104},{9,105},{16,112},{17,113},{24,120},{25,121},... | collective-permute-start | bytes 983048 | tf_op jit(solution)/shard_map/ppermute | solution.py:494
  106.2 8.4 %collective-permute-start.20 = (bf16[1280,128]{1,0:T(8,128)(2,1)S(1)}, bf16[1280,128]{1,0:T(8,128)(2,1)S(1)}, u32[]{:S(2)}, u32[]{:S(2)}) collective-permute-start(bf16[1280,128]{1,0:T(8,128)(2,1)S(1)} %get-tuple-element.102), channel_id=1, source_target_pairs={{0,32},{1,33},{8,40},{9,41},{16,48},{17,49},{24,56},{25,57},{32,64... | collective-permute-start | bytes 983048 | tf_op jit(solution)/shard_map/ppermute | solution.py:494
  117.5 14.7 %collective-permute-start.22 = (bf16[2304,128]{1,0:T(8,128)(2,1)S(1)}, bf16[2304,128]{1,0:T(8,128)(2,1)S(1)}, u32[]{:S(2)}, u32[]{:S(2)}) collective-permute-start(bf16[2304,128]{1,0:T(8,128)(2,1)S(1)} %pad_maximum_fusion), channel_id=1, source_target_pairs={{0,32},{1,33},{8,40},{9,41},{16,48},{17,49},{24,56},{25,57},{32,64... | collective-permute-start | bytes 1769480 | tf_op jit(solution)/shard_map/ppermute | solution.py:494
  117.6 14.7 %collective-permute-start.17 = (bf16[2048,128]{1,0:T(8,128)(2,1)S(1)}, bf16[2048,128]{1,0:T(8,128)(2,1)S(1)}, u32[]{:S(2)}, u32[]{:S(2)}) collective-permute-start(bf16[2048,128]{1,0:T(8,128)(2,1)S(1)} %get-tuple-element.75), channel_id=1, source_target_pairs={{0,7},{1,4},{8,15},{9,12},{16,23},{17,20},{24,31},{25,28},{32,39},... | collective-permute-start | bytes 1572872 | tf_op jit(solution)/shard_map/ppermute | solution.py:494
  119.2 13.1 %collective-permute-start.23 = (bf16[2048,128]{1,0:T(8,128)(2,1)S(1)}, bf16[2048,128]{1,0:T(8,128)(2,1)S(1)}, u32[]{:S(2)}, u32[]{:S(2)}) collective-permute-start(bf16[2048,128]{1,0:T(8,128)(2,1)S(1)} %pad_maximum_fusion.2), channel_id=1, source_target_pairs={{0,96},{1,97},{8,104},{9,105},{16,112},{17,113},{24,120},{25,121},... | collective-permute-start | bytes 1572872 | tf_op jit(solution)/shard_map/ppermute | solution.py:494
  135.7 13.1 %collective-permute-start.24 = (bf16[768,128]{1,0:T(8,128)(2,1)S(1)}, bf16[768,128]{1,0:T(8,128)(2,1)S(1)}, u32[]{:S(2)}, u32[]{:S(2)}) collective-permute-start(bf16[768,128]{1,0:T(8,128)(2,1)S(1)} %get-tuple-element.83), channel_id=1, source_target_pairs={{0,0},{1,23},{8,8},{9,31},{16,16},{17,7},{24,24},{25,15},{32,32},{... | collective-permute-start | bytes 589832 | tf_op jit(solution)/shard_map/ppermute | solution.py:494
  139.1 9.7 %collective-permute-start.25 = (bf16[768,128]{1,0:T(8,128)(2,1)S(1)}, bf16[768,128]{1,0:T(8,128)(2,1)S(1)}, u32[]{:S(2)}, u32[]{:S(2)}) collective-permute-start(bf16[768,128]{1,0:T(8,128)(2,1)S(1)} %get-tuple-element.84), channel_id=1, source_target_pairs={{0,1},{1,20},{8,9},{9,28},{16,17},{17,4},{24,25},{25,12},{32,33},{... | collective-permute-start | bytes 589832 | tf_op jit(solution)/shard_map/ppermute | solution.py:494
  139.2 11.5 %collective-permute-start.26 = (bf16[768,128]{1,0:T(8,128)(2,1)S(1)}, bf16[768,128]{1,0:T(8,128)(2,1)S(1)}, u32[]{:S(2)}, u32[]{:S(2)}) collective-permute-start(bf16[768,128]{1,0:T(8,128)(2,1)S(1)} %get-tuple-element.85), channel_id=1, source_target_pairs={{0,2},{1,21},{8,10},{9,29},{16,18},{17,5},{24,26},{25,13},{32,34},... | collective-permute-start | bytes 589832 | tf_op jit(solution)/shard_map/ppermute | solution.py:494
  144.9 10.8 %collective-permute-start.27 = (bf16[768,128]{1,0:T(8,128)(2,1)S(1)}, bf16[768,128]{1,0:T(8,128)(2,1)S(1)}, u32[]{:S(2)}, u32[]{:S(2)}) collective-permute-start(bf16[768,128]{1,0:T(8,128)(2,1)S(1)} %get-tuple-element.86), channel_id=1, source_target_pairs={{0,3},{1,22},{8,11},{9,30},{16,19},{17,6},{24,27},{25,14},{32,35},... | collective-permute-start | bytes 589832 | tf_op jit(solution)/shard_map/ppermute | solution.py:494

commit v5 on v4

--- a/solution.py
+++ b/solution.py
@@ -10,9 +10,9 @@
 
 TILE = 128
 FORWARD_TURN = 4
-BACKWARD_TURN = 8
+BACKWARD_TURN = 16
 FORWARD_WIDTH = 8
-BACKWARD_WIDTH = 4
+BACKWARD_WIDTH = 2
 FORWARD_WAVES = ((0, 1, 3, 2), (4, 5, 7, 6))
 BACKWARD_WAVES = ((6, 5, 7, 4), (0, 1, 2, 3))
 BACKWARD_OUTPUTS = ((1, 2, 1), (1, 1, 1, 1))
@@ -511,7 +511,8 @@
 
     blocked = order_rows(node_order, features)
     near = moved(blocked, fetch_pairs())
-    near_order = moved(node_order, fetch_pairs())
+    later_order, blocked = lax.optimization_barrier((node_order, blocked))
+    near_order = moved(later_order, fetch_pairs())
     alive = jnp.arange(per_slot, dtype=jnp.int32)[None, :] < counts[:, None]
     cells = jnp.take(jnp.where(alive, row_ids * CODE + col_ids, -1), slots, axis=0)
 

time: 159 us -> 157 us (0.987)
  Pallas kernels: 41.5 us -> 52.3 us
  starting transfers between devices: 55.8 us -> 49.4 us
  waiting for transfers between devices: 46.1 us -> 41.7 us
    pallas_call x2, Pallas kernels: 10.8 us -> 16.9 us  [forward_product(): pl.pallas_call(functools.partial(forward_kernel, len(xs), lists, wave, ca...]
    ppermute x22, starting transfers between devices: 42.4 us -> 36.4 us  [moved(): return lax.ppermute(value, both, listed)]
    ppermute x22, waiting for transfers between devices: 44.6 us -> 40.3 us  [moved(): return lax.ppermute(value, both, listed)]
    pallas_call x2, Pallas kernels: 10.2 us -> 14.2 us  [backward_product(): pl.pallas_call(functools.partial(backward_kernel, sizes, rows, lists, fir...]
  transfers between devices with their start and end apart: 28 -> 28, of which waited for: 14 -> 14; matrix products, arithmetic and copies ran while one was open for 6% -> 6% of each run, Pallas kernels for 18% -> 20%
where the time goes in v5:
time: 157 us
  Pallas kernels  52.3 us (33%)
  starting transfers between devices  49.4 us (31%)
  waiting for transfers between devices  41.7 us (27%)
  other arithmetic  7.41 us (5%)
  local copies, waits for them, and re-layouts  4.61 us (3%)
    ppermute x22, waiting for transfers between devices, moved(): return lax.ppermute(value, both, listed)  40.3 us
    ppermute x22, starting transfers between devices, moved(): return lax.ppermute(value, both, listed)  36.4 us
    pallas_call x2, Pallas kernels, forward_product(): pl.pallas_call(functools.partial(forward_kernel, len(xs), lists, wave, ca...  16.9 us
    pallas_call x2, Pallas kernels, backward_product(): pl.pallas_call(functools.partial(backward_kernel, sizes, rows, lists, fir...  14.2 us
    pallas_call x3, Pallas kernels, hold(): pl.pallas_call(functools.partial(hold_kernel, items), out_shape=jax.Shape...  14 us
    ppermute x6, starting transfers between devices, to_reps(): received.append(lax.ppermute(values[shift], 'rep', along))  13 us
  transfers between devices with their start and end apart: 28, of which 14 were waited for; matrix products, arithmetic and copies ran while one was open for 6% of the time, Pallas kernels for 20%

profile of v5, /device:TPU:1, one launch (start us, length us, event | category | flops | bytes accessed | tf_op | source)
XLA Modules:
  0.0 156.5 jit_solution(6933211586889213971)
XLA Ops:
  0.6 1.0 copy-done
  1.7 3.1 %shard_map.121 = bf16[2048,128]{1,0:T(8,128)(2,1)S(1)} custom-call(s32[1,2048]{1,0:T(1,128)} %order_ref.1, bf16[2048,128]{1,0:T(8,128)(2,1)S(1)} %copy-done), custom_call_target="tpu_custom_call" | custom-call | tf_op jit(solution)/shard_map/pallas_call | solution.py:123
  4.8 5.3 %collective-permute-start = (bf16[2048,128]{1,0:T(8,128)(2,1)S(1)}, bf16[2048,128]{1,0:T(8,128)(2,1)S(1)}, u32[]{:S(2)}, u32[]{:S(2)}) collective-permute-start(bf16[2048,128]{1,0:T(8,128)(2,1)S(1)} %shard_map.121), channel_id=1, source_target_pairs={{0,0},{23,1},{8,8},{31,9},{16,16},{7,17},{24,24},{15,25},{32,32},{... | collective-permute-start | bytes 1572872 | tf_op jit(solution)/shard_map/ppermute | solution.py:494
  10.1 4.5 %collective-permute-start.4 = (s32[1,2048]{1,0:T(1,128)}, s32[1,2048]{1,0:T(1,128)S(1)}, u32[]{:S(2)}, u32[]{:S(2)}) collective-permute-start(s32[1,2048]{1,0:T(1,128)} %order_ref.1), channel_id=1, source_target_pairs={{0,0},{23,1},{8,8},{31,9},{16,16},{7,17},{24,24},{15,25},{32,32},{... | collective-permute-start | bytes 24584 | tf_op jit(solution)/shard_map/ppermute | solution.py:494
  14.5 0.7 compare_and_fusion
  15.2 0.7 fusion.14
  16.0 0.8 bitcast_select_fusion
  16.8 0.6 gather_fusion
  17.7 0.1 convert_reduce_fusion.4
  18.3 0.4 convert_reduce_fusion
  18.7 1.2 collective-permute-done.refs_0_
  19.9 1.3 collective-permute-start.2
  21.1 1.5 collective-permute-start.1
  22.8 0.1 convert_reduce_fusion.2
  22.9 0.4 convert_reduce_fusion.1
  23.4 0.1 select_reduce_fusion.5
  23.9 0.3 select_reduce_fusion.3
  24.4 0.3 select_reduce_fusion.1
  24.8 0.7 fusion.15
  25.8 7.4 %collective-permute-done.3.refs_0_ = bf16[2048,128]{1,0:T(8,128)(2,1)S(1)} collective-permute-done((bf16[2048,128]{1,0:T(8,128)(2,1)S(1)}, bf16[2048,128]{1,0:T(8,128)(2,1)S(1)}, u32[]{:S(2)}, u32[]{:S(2)}) %collective-permute-start.3) | collective-permute-done | bytes 524320 | tf_op jit(solution)/shard_map/ppermute | solution.py:494
  33.4 2.7 %collective-permute-start.7 = (bf16[1024,128]{1,0:T(8,128)(2,1)S(1)}, bf16[1024,128]{1,0:T(8,128)(2,1)S(1)}, u32[]{:S(2)}, u32[]{:S(2)}) collective-permute-start(bf16[1024,128]{1,0:T(8,128)(2,1)S(1)} %slice.148), channel_id=1, source_target_pairs={{0,96},{1,97},{8,104},{9,105},{16,112},{17,113},{24,120},{25,121},... | collective-permute-start | bytes 786440 | tf_op jit(solution)/shard_map/ppermute | solution.py:494
  36.1 0.3 collective-permute-start.5
  36.4 1.5 collective-permute-start.6
  37.9 4.7 %shard_map.122.hold_ref = bf16[320,128,128]{2,1,0:T(8,128)(2,1)S(1)} custom-call(s32[9]{0:T(128)S(1)} %pad_add_fusion.place_ref, bf16[640,128,128]{2,1,0:T(8,128)(2,1)} %bitcast.14), custom_call_target="tpu_custom_call" | custom-call | bytes 20971520 | tf_op jit(solution)/shard_map/pallas_call | solution.py:160
  42.6 0.5 collective-permute-start.10
  43.1 1.3 collective-permute-start.8
  44.4 10.4 %shard_map.123.refs_5_ = f32[2176,128]{1,0:T(8,128)S(1)} custom-call(s32[1019]{0:T(1024)S(1)} %concatenate.46.list_ref, bf16[640,128,128]{2,1,0:T(8,128)(2,1)} %bitcast.15, bf16[2048,128]{1,0:T(8,128)(2,1)S(1)} %collective-permute-done.refs_0_, bf16[2048,128]{1,0:T(8,128)(2,1)S(1)} %collective-permute-done.1.refs_1_, ...), custom_call_target="tpu_custom_call" | custom-call | flops 5368709120 | bytes 10485760 | tf_op jit(solution)/shard_map/pallas_call | solution.py:302
  54.9 1.4 collective-permute-done.8.refs_3_
  56.2 6.6 %shard_map.124 = (bf16[512,128]{1,0:T(8,128)(2,1)S(1)}, bf16[512,128]{1,0:T(8,128)(2,1)S(1)}, bf16[512,128]{1,0:T(8,128)(2,1)S(1)}, bf16[512,128]{1,0:T(8,128)(2,1)S(1)}) custom-call(s32[1019]{0:T(1024)S(1)} %concatenate.46.list_ref, bf16[320,128,128]{2,1,0:T(8,128)(2,1)S(1)} %shard_map.122.hold_ref, bf16[2048,128]{1,0:T(8,128)(2,1)S(1)} %collective-permute-done.3.refs_0_, ...), custom_call_target="tpu_custom_call" | custom-call | flops 5368709120 | bytes 10485760 | tf_op jit(solution)/shard_map/pallas_call | solution.py:302
  62.8 0.9 collective-permute-start.11
  63.7 6.2 %collective-permute-start.12 = (bf16[512,128]{1,0:T(8,128)(2,1)S(1)}, bf16[512,128]{1,0:T(8,128)(2,1)S(1)}, u32[]{:S(2)}, u32[]{:S(2)}) collective-permute-start(bf16[512,128]{1,0:T(8,128)(2,1)S(1)} %get-tuple-element.62), channel_id=1, source_target_pairs={{0,2},{1,3},{2,0},{3,1},{4,6},{5,7},{6,4},{7,5},{8,10},{9,11},{10,... | collective-permute-start | bytes 393224 | tf_op jit(solution)/shard_map/ppermute | solution.py:509
  69.9 0.7 collective-permute-start.13
  70.6 4.7 %shard_map.125.hold_ref = bf16[320,128,128]{2,1,0:T(8,128)(2,1)S(1)} custom-call(s32[9]{0:T(128)S(1)} %pad_add_fusion.place_ref, bf16[640,128,128]{2,1,0:T(8,128)(2,1)} %bitcast.16), custom_call_target="tpu_custom_call" | custom-call | bytes 20971520 | tf_op jit(solution)/shard_map/pallas_call | solution.py:160
  75.3 0.2 collective-permute-done.12.refs_2_
  75.5 0.9 collective-permute-done.13.refs_3_
  76.4 1.0 shard_map.126
  77.4 1.7 %collective-permute-start.15 = (bf16[768,128]{1,0:T(8,128)(2,1)S(1)}, bf16[768,128]{1,0:T(8,128)(2,1)S(1)}, u32[]{:S(2)}, u32[]{:S(2)}) collective-permute-start(bf16[768,128]{1,0:T(8,128)(2,1)S(1)} %get-tuple-element.72.refs_0_), channel_id=1, source_target_pairs={{0,2},{1,3},{2,0},{3,1},{4,6},{5,7},{6,4},{7,5},{8,10},{9,11},{10,... | collective-permute-start | bytes 589832 | tf_op jit(solution)/shard_map/ppermute | solution.py:509
  79.1 3.5 %collective-permute-start.14 = (bf16[768,128]{1,0:T(8,128)(2,1)S(1)}, bf16[768,128]{1,0:T(8,128)(2,1)S(1)}, u32[]{:S(2)}, u32[]{:S(2)}) collective-permute-start(bf16[768,128]{1,0:T(8,128)(2,1)S(1)} %get-tuple-element.72.refs_0_), channel_id=1, source_target_pairs={{0,1},{1,2},{2,3},{3,0},{4,5},{5,6},{6,7},{7,4},{8,9},{9,10},{10,1... | collective-permute-start | bytes 589832 | tf_op jit(solution)/shard_map/ppermute | solution.py:509
  82.6 4.7 %shard_map.127.hold_ref = bf16[320,128,128]{2,1,0:T(8,128)(2,1)S(1)} custom-call(s32[9]{0:T(128)S(1)} %pad_add_fusion.place_ref, bf16[640,128,128]{2,1,0:T(8,128)(2,1)} %bitcast.17), custom_call_target="tpu_custom_call" | custom-call | bytes 20971520 | tf_op jit(solution)/shard_map/pallas_call | solution.py:160
  87.3 0.3 collective-permute-done.14.refs_1_
  87.6 7.2 %shard_map.128 = (bf16[2304,128]{1,0:T(8,128)(2,1)S(1)}, bf16[4096,128]{1,0:T(8,128)(2,1)S(1)}, bf16[2048,128]{1,0:T(8,128)(2,1)S(1)}) custom-call(s32[1157]{0:T(1024)S(1)} %concatenate.43.list_ref, bf16[320,128,128]{2,1,0:T(8,128)(2,1)S(1)} %shard_map.125.hold_ref, bf16[768,128]{1,0:T(8,128)(2,1)S(1)} %get-tuple-element.72.refs_0_, ...), custom_call_target="tpu_custom_call" | custom-call | flops 5368709120 | bytes 10485760 | tf_op jit(solution)/shard_map/pallas_call | solution.py:415
  94.8 1.7 %collective-permute-start.18 = (bf16[4096,128]{1,0:T(8,128)(2,1)S(1)}, bf16[4096,128]{1,0:T(8,128)(2,1)S(1)}, u32[]{:S(2)}, u32[]{:S(2)}) collective-permute-start(bf16[4096,128]{1,0:T(8,128)(2,1)S(1)} %get-tuple-element.79), channel_id=1, source_target_pairs={{0,7},{1,4},{8,15},{9,12},{16,23},{17,20},{24,31},{25,28},{32,39},... | collective-permute-start | bytes 3145736 | tf_op jit(solution)/shard_map/ppermute | solution.py:494
  96.6 7.0 %shard_map.129 = (bf16[2048,128]{1,0:T(8,128)(2,1)S(1)}, bf16[2048,128]{1,0:T(8,128)(2,1)S(1)}, bf16[2048,128]{1,0:T(8,128)(2,1)S(1)}, bf16[2048,128]{1,0:T(8,128)(2,1)S(1)}) custom-call(s32[1157]{0:T(1024)S(1)} %concatenate.43.list_ref, bf16[320,128,128]{2,1,0:T(8,128)(2,1)S(1)} %shard_map.127.hold_ref, bf16[768,128]{1,0:T(8,128)(2,1)S(1)} %get-tuple-element.72.refs_0_, ...), custom_call_target="tpu_custom_call" | custom-call | flops 5368709120 | bytes 10485760 | tf_op jit(solution)/shard_map/pallas_call | solution.py:415
  103.6 0.8 collective-permute-done.19
  104.4 0.1 add_convert_fusion.1
  104.8 1.5 collective-permute-start.20
  106.2 6.8 %collective-permute-done.21 = bf16[1280,128]{1,0:T(8,128)(2,1)S(1)} collective-permute-done((bf16[1280,128]{1,0:T(8,128)(2,1)S(1)}, bf16[1280,128]{1,0:T(8,128)(2,1)S(1)}, u32[]{:S(2)}, u32[]{:S(2)}) %collective-permute-start.21) | collective-permute-done | bytes 327712 | tf_op jit(solution)/shard_map/ppermute | solution.py:494
  113.0 0.3 collective-permute-done.20
  113.3 2.3 %collective-permute-done.18 = bf16[4096,128]{1,0:T(8,128)(2,1)S(1)} collective-permute-done((bf16[4096,128]{1,0:T(8,128)(2,1)S(1)}, bf16[4096,128]{1,0:T(8,128)(2,1)S(1)}, u32[]{:S(2)}, u32[]{:S(2)}) %collective-permute-start.18) | collective-permute-done | bytes 1048608 | tf_op jit(solution)/shard_map/ppermute | solution.py:494
  115.7 0.3 add_convert_fusion.3
  116.1 0.7 collective-permute-start.17
  116.9 2.9 %collective-permute-start.23 = (bf16[2048,128]{1,0:T(8,128)(2,1)S(1)}, bf16[2048,128]{1,0:T(8,128)(2,1)S(1)}, u32[]{:S(2)}, u32[]{:S(2)}) collective-permute-start(bf16[2048,128]{1,0:T(8,128)(2,1)S(1)} %pad_maximum_fusion.2), channel_id=1, source_target_pairs={{0,96},{1,97},{8,104},{9,105},{16,112},{17,113},{24,120},{25,121},... | collective-permute-start | bytes 1572872 | tf_op jit(solution)/shard_map/ppermute | solution.py:494
  119.8 1.2 constant_dynamic-slice_fusion
  121.0 10.2 %collective-permute-done.22 = bf16[2304,128]{1,0:T(8,128)(2,1)S(1)} collective-permute-done((bf16[2304,128]{1,0:T(8,128)(2,1)S(1)}, bf16[2304,128]{1,0:T(8,128)(2,1)S(1)}, u32[]{:S(2)}, u32[]{:S(2)}) %collective-permute-start.22) | collective-permute-done | bytes 589856 | tf_op jit(solution)/shard_map/ppermute | solution.py:494
  131.3 0.3 add_convert_fusion
  131.6 3.1 %shard_map.130 = (bf16[768,128]{1,0:T(8,128)(2,1)S(1)}, bf16[768,128]{1,0:T(8,128)(2,1)S(1)}, bf16[768,128]{1,0:T(8,128)(2,1)S(1)}, bf16[768,128]{1,0:T(8,128)(2,1)S(1)}) custom-call(s32[1]{0:T(128)} %bitcast.7.place_ref, s32[1,2048]{1,0:T(1,128)S(1)} %collective-permute-done.4.order_ref, bf16[2304,128]{1,0:T(8,128)(2,1)S(1)} %pad_maximum_fusion.1.home_ref), custom_call_target="tpu_custom_call" | custom-call | tf_op jit(solution)/shard_map/pallas_call | solution.py:457
  134.7 6.9 %collective-permute-start.24 = (bf16[768,128]{1,0:T(8,128)(2,1)S(1)}, bf16[768,128]{1,0:T(8,128)(2,1)S(1)}, u32[]{:S(2)}, u32[]{:S(2)}) collective-permute-start(bf16[768,128]{1,0:T(8,128)(2,1)S(1)} %get-tuple-element.85), channel_id=1, source_target_pairs={{0,0},{1,23},{8,8},{9,31},{16,16},{17,7},{24,24},{25,15},{32,32},{... | collective-permute-start | bytes 589832 | tf_op jit(solution)/shard_map/ppermute | solution.py:494
  141.7 2.2 %collective-permute-start.26 = (bf16[768,128]{1,0:T(8,128)(2,1)S(1)}, bf16[768,128]{1,0:T(8,128)(2,1)S(1)}, u32[]{:S(2)}, u32[]{:S(2)}) collective-permute-start(bf16[768,128]{1,0:T(8,128)(2,1)S(1)} %get-tuple-element.87), channel_id=1, source_target_pairs={{0,2},{1,21},{8,10},{9,29},{16,18},{17,5},{24,26},{25,13},{32,34},... | collective-permute-start | bytes 589832 | tf_op jit(solution)/shard_map/ppermute | solution.py:494
  144.0 1.2 collective-permute-start.27
  145.2 0.6 collective-permute-done.25
  145.8 6.5 %collective-permute-done.26 = bf16[768,128]{1,0:T(8,128)(2,1)S(1)} collective-permute-done((bf16[768,128]{1,0:T(8,128)(2,1)S(1)}, bf16[768,128]{1,0:T(8,128)(2,1)S(1)}, u32[]{:S(2)}, u32[]{:S(2)}) %collective-permute-start.26) | collective-permute-done | bytes 196640 | tf_op jit(solution)/shard_map/ppermute | solution.py:494
  152.3 2.7 %collective-permute-done.27 = bf16[768,128]{1,0:T(8,128)(2,1)S(1)} collective-permute-done((bf16[768,128]{1,0:T(8,128)(2,1)S(1)}, bf16[768,128]{1,0:T(8,128)(2,1)S(1)}, u32[]{:S(2)}, u32[]{:S(2)}) %collective-permute-start.27) | collective-permute-done | bytes 196640 | tf_op jit(solution)/shard_map/ppermute | solution.py:494
  155.1 0.7 pad_maximum_fusion.5
  155.8 0.7 add_convert_fusion.6
  (80 shorter events, 2.9 us)
Async XLA Ops:
  0.6 1.0 copy-start
  4.8 15.1 %collective-permute-start = (bf16[2048,128]{1,0:T(8,128)(2,1)S(1)}, bf16[2048,128]{1,0:T(8,128)(2,1)S(1)}, u32[]{:S(2)}, u32[]{:S(2)}) collective-permute-start(bf16[2048,128]{1,0:T(8,128)(2,1)S(1)} %shard_map.121), channel_id=1, source_target_pairs={{0,0},{23,1},{8,8},{31,9},{16,16},{7,17},{24,24},{15,25},{32,32},{... | collective-permute-start | bytes 1572872 | tf_op jit(solution)/shard_map/ppermute | solution.py:494
  10.1 15.8 %collective-permute-start.4 = (s32[1,2048]{1,0:T(1,128)}, s32[1,2048]{1,0:T(1,128)S(1)}, u32[]{:S(2)}, u32[]{:S(2)}) collective-permute-start(s32[1,2048]{1,0:T(1,128)} %order_ref.1), channel_id=1, source_target_pairs={{0,0},{23,1},{8,8},{31,9},{16,16},{7,17},{24,24},{15,25},{32,32},{... | collective-permute-start | bytes 24584 | tf_op jit(solution)/shard_map/ppermute | solution.py:494
  19.9 13.4 %collective-permute-start.2 = (bf16[2048,128]{1,0:T(8,128)(2,1)S(1)}, bf16[2048,128]{1,0:T(8,128)(2,1)S(1)}, u32[]{:S(2)}, u32[]{:S(2)}) collective-permute-start(bf16[2048,128]{1,0:T(8,128)(2,1)S(1)} %collective-permute-done.refs_0_), channel_id=1, source_target_pairs={{0,32},{1,33},{8,40},{9,41},{16,48},{17,49},{24,56},{25,57},{32,64... | collective-permute-start | bytes 1572872 | tf_op jit(solution)/shard_map/ppermute | solution.py:494
  21.1 12.1 %collective-permute-start.1 = (bf16[2048,128]{1,0:T(8,128)(2,1)S(1)}, bf16[2048,128]{1,0:T(8,128)(2,1)S(1)}, u32[]{:S(2)}, u32[]{:S(2)}) collective-permute-start(bf16[2048,128]{1,0:T(8,128)(2,1)S(1)} %collective-permute-done.refs_0_), channel_id=1, source_target_pairs={{0,96},{1,97},{8,104},{9,105},{16,112},{17,113},{24,120},{25,121},... | collective-permute-start | bytes 1572872 | tf_op jit(solution)/shard_map/ppermute | solution.py:494
  24.3 8.9 %collective-permute-start.3 = (bf16[2048,128]{1,0:T(8,128)(2,1)S(1)}, bf16[2048,128]{1,0:T(8,128)(2,1)S(1)}, u32[]{:S(2)}, u32[]{:S(2)}) collective-permute-start(bf16[2048,128]{1,0:T(8,128)(2,1)S(1)} %collective-permute-done.refs_0_), channel_id=1, source_target_pairs={{0,7},{1,4},{8,15},{9,12},{16,23},{17,20},{24,31},{25,28},{32,39},... | collective-permute-start | bytes 1572872 | tf_op jit(solution)/shard_map/ppermute | solution.py:494
  33.3 9.3 %collective-permute-start.9 = (bf16[1024,128]{1,0:T(8,128)(2,1)S(1)}, bf16[1024,128]{1,0:T(8,128)(2,1)S(1)}, u32[]{:S(2)}, u32[]{:S(2)}) collective-permute-start(bf16[1024,128]{1,0:T(8,128)(2,1)S(1)} %slice.149), channel_id=1, source_target_pairs={{0,32},{1,33},{8,40},{9,41},{16,48},{17,49},{24,56},{25,57},{32,64... | collective-permute-start | bytes 786440 | tf_op jit(solution)/shard_map/ppermute | solution.py:494
  33.4 9.7 %collective-permute-start.7 = (bf16[1024,128]{1,0:T(8,128)(2,1)S(1)}, bf16[1024,128]{1,0:T(8,128)(2,1)S(1)}, u32[]{:S(2)}, u32[]{:S(2)}) collective-permute-start(bf16[1024,128]{1,0:T(8,128)(2,1)S(1)} %slice.148), channel_id=1, source_target_pairs={{0,96},{1,97},{8,104},{9,105},{16,112},{17,113},{24,120},{25,121},... | collective-permute-start | bytes 786440 | tf_op jit(solution)/shard_map/ppermute | solution.py:494
  36.1 18.7 %collective-permute-start.5 = (bf16[2048,128]{1,0:T(8,128)(2,1)S(1)}, bf16[2048,128]{1,0:T(8,128)(2,1)S(1)}, u32[]{:S(2)}, u32[]{:S(2)}) collective-permute-start(bf16[2048,128]{1,0:T(8,128)(2,1)S(1)} %collective-permute-done.1.refs_1_), channel_id=1, source_target_pairs={{0,7},{1,4},{8,15},{9,12},{16,23},{17,20},{24,31},{25,28},{32,39},... | collective-permute-start | bytes 1572872 | tf_op jit(solution)/shard_map/ppermute | solution.py:494
  36.4 18.5 %collective-permute-start.6 = (bf16[2048,128]{1,0:T(8,128)(2,1)S(1)}, bf16[2048,128]{1,0:T(8,128)(2,1)S(1)}, u32[]{:S(2)}, u32[]{:S(2)}) collective-permute-start(bf16[2048,128]{1,0:T(8,128)(2,1)S(1)} %collective-permute-done.2.refs_2_), channel_id=1, source_target_pairs={{0,7},{1,4},{8,15},{9,12},{16,23},{17,20},{24,31},{25,28},{32,39},... | collective-permute-start | bytes 1572872 | tf_op jit(solution)/shard_map/ppermute | solution.py:494
  42.6 12.2 %collective-permute-start.10 = (bf16[1024,128]{1,0:T(8,128)(2,1)S(1)}, bf16[1024,128]{1,0:T(8,128)(2,1)S(1)}, u32[]{:S(2)}, u32[]{:S(2)}) collective-permute-start(bf16[1024,128]{1,0:T(8,128)(2,1)S(1)} %collective-permute-done.9.refs_4_), channel_id=1, source_target_pairs={{0,7},{1,4},{8,15},{9,12},{16,23},{17,20},{24,31},{25,28},{32,39},... | collective-permute-start | bytes 786440 | tf_op jit(solution)/shard_map/ppermute | solution.py:494
  43.1 13.1 %collective-permute-start.8 = (bf16[1024,128]{1,0:T(8,128)(2,1)S(1)}, bf16[1024,128]{1,0:T(8,128)(2,1)S(1)}, u32[]{:S(2)}, u32[]{:S(2)}) collective-permute-start(bf16[1024,128]{1,0:T(8,128)(2,1)S(1)} %collective-permute-done.7.refs_3_), channel_id=1, source_target_pairs={{0,7},{1,4},{8,15},{9,12},{16,23},{17,20},{24,31},{25,28},{32,39},... | collective-permute-start | bytes 786440 | tf_op jit(solution)/shard_map/ppermute | solution.py:494
  62.8 12.5 %collective-permute-start.11 = (bf16[512,128]{1,0:T(8,128)(2,1)S(1)}, bf16[512,128]{1,0:T(8,128)(2,1)S(1)}, u32[]{:S(2)}, u32[]{:S(2)}) collective-permute-start(bf16[512,128]{1,0:T(8,128)(2,1)S(1)} %get-tuple-element.59), channel_id=1, source_target_pairs={{0,1},{1,2},{2,3},{3,0},{4,5},{5,6},{6,7},{7,4},{8,9},{9,10},{10,1... | collective-permute-start | bytes 393224 | tf_op jit(solution)/shard_map/ppermute | solution.py:509
  63.7 11.8 %collective-permute-start.12 = (bf16[512,128]{1,0:T(8,128)(2,1)S(1)}, bf16[512,128]{1,0:T(8,128)(2,1)S(1)}, u32[]{:S(2)}, u32[]{:S(2)}) collective-permute-start(bf16[512,128]{1,0:T(8,128)(2,1)S(1)} %get-tuple-element.62), channel_id=1, source_target_pairs={{0,2},{1,3},{2,0},{3,1},{4,6},{5,7},{6,4},{7,5},{8,10},{9,11},{10,... | collective-permute-start | bytes 393224 | tf_op jit(solution)/shard_map/ppermute | solution.py:509
  69.9 6.5 %collective-permute-start.13 = (bf16[512,128]{1,0:T(8,128)(2,1)S(1)}, bf16[512,128]{1,0:T(8,128)(2,1)S(1)}, u32[]{:S(2)}, u32[]{:S(2)}) collective-permute-start(bf16[512,128]{1,0:T(8,128)(2,1)S(1)} %get-tuple-element.63), channel_id=1, source_target_pairs={{0,3},{1,0},{2,1},{3,2},{4,7},{5,4},{6,5},{7,6},{8,11},{9,8},{10,9... | collective-permute-start | bytes 393224 | tf_op jit(solution)/shard_map/ppermute | solution.py:509
  70.6 5.8 %copy-start.1 = (bf16[512,256]{1,0:T(8,128)(2,1)S(1)}, bf16[512,256]{1,0:T(8,128)(2,1)}, u32[]{:S(2)}) copy-start(bf16[512,256]{1,0:T(8,128)(2,1)} %refs_5_.1) | copy-start | bytes 786436
  70.6 5.8 %copy-start.2 = (bf16[128,256]{1,0:T(8,128)(2,1)S(1)}, bf16[128,256]{1,0:T(8,128)(2,1)}, u32[]{:S(2)}) copy-start(bf16[128,256]{1,0:T(8,128)(2,1)} %refs_4_.1) | copy-start | bytes 196612
  77.4 9.9 %collective-permute-start.16 = (bf16[768,128]{1,0:T(8,128)(2,1)S(1)}, bf16[768,128]{1,0:T(8,128)(2,1)S(1)}, u32[]{:S(2)}, u32[]{:S(2)}) collective-permute-start(bf16[768,128]{1,0:T(8,128)(2,1)S(1)} %get-tuple-element.72.refs_0_), channel_id=1, source_target_pairs={{0,3},{1,0},{2,1},{3,2},{4,7},{5,4},{6,5},{7,6},{8,11},{9,8},{10,9... | collective-permute-start | bytes 589832 | tf_op jit(solution)/shard_map/ppermute | solution.py:509
  77.4 9.9 %collective-permute-start.15 = (bf16[768,128]{1,0:T(8,128)(2,1)S(1)}, bf16[768,128]{1,0:T(8,128)(2,1)S(1)}, u32[]{:S(2)}, u32[]{:S(2)}) collective-permute-start(bf16[768,128]{1,0:T(8,128)(2,1)S(1)} %get-tuple-element.72.refs_0_), channel_id=1, source_target_pairs={{0,2},{1,3},{2,0},{3,1},{4,6},{5,7},{6,4},{7,5},{8,10},{9,11},{10,... | collective-permute-start | bytes 589832 | tf_op jit(solution)/shard_map/ppermute | solution.py:509
  79.1 8.5 %collective-permute-start.14 = (bf16[768,128]{1,0:T(8,128)(2,1)S(1)}, bf16[768,128]{1,0:T(8,128)(2,1)S(1)}, u32[]{:S(2)}, u32[]{:S(2)}) collective-permute-start(bf16[768,128]{1,0:T(8,128)(2,1)S(1)} %get-tuple-element.72.refs_0_), channel_id=1, source_target_pairs={{0,1},{1,2},{2,3},{3,0},{4,5},{5,6},{6,7},{7,4},{8,9},{9,10},{10,1... | collective-permute-start | bytes 589832 | tf_op jit(solution)/shard_map/ppermute | solution.py:509
  94.7 9.7 %collective-permute-start.19 = (bf16[2304,128]{1,0:T(8,128)(2,1)S(1)}, bf16[2304,128]{1,0:T(8,128)(2,1)S(1)}, u32[]{:S(2)}, u32[]{:S(2)}) collective-permute-start(bf16[2304,128]{1,0:T(8,128)(2,1)S(1)} %get-tuple-element.81), channel_id=1, source_target_pairs={{0,7},{1,4},{8,15},{9,12},{16,23},{17,20},{24,31},{25,28},{32,39},... | collective-permute-start | bytes 1769480 | tf_op jit(solution)/shard_map/ppermute | solution.py:494
  94.8 20.8 %collective-permute-start.18 = (bf16[4096,128]{1,0:T(8,128)(2,1)S(1)}, bf16[4096,128]{1,0:T(8,128)(2,1)S(1)}, u32[]{:S(2)}, u32[]{:S(2)}) collective-permute-start(bf16[4096,128]{1,0:T(8,128)(2,1)S(1)} %get-tuple-element.79), channel_id=1, source_target_pairs={{0,7},{1,4},{8,15},{9,12},{16,23},{17,20},{24,31},{25,28},{32,39},... | collective-permute-start | bytes 3145736 | tf_op jit(solution)/shard_map/ppermute | solution.py:494
  104.7 8.3 %collective-permute-start.21 = (bf16[1280,128]{1,0:T(8,128)(2,1)S(1)}, bf16[1280,128]{1,0:T(8,128)(2,1)S(1)}, u32[]{:S(2)}, u32[]{:S(2)}) collective-permute-start(bf16[1280,128]{1,0:T(8,128)(2,1)S(1)} %get-tuple-element.103), channel_id=1, source_target_pairs={{0,96},{1,97},{8,104},{9,105},{16,112},{17,113},{24,120},{25,121},... | collective-permute-start | bytes 983048 | tf_op jit(solution)/shard_map/ppermute | solution.py:494
  104.8 8.6 %collective-permute-start.20 = (bf16[1280,128]{1,0:T(8,128)(2,1)S(1)}, bf16[1280,128]{1,0:T(8,128)(2,1)S(1)}, u32[]{:S(2)}, u32[]{:S(2)}) collective-permute-start(bf16[1280,128]{1,0:T(8,128)(2,1)S(1)} %get-tuple-element.104), channel_id=1, source_target_pairs={{0,32},{1,33},{8,40},{9,41},{16,48},{17,49},{24,56},{25,57},{32,64... | collective-permute-start | bytes 983048 | tf_op jit(solution)/shard_map/ppermute | solution.py:494
  116.0 15.2 %collective-permute-start.22 = (bf16[2304,128]{1,0:T(8,128)(2,1)S(1)}, bf16[2304,128]{1,0:T(8,128)(2,1)S(1)}, u32[]{:S(2)}, u32[]{:S(2)}) collective-permute-start(bf16[2304,128]{1,0:T(8,128)(2,1)S(1)} %pad_maximum_fusion), channel_id=1, source_target_pairs={{0,32},{1,33},{8,40},{9,41},{16,48},{17,49},{24,56},{25,57},{32,64... | collective-permute-start | bytes 1769480 | tf_op jit(solution)/shard_map/ppermute | solution.py:494
  116.1 15.1 %collective-permute-start.17 = (bf16[2048,128]{1,0:T(8,128)(2,1)S(1)}, bf16[2048,128]{1,0:T(8,128)(2,1)S(1)}, u32[]{:S(2)}, u32[]{:S(2)}) collective-permute-start(bf16[2048,128]{1,0:T(8,128)(2,1)S(1)} %get-tuple-element.77), channel_id=1, source_target_pairs={{0,7},{1,4},{8,15},{9,12},{16,23},{17,20},{24,31},{25,28},{32,39},... | collective-permute-start | bytes 1572872 | tf_op jit(solution)/shard_map/ppermute | solution.py:494
  116.9 14.4 %collective-permute-start.23 = (bf16[2048,128]{1,0:T(8,128)(2,1)S(1)}, bf16[2048,128]{1,0:T(8,128)(2,1)S(1)}, u32[]{:S(2)}, u32[]{:S(2)}) collective-permute-start(bf16[2048,128]{1,0:T(8,128)(2,1)S(1)} %pad_maximum_fusion.2), channel_id=1, source_target_pairs={{0,96},{1,97},{8,104},{9,105},{16,112},{17,113},{24,120},{25,121},... | collective-permute-start | bytes 1572872 | tf_op jit(solution)/shard_map/ppermute | solution.py:494
  134.7 10.4 %collective-permute-start.24 = (bf16[768,128]{1,0:T(8,128)(2,1)S(1)}, bf16[768,128]{1,0:T(8,128)(2,1)S(1)}, u32[]{:S(2)}, u32[]{:S(2)}) collective-permute-start(bf16[768,128]{1,0:T(8,128)(2,1)S(1)} %get-tuple-element.85), channel_id=1, source_target_pairs={{0,0},{1,23},{8,8},{9,31},{16,16},{17,7},{24,24},{25,15},{32,32},{... | collective-permute-start | bytes 589832 | tf_op jit(solution)/shard_map/ppermute | solution.py:494
  141.7 4.1 %collective-permute-start.25 = (bf16[768,128]{1,0:T(8,128)(2,1)S(1)}, bf16[768,128]{1,0:T(8,128)(2,1)S(1)}, u32[]{:S(2)}, u32[]{:S(2)}) collective-permute-start(bf16[768,128]{1,0:T(8,128)(2,1)S(1)} %get-tuple-element.86), channel_id=1, source_target_pairs={{0,1},{1,20},{8,9},{9,28},{16,17},{17,4},{24,25},{25,12},{32,33},{... | collective-permute-start | bytes 589832 | tf_op jit(solution)/shard_map/ppermute | solution.py:494
  141.7 10.6 %collective-permute-start.26 = (bf16[768,128]{1,0:T(8,128)(2,1)S(1)}, bf16[768,128]{1,0:T(8,128)(2,1)S(1)}, u32[]{:S(2)}, u32[]{:S(2)}) collective-permute-start(bf16[768,128]{1,0:T(8,128)(2,1)S(1)} %get-tuple-element.87), channel_id=1, source_target_pairs={{0,2},{1,21},{8,10},{9,29},{16,18},{17,5},{24,26},{25,13},{32,34},... | collective-permute-start | bytes 589832 | tf_op jit(solution)/shard_map/ppermute | solution.py:494
  144.0 11.1 %collective-permute-start.27 = (bf16[768,128]{1,0:T(8,128)(2,1)S(1)}, bf16[768,128]{1,0:T(8,128)(2,1)S(1)}, u32[]{:S(2)}, u32[]{:S(2)}) collective-permute-start(bf16[768,128]{1,0:T(8,128)(2,1)S(1)} %get-tuple-element.88), channel_id=1, source_target_pairs={{0,3},{1,22},{8,11},{9,30},{16,19},{17,6},{24,27},{25,14},{32,35},... | collective-permute-start | bytes 589832 | tf_op jit(solution)/shard_map/ppermute | solution.py:494

commit v6 on v5

--- a/solution.py
+++ b/solution.py
@@ -9,9 +9,9 @@
 from jax.sharding import PartitionSpec as P
 
 TILE = 128
-FORWARD_TURN = 4
+FORWARD_TURN = 8
 BACKWARD_TURN = 16
-FORWARD_WIDTH = 8
+FORWARD_WIDTH = 4
 BACKWARD_WIDTH = 2
 FORWARD_WAVES = ((0, 1, 3, 2), (4, 5, 7, 6))
 BACKWARD_WAVES = ((6, 5, 7, 4), (0, 1, 2, 3))
@@ -511,8 +511,6 @@
 
     blocked = order_rows(node_order, features)
     near = moved(blocked, fetch_pairs())
-    later_order, blocked = lax.optimization_barrier((node_order, blocked))
-    near_order = moved(later_order, fetch_pairs())
     alive = jnp.arange(per_slot, dtype=jnp.int32)[None, :] < counts[:, None]
     cells = jnp.take(jnp.where(alive, row_ids * CODE + col_ids, -1), slots, axis=0)
 
@@ -548,8 +546,8 @@
     above, below = down(near), up(near)
     ready, packed = lax.optimization_barrier((near, packed))
     far = swapped(ready)
-    above, below, far, forward_list, packed, near_order = lax.optimization_barrier(
-        (above, below, far, forward_list, packed, near_order)
+    above, below, far, forward_list, packed = lax.optimization_barrier(
+        (above, below, far, forward_list, packed)
     )
     middle = [down(above[:half]), up(below[half:])]
     known, far = lax.optimization_barrier((place, far))
@@ -589,9 +587,14 @@
     mine = products(1, packed)
     two = added(mine[2], returned[:rows_dev])
     ride = added(others[0][rows_dev:], returned[rows_dev:])
-    from_below, from_above = lax.optimization_barrier(
-        (up(jnp.concatenate([two[:half], ride])), down(jnp.concatenate([two[half:], ride])))
-    )
+    from_below, from_above, later_order = lax.optimization_barrier(
+        (
+            up(jnp.concatenate([two[:half], ride])),
+            down(jnp.concatenate([two[half:], ride])),
+            node_order,
+        )
+    )
+    near_order = moved(later_order, fetch_pairs())
     one = jnp.concatenate(
         [
             added(mine[1][:half], sides[:half], from_below[:half]),

time: 157 us -> 155 us (0.987)
  Pallas kernels: 52.3 us -> 38.2 us
  waiting for transfers between devices: 41.7 us -> 49.9 us
  starting transfers between devices: 49.4 us -> 53.4 us
    ppermute x22, waiting for transfers between devices: 40.3 us -> 48.6 us  [moved(): return lax.ppermute(value, both, listed)]
    pallas_call x2, Pallas kernels: 14.2 us -> 7.35 us  [backward_product(): pl.pallas_call(functools.partial(backward_kernel, sizes, rows, lists, fir...]
    pallas_call x2, Pallas kernels: 16.9 us -> 10.3 us  [forward_product(): pl.pallas_call(functools.partial(forward_kernel, len(xs), lists, wave, ca...]
    ppermute x22, starting transfers between devices: 36.4 us -> 39.8 us  [moved(): return lax.ppermute(value, both, listed)]
  transfers between devices with their start and end apart: 28 -> 28, of which waited for: 14 -> 16; matrix products, arithmetic and copies ran while one was open for 6% -> 6% of each run, Pallas kernels for 20% -> 16%
where the time goes in v6:
time: 155 us
  starting transfers between devices  53.4 us (34%)
  waiting for transfers between devices  49.9 us (32%)
  Pallas kernels  38.2 us (25%)
  other arithmetic  7.33 us (5%)
  local copies, waits for them, and re-layouts  5.25 us (3%)
    ppermute x22, waiting for transfers between devices, moved(): return lax.ppermute(value, both, listed)  48.6 us
    ppermute x22, starting transfers between devices, moved(): return lax.ppermute(value, both, listed)  39.8 us
    pallas_call x3, Pallas kernels, hold(): pl.pallas_call(functools.partial(hold_kernel, items), out_shape=jax.Shape...  14 us
    ppermute x6, starting transfers between devices, to_reps(): received.append(lax.ppermute(values[shift], 'rep', along))  13.7 us
    pallas_call x2, Pallas kernels, forward_product(): pl.pallas_call(functools.partial(forward_kernel, len(xs), lists, wave, ca...  10.3 us
    pallas_call x2, Pallas kernels, backward_product(): pl.pallas_call(functools.partial(backward_kernel, sizes, rows, lists, fir...  7.35 us
    pallas_call x1, Pallas kernels, restore(): pl.pallas_call(restore_kernel, out_shape=[out_shape] * reps, grid_spec=pl...  3.13 us
  transfers between devices with their start and end apart: 28, of which 16 were waited for; matrix products, arithmetic and copies ran while one was open for 6% of the time, Pallas kernels for 16%

profile of v6, /device:TPU:1, one launch (start us, length us, event | category | flops | bytes accessed | tf_op | source)
XLA Modules:
  0.0 155.2 jit_solution(8495987552033477499)
XLA Ops:
  0.6 1.0 copy-done
  1.7 0.7 copy-done.3
  2.4 2.4 %shard_map.121 = bf16[2048,128]{1,0:T(8,128)(2,1)S(1)} custom-call(s32[1,2048]{1,0:T(1,128)S(1)} %copy-done.3, bf16[2048,128]{1,0:T(8,128)(2,1)S(1)} %copy-done), custom_call_target="tpu_custom_call" | custom-call | tf_op jit(solution)/shard_map/pallas_call | solution.py:123
  4.7 5.3 %collective-permute-start = (bf16[2048,128]{1,0:T(8,128)(2,1)S(1)}, bf16[2048,128]{1,0:T(8,128)(2,1)S(1)}, u32[]{:S(2)}, u32[]{:S(2)}) collective-permute-start(bf16[2048,128]{1,0:T(8,128)(2,1)S(1)} %shard_map.121), channel_id=1, source_target_pairs={{0,0},{23,1},{8,8},{31,9},{16,16},{7,17},{24,24},{15,25},{32,32},{... | collective-permute-start | bytes 1572872 | tf_op jit(solution)/shard_map/ppermute | solution.py:494
  10.1 0.7 compare_and_fusion
  10.8 0.7 fusion.14
  11.5 0.8 bitcast_select_fusion
  12.3 0.6 gather_fusion
  13.8 0.4 convert_reduce_fusion
  14.2 5.6 %collective-permute-done.refs_0_ = bf16[2048,128]{1,0:T(8,128)(2,1)S(1)} collective-permute-done((bf16[2048,128]{1,0:T(8,128)(2,1)S(1)}, bf16[2048,128]{1,0:T(8,128)(2,1)S(1)}, u32[]{:S(2)}, u32[]{:S(2)}) %collective-permute-start) | collective-permute-done | bytes 524320 | tf_op jit(solution)/shard_map/ppermute | solution.py:494
  19.8 1.3 collective-permute-start.2
  21.1 1.5 collective-permute-start.1
  22.9 0.4 convert_reduce_fusion.1
  24.9 0.7 fusion.15
  25.7 7.2 %collective-permute-done.3.refs_0_ = bf16[2048,128]{1,0:T(8,128)(2,1)S(1)} collective-permute-done((bf16[2048,128]{1,0:T(8,128)(2,1)S(1)}, bf16[2048,128]{1,0:T(8,128)(2,1)S(1)}, u32[]{:S(2)}, u32[]{:S(2)}) %collective-permute-start.3) | collective-permute-done | bytes 524320 | tf_op jit(solution)/shard_map/ppermute | solution.py:494
  33.1 2.7 %collective-permute-start.6 = (bf16[1024,128]{1,0:T(8,128)(2,1)S(1)}, bf16[1024,128]{1,0:T(8,128)(2,1)S(1)}, u32[]{:S(2)}, u32[]{:S(2)}) collective-permute-start(bf16[1024,128]{1,0:T(8,128)(2,1)S(1)} %slice.148), channel_id=1, source_target_pairs={{0,96},{1,97},{8,104},{9,105},{16,112},{17,113},{24,120},{25,121},... | collective-permute-start | bytes 786440 | tf_op jit(solution)/shard_map/ppermute | solution.py:494
  35.8 0.6 collective-permute-start.4
  36.4 1.2 collective-permute-start.5
  37.6 4.7 %shard_map.122.hold_ref = bf16[320,128,128]{2,1,0:T(8,128)(2,1)S(1)} custom-call(s32[9]{0:T(128)S(1)} %pad_add_fusion.place_ref, bf16[640,128,128]{2,1,0:T(8,128)(2,1)} %bitcast.14), custom_call_target="tpu_custom_call" | custom-call | bytes 20971520 | tf_op jit(solution)/shard_map/pallas_call | solution.py:160
  42.3 0.6 collective-permute-start.9
  42.9 1.2 collective-permute-start.7
  44.1 7.1 %shard_map.123.refs_5_ = f32[2176,128]{1,0:T(8,128)S(1)} custom-call(s32[971]{0:T(1024)S(1)} %concatenate.46.list_ref, bf16[640,128,128]{2,1,0:T(8,128)(2,1)} %bitcast.15, bf16[2048,128]{1,0:T(8,128)(2,1)S(1)} %collective-permute-done.refs_0_, bf16[2048,128]{1,0:T(8,128)(2,1)S(1)} %collective-permute-done.1.refs_1_, ...), custom_call_target="tpu_custom_call" | custom-call | flops 5368709120 | bytes 10485760 | tf_op jit(solution)/shard_map/pallas_call | solution.py:302
  51.2 1.9 %collective-permute-done.9.refs_4_ = bf16[1024,128]{1,0:T(8,128)(2,1)S(1)} collective-permute-done((bf16[1024,128]{1,0:T(8,128)(2,1)S(1)}, bf16[1024,128]{1,0:T(8,128)(2,1)S(1)}, u32[]{:S(2)}, u32[]{:S(2)}) %collective-permute-start.9) | collective-permute-done | bytes 262176 | tf_op jit(solution)/shard_map/ppermute | solution.py:494
  53.1 2.8 %collective-permute-done.7.refs_3_ = bf16[1024,128]{1,0:T(8,128)(2,1)S(1)} collective-permute-done((bf16[1024,128]{1,0:T(8,128)(2,1)S(1)}, bf16[1024,128]{1,0:T(8,128)(2,1)S(1)}, u32[]{:S(2)}, u32[]{:S(2)}) %collective-permute-start.7) | collective-permute-done | bytes 262176 | tf_op jit(solution)/shard_map/ppermute | solution.py:494
  55.9 3.3 %shard_map.124 = (bf16[512,128]{1,0:T(8,128)(2,1)S(1)}, bf16[512,128]{1,0:T(8,128)(2,1)S(1)}, bf16[512,128]{1,0:T(8,128)(2,1)S(1)}, bf16[512,128]{1,0:T(8,128)(2,1)S(1)}) custom-call(s32[971]{0:T(1024)S(1)} %concatenate.46.list_ref, bf16[320,128,128]{2,1,0:T(8,128)(2,1)S(1)} %shard_map.122.hold_ref, bf16[2048,128]{1,0:T(8,128)(2,1)S(1)} %collective-permute-done.3.refs_0_, ...), custom_call_target="tpu_custom_call" | custom-call | flops 5368709120 | bytes 10485760 | tf_op jit(solution)/shard_map/pallas_call | solution.py:302
  59.2 6.4 %collective-permute-start.10 = (bf16[512,128]{1,0:T(8,128)(2,1)S(1)}, bf16[512,128]{1,0:T(8,128)(2,1)S(1)}, u32[]{:S(2)}, u32[]{:S(2)}) collective-permute-start(bf16[512,128]{1,0:T(8,128)(2,1)S(1)} %get-tuple-element.57), channel_id=1, source_target_pairs={{0,1},{1,2},{2,3},{3,0},{4,5},{5,6},{6,7},{7,4},{8,9},{9,10},{10,1... | collective-permute-start | bytes 393224 | tf_op jit(solution)/shard_map/ppermute | solution.py:509
  65.6 0.4 collective-permute-start.11
  66.0 0.7 collective-permute-start.12
  66.7 4.7 %shard_map.125.hold_ref = bf16[320,128,128]{2,1,0:T(8,128)(2,1)S(1)} custom-call(s32[9]{0:T(128)S(1)} %pad_add_fusion.place_ref, bf16[640,128,128]{2,1,0:T(8,128)(2,1)} %bitcast.16), custom_call_target="tpu_custom_call" | custom-call | bytes 20971520 | tf_op jit(solution)/shard_map/pallas_call | solution.py:160
  71.4 0.3 collective-permute-done.11.refs_2_
  71.7 0.8 collective-permute-done.12.refs_3_
  72.5 1.0 shard_map.126
  73.6 1.2 collective-permute-start.15
  74.7 1.5 collective-permute-start.14
  76.2 3.5 %collective-permute-start.13 = (bf16[768,128]{1,0:T(8,128)(2,1)S(1)}, bf16[768,128]{1,0:T(8,128)(2,1)S(1)}, u32[]{:S(2)}, u32[]{:S(2)}) collective-permute-start(bf16[768,128]{1,0:T(8,128)(2,1)S(1)} %get-tuple-element.69.refs_0_), channel_id=1, source_target_pairs={{0,1},{1,2},{2,3},{3,0},{4,5},{5,6},{6,7},{7,4},{8,9},{9,10},{10,1... | collective-permute-start | bytes 589832 | tf_op jit(solution)/shard_map/ppermute | solution.py:509
  79.7 4.7 %shard_map.127.hold_ref = bf16[320,128,128]{2,1,0:T(8,128)(2,1)S(1)} custom-call(s32[9]{0:T(128)S(1)} %pad_add_fusion.place_ref, bf16[640,128,128]{2,1,0:T(8,128)(2,1)} %bitcast.17), custom_call_target="tpu_custom_call" | custom-call | bytes 20971520 | tf_op jit(solution)/shard_map/pallas_call | solution.py:160
  84.4 0.3 collective-permute-done.13.refs_1_
  84.7 3.8 %shard_map.128 = (bf16[2304,128]{1,0:T(8,128)(2,1)S(1)}, bf16[4096,128]{1,0:T(8,128)(2,1)S(1)}, bf16[2048,128]{1,0:T(8,128)(2,1)S(1)}) custom-call(s32[1157]{0:T(1024)S(1)} %concatenate.43.list_ref, bf16[320,128,128]{2,1,0:T(8,128)(2,1)S(1)} %shard_map.125.hold_ref, bf16[768,128]{1,0:T(8,128)(2,1)S(1)} %get-tuple-element.69.refs_0_, ...), custom_call_target="tpu_custom_call" | custom-call | flops 5368709120 | bytes 10485760 | tf_op jit(solution)/shard_map/pallas_call | solution.py:415
  88.4 7.6 %collective-permute-start.16 = (bf16[2304,128]{1,0:T(8,128)(2,1)S(1)}, bf16[2304,128]{1,0:T(8,128)(2,1)S(1)}, u32[]{:S(2)}, u32[]{:S(2)}) collective-permute-start(bf16[2304,128]{1,0:T(8,128)(2,1)S(1)} %get-tuple-element.74), channel_id=1, source_target_pairs={{0,7},{1,4},{8,15},{9,12},{16,23},{17,20},{24,31},{25,28},{32,39},... | collective-permute-start | bytes 1769480 | tf_op jit(solution)/shard_map/ppermute | solution.py:494
  96.2 3.6 %shard_map.129 = (bf16[2048,128]{1,0:T(8,128)(2,1)S(1)}, bf16[2048,128]{1,0:T(8,128)(2,1)S(1)}, bf16[2048,128]{1,0:T(8,128)(2,1)S(1)}, bf16[2048,128]{1,0:T(8,128)(2,1)S(1)}) custom-call(s32[1157]{0:T(1024)S(1)} %concatenate.43.list_ref, bf16[320,128,128]{2,1,0:T(8,128)(2,1)S(1)} %shard_map.127.hold_ref, bf16[768,128]{1,0:T(8,128)(2,1)S(1)} %get-tuple-element.69.refs_0_, ...), custom_call_target="tpu_custom_call" | custom-call | flops 5368709120 | bytes 10485760 | tf_op jit(solution)/shard_map/pallas_call | solution.py:415
  99.8 4.2 %collective-permute-done.16 = bf16[2304,128]{1,0:T(8,128)(2,1)S(1)} collective-permute-done((bf16[2304,128]{1,0:T(8,128)(2,1)S(1)}, bf16[2304,128]{1,0:T(8,128)(2,1)S(1)}, u32[]{:S(2)}, u32[]{:S(2)}) %collective-permute-start.16) | collective-permute-done | bytes 589856 | tf_op jit(solution)/shard_map/ppermute | solution.py:494
  104.2 0.4 collective-permute-start.18
  104.6 1.6 %collective-permute-start.17 = (bf16[1280,128]{1,0:T(8,128)(2,1)S(1)}, bf16[1280,128]{1,0:T(8,128)(2,1)S(1)}, u32[]{:S(2)}, u32[]{:S(2)}) collective-permute-start(bf16[1280,128]{1,0:T(8,128)(2,1)S(1)} %get-tuple-element.102), channel_id=1, source_target_pairs={{0,32},{1,33},{8,40},{9,41},{16,48},{17,49},{24,56},{25,57},{32,64... | collective-permute-start | bytes 983048 | tf_op jit(solution)/shard_map/ppermute | solution.py:494
  106.2 6.8 %collective-permute-done.18 = bf16[1280,128]{1,0:T(8,128)(2,1)S(1)} collective-permute-done((bf16[1280,128]{1,0:T(8,128)(2,1)S(1)}, bf16[1280,128]{1,0:T(8,128)(2,1)S(1)}, u32[]{:S(2)}, u32[]{:S(2)}) %collective-permute-start.18) | collective-permute-done | bytes 327712 | tf_op jit(solution)/shard_map/ppermute | solution.py:494
  113.0 0.8 collective-permute-done.17
  113.8 1.4 collective-permute-done.21
  115.2 0.3 add_convert_fusion.3
  115.6 1.6 %collective-permute-start.22 = (bf16[2304,128]{1,0:T(8,128)(2,1)S(1)}, bf16[2304,128]{1,0:T(8,128)(2,1)S(1)}, u32[]{:S(2)}, u32[]{:S(2)}) collective-permute-start(bf16[2304,128]{1,0:T(8,128)(2,1)S(1)} %pad_maximum_fusion), channel_id=1, source_target_pairs={{0,32},{1,33},{8,40},{9,41},{16,48},{17,49},{24,56},{25,57},{32,64... | collective-permute-start | bytes 1769480 | tf_op jit(solution)/shard_map/ppermute | solution.py:494
  117.1 2.0 %collective-permute-start.20 = (bf16[2048,128]{1,0:T(8,128)(2,1)S(1)}, bf16[2048,128]{1,0:T(8,128)(2,1)S(1)}, u32[]{:S(2)}, u32[]{:S(2)}) collective-permute-start(bf16[2048,128]{1,0:T(8,128)(2,1)S(1)} %get-tuple-element.77), channel_id=1, source_target_pairs={{0,7},{1,4},{8,15},{9,12},{16,23},{17,20},{24,31},{25,28},{32,39},... | collective-permute-start | bytes 1572872 | tf_op jit(solution)/shard_map/ppermute | solution.py:494
  119.2 1.0 collective-permute-start.23
  120.2 1.2 constant_dynamic-slice_fusion
  121.4 2.4 %collective-permute-start.19 = (s32[1,2048]{1,0:T(1,128)S(1)}, s32[1,2048]{1,0:T(1,128)S(1)}, u32[]{:S(2)}, u32[]{:S(2)}) collective-permute-start(s32[1,2048]{1,0:T(1,128)S(1)} %copy-done.4), channel_id=1, source_target_pairs={{0,0},{23,1},{8,8},{31,9},{16,16},{7,17},{24,24},{15,25},{32,32},{... | collective-permute-start | bytes 24584 | tf_op jit(solution)/shard_map/ppermute | solution.py:494
  123.8 7.2 %collective-permute-done.22 = bf16[2304,128]{1,0:T(8,128)(2,1)S(1)} collective-permute-done((bf16[2304,128]{1,0:T(8,128)(2,1)S(1)}, bf16[2304,128]{1,0:T(8,128)(2,1)S(1)}, u32[]{:S(2)}, u32[]{:S(2)}) %collective-permute-start.22) | collective-permute-done | bytes 589856 | tf_op jit(solution)/shard_map/ppermute | solution.py:494
  131.0 1.0 collective-permute-done.23
  132.0 0.3 add_convert_fusion
  132.4 3.1 %shard_map.130 = (bf16[768,128]{1,0:T(8,128)(2,1)S(1)}, bf16[768,128]{1,0:T(8,128)(2,1)S(1)}, bf16[768,128]{1,0:T(8,128)(2,1)S(1)}, bf16[768,128]{1,0:T(8,128)(2,1)S(1)}) custom-call(s32[1]{0:T(128)} %bitcast.7.place_ref, s32[1,2048]{1,0:T(1,128)S(1)} %collective-permute-done.19.order_ref, bf16[2304,128]{1,0:T(8,128)(2,1)S(1)} %pad_maximum_fusion.1.home_ref), custom_call_target="tpu_custom_call" | custom-call | tf_op jit(solution)/shard_map/pallas_call | solution.py:457
  135.5 4.6 %collective-permute-start.24 = (bf16[768,128]{1,0:T(8,128)(2,1)S(1)}, bf16[768,128]{1,0:T(8,128)(2,1)S(1)}, u32[]{:S(2)}, u32[]{:S(2)}) collective-permute-start(bf16[768,128]{1,0:T(8,128)(2,1)S(1)} %get-tuple-element.83), channel_id=1, source_target_pairs={{0,0},{1,23},{8,8},{9,31},{16,16},{17,7},{24,24},{25,15},{32,32},{... | collective-permute-start | bytes 589832 | tf_op jit(solution)/shard_map/ppermute | solution.py:494
  140.2 0.7 collective-permute-start.26
  140.9 3.3 %collective-permute-start.27 = (bf16[768,128]{1,0:T(8,128)(2,1)S(1)}, bf16[768,128]{1,0:T(8,128)(2,1)S(1)}, u32[]{:S(2)}, u32[]{:S(2)}) collective-permute-start(bf16[768,128]{1,0:T(8,128)(2,1)S(1)} %get-tuple-element.86), channel_id=1, source_target_pairs={{0,3},{1,22},{8,11},{9,30},{16,19},{17,6},{24,27},{25,14},{32,35},... | collective-permute-start | bytes 589832 | tf_op jit(solution)/shard_map/ppermute | solution.py:494
  144.2 2.7 %collective-permute-done.24 = bf16[768,128]{1,0:T(8,128)(2,1)S(1)} collective-permute-done((bf16[768,128]{1,0:T(8,128)(2,1)S(1)}, bf16[768,128]{1,0:T(8,128)(2,1)S(1)}, u32[]{:S(2)}, u32[]{:S(2)}) %collective-permute-start.24) | collective-permute-done | bytes 196640 | tf_op jit(solution)/shard_map/ppermute | solution.py:494
  146.9 5.6 %collective-permute-done.26 = bf16[768,128]{1,0:T(8,128)(2,1)S(1)} collective-permute-done((bf16[768,128]{1,0:T(8,128)(2,1)S(1)}, bf16[768,128]{1,0:T(8,128)(2,1)S(1)}, u32[]{:S(2)}, u32[]{:S(2)}) %collective-permute-start.26) | collective-permute-done | bytes 196640 | tf_op jit(solution)/shard_map/ppermute | solution.py:494
  152.5 1.2 collective-permute-done.27
  153.8 0.7 pad_maximum_fusion.5
  154.5 0.7 add_convert_fusion.6
  (84 shorter events, 3.7 us)
Async XLA Ops:
  0.6 1.0 copy-start
  1.7 0.7 copy-start.3
  4.7 15.1 %collective-permute-start = (bf16[2048,128]{1,0:T(8,128)(2,1)S(1)}, bf16[2048,128]{1,0:T(8,128)(2,1)S(1)}, u32[]{:S(2)}, u32[]{:S(2)}) collective-permute-start(bf16[2048,128]{1,0:T(8,128)(2,1)S(1)} %shard_map.121), channel_id=1, source_target_pairs={{0,0},{23,1},{8,8},{31,9},{16,16},{7,17},{24,24},{15,25},{32,32},{... | collective-permute-start | bytes 1572872 | tf_op jit(solution)/shard_map/ppermute | solution.py:494
  19.8 13.1 %collective-permute-start.2 = (bf16[2048,128]{1,0:T(8,128)(2,1)S(1)}, bf16[2048,128]{1,0:T(8,128)(2,1)S(1)}, u32[]{:S(2)}, u32[]{:S(2)}) collective-permute-start(bf16[2048,128]{1,0:T(8,128)(2,1)S(1)} %collective-permute-done.refs_0_), channel_id=1, source_target_pairs={{0,32},{1,33},{8,40},{9,41},{16,48},{17,49},{24,56},{25,57},{32,64... | collective-permute-start | bytes 1572872 | tf_op jit(solution)/shard_map/ppermute | solution.py:494
  21.1 11.8 %collective-permute-start.1 = (bf16[2048,128]{1,0:T(8,128)(2,1)S(1)}, bf16[2048,128]{1,0:T(8,128)(2,1)S(1)}, u32[]{:S(2)}, u32[]{:S(2)}) collective-permute-start(bf16[2048,128]{1,0:T(8,128)(2,1)S(1)} %collective-permute-done.refs_0_), channel_id=1, source_target_pairs={{0,96},{1,97},{8,104},{9,105},{16,112},{17,113},{24,120},{25,121},... | collective-permute-start | bytes 1572872 | tf_op jit(solution)/shard_map/ppermute | solution.py:494
  24.3 8.6 %collective-permute-start.3 = (bf16[2048,128]{1,0:T(8,128)(2,1)S(1)}, bf16[2048,128]{1,0:T(8,128)(2,1)S(1)}, u32[]{:S(2)}, u32[]{:S(2)}) collective-permute-start(bf16[2048,128]{1,0:T(8,128)(2,1)S(1)} %collective-permute-done.refs_0_), channel_id=1, source_target_pairs={{0,7},{1,4},{8,15},{9,12},{16,23},{17,20},{24,31},{25,28},{32,39},... | collective-permute-start | bytes 1572872 | tf_op jit(solution)/shard_map/ppermute | solution.py:494
  33.0 9.3 %collective-permute-start.8 = (bf16[1024,128]{1,0:T(8,128)(2,1)S(1)}, bf16[1024,128]{1,0:T(8,128)(2,1)S(1)}, u32[]{:S(2)}, u32[]{:S(2)}) collective-permute-start(bf16[1024,128]{1,0:T(8,128)(2,1)S(1)} %slice.149), channel_id=1, source_target_pairs={{0,32},{1,33},{8,40},{9,41},{16,48},{17,49},{24,56},{25,57},{32,64... | collective-permute-start | bytes 786440 | tf_op jit(solution)/shard_map/ppermute | solution.py:494
  33.1 9.9 %collective-permute-start.6 = (bf16[1024,128]{1,0:T(8,128)(2,1)S(1)}, bf16[1024,128]{1,0:T(8,128)(2,1)S(1)}, u32[]{:S(2)}, u32[]{:S(2)}) collective-permute-start(bf16[1024,128]{1,0:T(8,128)(2,1)S(1)} %slice.148), channel_id=1, source_target_pairs={{0,96},{1,97},{8,104},{9,105},{16,112},{17,113},{24,120},{25,121},... | collective-permute-start | bytes 786440 | tf_op jit(solution)/shard_map/ppermute | solution.py:494
  35.8 15.4 %collective-permute-start.4 = (bf16[2048,128]{1,0:T(8,128)(2,1)S(1)}, bf16[2048,128]{1,0:T(8,128)(2,1)S(1)}, u32[]{:S(2)}, u32[]{:S(2)}) collective-permute-start(bf16[2048,128]{1,0:T(8,128)(2,1)S(1)} %collective-permute-done.1.refs_1_), channel_id=1, source_target_pairs={{0,7},{1,4},{8,15},{9,12},{16,23},{17,20},{24,31},{25,28},{32,39},... | collective-permute-start | bytes 1572872 | tf_op jit(solution)/shard_map/ppermute | solution.py:494
  36.4 14.9 %collective-permute-start.5 = (bf16[2048,128]{1,0:T(8,128)(2,1)S(1)}, bf16[2048,128]{1,0:T(8,128)(2,1)S(1)}, u32[]{:S(2)}, u32[]{:S(2)}) collective-permute-start(bf16[2048,128]{1,0:T(8,128)(2,1)S(1)} %collective-permute-done.2.refs_2_), channel_id=1, source_target_pairs={{0,7},{1,4},{8,15},{9,12},{16,23},{17,20},{24,31},{25,28},{32,39},... | collective-permute-start | bytes 1572872 | tf_op jit(solution)/shard_map/ppermute | solution.py:494
  42.3 10.8 %collective-permute-start.9 = (bf16[1024,128]{1,0:T(8,128)(2,1)S(1)}, bf16[1024,128]{1,0:T(8,128)(2,1)S(1)}, u32[]{:S(2)}, u32[]{:S(2)}) collective-permute-start(bf16[1024,128]{1,0:T(8,128)(2,1)S(1)} %collective-permute-done.8.refs_4_), channel_id=1, source_target_pairs={{0,7},{1,4},{8,15},{9,12},{16,23},{17,20},{24,31},{25,28},{32,39},... | collective-permute-start | bytes 786440 | tf_op jit(solution)/shard_map/ppermute | solution.py:494
  42.9 13.0 %collective-permute-start.7 = (bf16[1024,128]{1,0:T(8,128)(2,1)S(1)}, bf16[1024,128]{1,0:T(8,128)(2,1)S(1)}, u32[]{:S(2)}, u32[]{:S(2)}) collective-permute-start(bf16[1024,128]{1,0:T(8,128)(2,1)S(1)} %collective-permute-done.6.refs_3_), channel_id=1, source_target_pairs={{0,7},{1,4},{8,15},{9,12},{16,23},{17,20},{24,31},{25,28},{32,39},... | collective-permute-start | bytes 786440 | tf_op jit(solution)/shard_map/ppermute | solution.py:494
  59.2 12.2 %collective-permute-start.10 = (bf16[512,128]{1,0:T(8,128)(2,1)S(1)}, bf16[512,128]{1,0:T(8,128)(2,1)S(1)}, u32[]{:S(2)}, u32[]{:S(2)}) collective-permute-start(bf16[512,128]{1,0:T(8,128)(2,1)S(1)} %get-tuple-element.57), channel_id=1, source_target_pairs={{0,1},{1,2},{2,3},{3,0},{4,5},{5,6},{6,7},{7,4},{8,9},{9,10},{10,1... | collective-permute-start | bytes 393224 | tf_op jit(solution)/shard_map/ppermute | solution.py:509
  65.6 6.1 %collective-permute-start.11 = (bf16[512,128]{1,0:T(8,128)(2,1)S(1)}, bf16[512,128]{1,0:T(8,128)(2,1)S(1)}, u32[]{:S(2)}, u32[]{:S(2)}) collective-permute-start(bf16[512,128]{1,0:T(8,128)(2,1)S(1)} %get-tuple-element.60), channel_id=1, source_target_pairs={{0,2},{1,3},{2,0},{3,1},{4,6},{5,7},{6,4},{7,5},{8,10},{9,11},{10,... | collective-permute-start | bytes 393224 | tf_op jit(solution)/shard_map/ppermute | solution.py:509
  66.0 6.5 %collective-permute-start.12 = (bf16[512,128]{1,0:T(8,128)(2,1)S(1)}, bf16[512,128]{1,0:T(8,128)(2,1)S(1)}, u32[]{:S(2)}, u32[]{:S(2)}) collective-permute-start(bf16[512,128]{1,0:T(8,128)(2,1)S(1)} %get-tuple-element.61), channel_id=1, source_target_pairs={{0,3},{1,0},{2,1},{3,2},{4,7},{5,4},{6,5},{7,6},{8,11},{9,8},{10,9... | collective-permute-start | bytes 393224 | tf_op jit(solution)/shard_map/ppermute | solution.py:509
  66.7 5.8 %copy-start.1 = (bf16[512,256]{1,0:T(8,128)(2,1)S(1)}, bf16[512,256]{1,0:T(8,128)(2,1)}, u32[]{:S(2)}) copy-start(bf16[512,256]{1,0:T(8,128)(2,1)} %refs_5_.1) | copy-start | bytes 786436
  66.7 5.8 %copy-start.2 = (bf16[128,256]{1,0:T(8,128)(2,1)S(1)}, bf16[128,256]{1,0:T(8,128)(2,1)}, u32[]{:S(2)}) copy-start(bf16[128,256]{1,0:T(8,128)(2,1)} %refs_4_.1) | copy-start | bytes 196612
  73.6 10.8 %collective-permute-start.15 = (bf16[768,128]{1,0:T(8,128)(2,1)S(1)}, bf16[768,128]{1,0:T(8,128)(2,1)S(1)}, u32[]{:S(2)}, u32[]{:S(2)}) collective-permute-start(bf16[768,128]{1,0:T(8,128)(2,1)S(1)} %get-tuple-element.69.refs_0_), channel_id=1, source_target_pairs={{0,3},{1,0},{2,1},{3,2},{4,7},{5,4},{6,5},{7,6},{8,11},{9,8},{10,9... | collective-permute-start | bytes 589832 | tf_op jit(solution)/shard_map/ppermute | solution.py:509
  74.7 9.7 %collective-permute-start.14 = (bf16[768,128]{1,0:T(8,128)(2,1)S(1)}, bf16[768,128]{1,0:T(8,128)(2,1)S(1)}, u32[]{:S(2)}, u32[]{:S(2)}) collective-permute-start(bf16[768,128]{1,0:T(8,128)(2,1)S(1)} %get-tuple-element.69.refs_0_), channel_id=1, source_target_pairs={{0,2},{1,3},{2,0},{3,1},{4,6},{5,7},{6,4},{7,5},{8,10},{9,11},{10,... | collective-permute-start | bytes 589832 | tf_op jit(solution)/shard_map/ppermute | solution.py:509
  76.2 8.5 %collective-permute-start.13 = (bf16[768,128]{1,0:T(8,128)(2,1)S(1)}, bf16[768,128]{1,0:T(8,128)(2,1)S(1)}, u32[]{:S(2)}, u32[]{:S(2)}) collective-permute-start(bf16[768,128]{1,0:T(8,128)(2,1)S(1)} %get-tuple-element.69.refs_0_), channel_id=1, source_target_pairs={{0,1},{1,2},{2,3},{3,0},{4,5},{5,6},{6,7},{7,4},{8,9},{9,10},{10,1... | collective-permute-start | bytes 589832 | tf_op jit(solution)/shard_map/ppermute | solution.py:509
  88.4 15.5 %collective-permute-start.16 = (bf16[2304,128]{1,0:T(8,128)(2,1)S(1)}, bf16[2304,128]{1,0:T(8,128)(2,1)S(1)}, u32[]{:S(2)}, u32[]{:S(2)}) collective-permute-start(bf16[2304,128]{1,0:T(8,128)(2,1)S(1)} %get-tuple-element.74), channel_id=1, source_target_pairs={{0,7},{1,4},{8,15},{9,12},{16,23},{17,20},{24,31},{25,28},{32,39},... | collective-permute-start | bytes 1769480 | tf_op jit(solution)/shard_map/ppermute | solution.py:494
  96.1 19.1 %collective-permute-start.21 = (bf16[4096,128]{1,0:T(8,128)(2,1)S(1)}, bf16[4096,128]{1,0:T(8,128)(2,1)S(1)}, u32[]{:S(2)}, u32[]{:S(2)}) collective-permute-start(bf16[4096,128]{1,0:T(8,128)(2,1)S(1)} %get-tuple-element.79), channel_id=1, source_target_pairs={{0,7},{1,4},{8,15},{9,12},{16,23},{17,20},{24,31},{25,28},{32,39},... | collective-permute-start | bytes 3145736 | tf_op jit(solution)/shard_map/ppermute | solution.py:494
  104.2 8.8 %collective-permute-start.18 = (bf16[1280,128]{1,0:T(8,128)(2,1)S(1)}, bf16[1280,128]{1,0:T(8,128)(2,1)S(1)}, u32[]{:S(2)}, u32[]{:S(2)}) collective-permute-start(bf16[1280,128]{1,0:T(8,128)(2,1)S(1)} %get-tuple-element.101), channel_id=1, source_target_pairs={{0,96},{1,97},{8,104},{9,105},{16,112},{17,113},{24,120},{25,121},... | collective-permute-start | bytes 983048 | tf_op jit(solution)/shard_map/ppermute | solution.py:494
  104.6 9.2 %collective-permute-start.17 = (bf16[1280,128]{1,0:T(8,128)(2,1)S(1)}, bf16[1280,128]{1,0:T(8,128)(2,1)S(1)}, u32[]{:S(2)}, u32[]{:S(2)}) collective-permute-start(bf16[1280,128]{1,0:T(8,128)(2,1)S(1)} %get-tuple-element.102), channel_id=1, source_target_pairs={{0,32},{1,33},{8,40},{9,41},{16,48},{17,49},{24,56},{25,57},{32,64... | collective-permute-start | bytes 983048 | tf_op jit(solution)/shard_map/ppermute | solution.py:494
  115.5 5.8 %copy-start.4 = (s32[1,2048]{1,0:T(1,128)S(1)}, s32[1,2048]{1,0:T(1,128)}, u32[]{:S(2)}) copy-start(s32[1,2048]{1,0:T(1,128)} %order_ref.1) | copy-start | bytes 24580
  115.6 15.4 %collective-permute-start.22 = (bf16[2304,128]{1,0:T(8,128)(2,1)S(1)}, bf16[2304,128]{1,0:T(8,128)(2,1)S(1)}, u32[]{:S(2)}, u32[]{:S(2)}) collective-permute-start(bf16[2304,128]{1,0:T(8,128)(2,1)S(1)} %pad_maximum_fusion), channel_id=1, source_target_pairs={{0,32},{1,33},{8,40},{9,41},{16,48},{17,49},{24,56},{25,57},{32,64... | collective-permute-start | bytes 1769480 | tf_op jit(solution)/shard_map/ppermute | solution.py:494
  117.1 13.8 %collective-permute-start.20 = (bf16[2048,128]{1,0:T(8,128)(2,1)S(1)}, bf16[2048,128]{1,0:T(8,128)(2,1)S(1)}, u32[]{:S(2)}, u32[]{:S(2)}) collective-permute-start(bf16[2048,128]{1,0:T(8,128)(2,1)S(1)} %get-tuple-element.77), channel_id=1, source_target_pairs={{0,7},{1,4},{8,15},{9,12},{16,23},{17,20},{24,31},{25,28},{32,39},... | collective-permute-start | bytes 1572872 | tf_op jit(solution)/shard_map/ppermute | solution.py:494
  119.2 12.8 %collective-permute-start.23 = (bf16[2048,128]{1,0:T(8,128)(2,1)S(1)}, bf16[2048,128]{1,0:T(8,128)(2,1)S(1)}, u32[]{:S(2)}, u32[]{:S(2)}) collective-permute-start(bf16[2048,128]{1,0:T(8,128)(2,1)S(1)} %pad_maximum_fusion.2), channel_id=1, source_target_pairs={{0,96},{1,97},{8,104},{9,105},{16,112},{17,113},{24,120},{25,121},... | collective-permute-start | bytes 1572872 | tf_op jit(solution)/shard_map/ppermute | solution.py:494
  121.4 11.0 %collective-permute-start.19 = (s32[1,2048]{1,0:T(1,128)S(1)}, s32[1,2048]{1,0:T(1,128)S(1)}, u32[]{:S(2)}, u32[]{:S(2)}) collective-permute-start(s32[1,2048]{1,0:T(1,128)S(1)} %copy-done.4), channel_id=1, source_target_pairs={{0,0},{23,1},{8,8},{31,9},{16,16},{7,17},{24,24},{15,25},{32,32},{... | collective-permute-start | bytes 24584 | tf_op jit(solution)/shard_map/ppermute | solution.py:494
  135.5 11.4 %collective-permute-start.24 = (bf16[768,128]{1,0:T(8,128)(2,1)S(1)}, bf16[768,128]{1,0:T(8,128)(2,1)S(1)}, u32[]{:S(2)}, u32[]{:S(2)}) collective-permute-start(bf16[768,128]{1,0:T(8,128)(2,1)S(1)} %get-tuple-element.83), channel_id=1, source_target_pairs={{0,0},{1,23},{8,8},{9,31},{16,16},{17,7},{24,24},{25,15},{32,32},{... | collective-permute-start | bytes 589832 | tf_op jit(solution)/shard_map/ppermute | solution.py:494
  140.1 6.8 %collective-permute-start.25 = (bf16[768,128]{1,0:T(8,128)(2,1)S(1)}, bf16[768,128]{1,0:T(8,128)(2,1)S(1)}, u32[]{:S(2)}, u32[]{:S(2)}) collective-permute-start(bf16[768,128]{1,0:T(8,128)(2,1)S(1)} %get-tuple-element.84), channel_id=1, source_target_pairs={{0,1},{1,20},{8,9},{9,28},{16,17},{17,4},{24,25},{25,12},{32,33},{... | collective-permute-start | bytes 589832 | tf_op jit(solution)/shard_map/ppermute | solution.py:494
  140.2 12.3 %collective-permute-start.26 = (bf16[768,128]{1,0:T(8,128)(2,1)S(1)}, bf16[768,128]{1,0:T(8,128)(2,1)S(1)}, u32[]{:S(2)}, u32[]{:S(2)}) collective-permute-start(bf16[768,128]{1,0:T(8,128)(2,1)S(1)} %get-tuple-element.85), channel_id=1, source_target_pairs={{0,2},{1,21},{8,10},{9,29},{16,18},{17,5},{24,26},{25,13},{32,34},... | collective-permute-start | bytes 589832 | tf_op jit(solution)/shard_map/ppermute | solution.py:494
  140.9 12.9 %collective-permute-start.27 = (bf16[768,128]{1,0:T(8,128)(2,1)S(1)}, bf16[768,128]{1,0:T(8,128)(2,1)S(1)}, u32[]{:S(2)}, u32[]{:S(2)}) collective-permute-start(bf16[768,128]{1,0:T(8,128)(2,1)S(1)} %get-tuple-element.86), channel_id=1, source_target_pairs={{0,3},{1,22},{8,11},{9,30},{16,19},{17,6},{24,27},{25,14},{32,35},... | collective-permute-start | bytes 589832 | tf_op jit(solution)/shard_map/ppermute | solution.py:494

commit v7 on v6

--- a/solution.py
+++ b/solution.py
@@ -265,7 +265,7 @@
         own = out_refs[0].shape[0]
         here = list_ref[ends + lists]
         for shift, out_ref in enumerate(out_refs):
-            start = pl.multiple_of((here + shift) % reps * own, own)
+            start = pl.multiple_of((here ^ shift) * own, own)
             out_ref[...] = total_ref[pl.ds(start, own), :]
 
 
@@ -370,7 +370,7 @@
     place = ends + lists
     here = list_ref[place]
     for shift, pay_ref in enumerate(pay_refs):
-        start = pl.multiple_of((here + reps - shift) % reps * own, own)
+        start = pl.multiple_of((here ^ shift) * own, own)
         back_ref[pl.ds(start, own), :] = pay_ref[:own, :]
     back_ref[rows:, :] = jnp.zeros((TILE, TILE), jnp.bfloat16)
     total_ref[...] = jnp.zeros_like(total_ref)
@@ -505,7 +505,7 @@
     def to_reps(values):
         received = [values[0]]
         for shift in range(1, reps):
-            along = [(rep, (rep + shift) % reps) for rep in range(reps)]
+            along = [(rep, rep ^ shift) for rep in range(reps)]
             received.append(lax.ppermute(values[shift], "rep", along))
         return received
 

time: 155 us -> 157 us (1.013)
  waiting for transfers between devices: 49.9 us -> 53 us
  starting transfers between devices: 53.4 us -> 51 us
    ppermute x6, waiting for transfers between devices: 1.37 us -> 6.89 us  [to_reps(): received.append(lax.ppermute(values[shift], 'rep', along))]
    ppermute x6, starting transfers between devices: 13.7 us -> 10.8 us  [to_reps(): received.append(lax.ppermute(values[shift], 'rep', along))]
    ppermute x22, waiting for transfers between devices: 48.6 us -> 46.1 us  [moved(): return lax.ppermute(value, both, listed)]
where the time goes in v7:
time: 157 us; the launch traced here: 156 us
  waiting for transfers between devices  53 us (34%)
  starting transfers between devices  51 us (32%)
  Pallas kernels  38.2 us (24%)
  other arithmetic  7.33 us (5%)
  local copies, waits for them, and re-layouts  5.25 us (3%)
    ppermute x22, waiting for transfers between devices, moved(): return lax.ppermute(value, both, listed)  46.1 us
    ppermute x22, starting transfers between devices, moved(): return lax.ppermute(value, both, listed)  40.2 us
    pallas_call x3, Pallas kernels, hold(): pl.pallas_call(functools.partial(hold_kernel, items), out_shape=jax.Shape...  14 us
    ppermute x6, starting transfers between devices, to_reps(): received.append(lax.ppermute(values[shift], 'rep', along))  10.8 us
    pallas_call x2, Pallas kernels, forward_product(): pl.pallas_call(functools.partial(forward_kernel, len(xs), lists, wave, ca...  9.87 us
    pallas_call x2, Pallas kernels, backward_product(): pl.pallas_call(functools.partial(backward_kernel, sizes, rows, lists, fir...  7.84 us
    ppermute x6, waiting for transfers between devices, to_reps(): received.append(lax.ppermute(values[shift], 'rep', along))  6.89 us
  transfers between devices with their start and end apart: 28, of which 16 were waited for; matrix products, arithmetic and copies ran while one was open for 6% of the time, Pallas kernels for 16%

profile of v7, /device:TPU:1, one launch (start us, length us, event | category | flops | bytes accessed | tf_op | source)
XLA Modules:
  0.0 155.9 jit_solution(2205082109300030504)
XLA Ops:
  0.6 1.0 copy-done
  1.7 0.7 copy-done.3
  2.4 2.4 %shard_map.121 = bf16[2048,128]{1,0:T(8,128)(2,1)S(1)} custom-call(s32[1,2048]{1,0:T(1,128)S(1)} %copy-done.3, bf16[2048,128]{1,0:T(8,128)(2,1)S(1)} %copy-done), custom_call_target="tpu_custom_call" | custom-call | tf_op jit(solution)/shard_map/pallas_call | solution.py:123
  4.7 5.3 %collective-permute-start = (bf16[2048,128]{1,0:T(8,128)(2,1)S(1)}, bf16[2048,128]{1,0:T(8,128)(2,1)S(1)}, u32[]{:S(2)}, u32[]{:S(2)}) collective-permute-start(bf16[2048,128]{1,0:T(8,128)(2,1)S(1)} %shard_map.121), channel_id=1, source_target_pairs={{0,0},{23,1},{8,8},{31,9},{16,16},{7,17},{24,24},{15,25},{32,32},{... | collective-permute-start | bytes 1572872 | tf_op jit(solution)/shard_map/ppermute | solution.py:494
  10.1 0.7 compare_and_fusion
  10.8 0.7 fusion.14
  11.5 0.8 bitcast_select_fusion
  12.3 0.6 gather_fusion
  13.8 0.4 convert_reduce_fusion
  14.2 5.6 %collective-permute-done.refs_0_ = bf16[2048,128]{1,0:T(8,128)(2,1)S(1)} collective-permute-done((bf16[2048,128]{1,0:T(8,128)(2,1)S(1)}, bf16[2048,128]{1,0:T(8,128)(2,1)S(1)}, u32[]{:S(2)}, u32[]{:S(2)}) %collective-permute-start) | collective-permute-done | bytes 524320 | tf_op jit(solution)/shard_map/ppermute | solution.py:494
  19.8 1.3 collective-permute-start.2
  21.1 1.5 collective-permute-start.1
  22.9 0.4 convert_reduce_fusion.1
  23.9 0.3 select_reduce_fusion.3
  24.9 0.7 fusion.15
  25.7 7.2 %collective-permute-done.3.refs_0_ = bf16[2048,128]{1,0:T(8,128)(2,1)S(1)} collective-permute-done((bf16[2048,128]{1,0:T(8,128)(2,1)S(1)}, bf16[2048,128]{1,0:T(8,128)(2,1)S(1)}, u32[]{:S(2)}, u32[]{:S(2)}) %collective-permute-start.3) | collective-permute-done | bytes 524320 | tf_op jit(solution)/shard_map/ppermute | solution.py:494
  33.1 2.7 %collective-permute-start.6 = (bf16[1024,128]{1,0:T(8,128)(2,1)S(1)}, bf16[1024,128]{1,0:T(8,128)(2,1)S(1)}, u32[]{:S(2)}, u32[]{:S(2)}) collective-permute-start(bf16[1024,128]{1,0:T(8,128)(2,1)S(1)} %slice.148), channel_id=1, source_target_pairs={{0,96},{1,97},{8,104},{9,105},{16,112},{17,113},{24,120},{25,121},... | collective-permute-start | bytes 786440 | tf_op jit(solution)/shard_map/ppermute | solution.py:494
  35.8 0.6 collective-permute-start.4
  36.4 1.2 collective-permute-start.5
  37.6 4.7 %shard_map.122.hold_ref = bf16[320,128,128]{2,1,0:T(8,128)(2,1)S(1)} custom-call(s32[9]{0:T(128)S(1)} %pad_add_fusion.place_ref, bf16[640,128,128]{2,1,0:T(8,128)(2,1)} %bitcast.14), custom_call_target="tpu_custom_call" | custom-call | bytes 20971520 | tf_op jit(solution)/shard_map/pallas_call | solution.py:160
  42.3 0.6 collective-permute-start.9
  42.9 1.2 collective-permute-start.7
  44.1 6.6 %shard_map.123.refs_5_ = f32[2176,128]{1,0:T(8,128)S(1)} custom-call(s32[971]{0:T(1024)S(1)} %concatenate.46.list_ref, bf16[640,128,128]{2,1,0:T(8,128)(2,1)} %bitcast.15, bf16[2048,128]{1,0:T(8,128)(2,1)S(1)} %collective-permute-done.refs_0_, bf16[2048,128]{1,0:T(8,128)(2,1)S(1)} %collective-permute-done.1.refs_1_, ...), custom_call_target="tpu_custom_call" | custom-call | flops 5368709120 | bytes 10485760 | tf_op jit(solution)/shard_map/pallas_call | solution.py:302
  50.8 2.4 %collective-permute-done.9.refs_4_ = bf16[1024,128]{1,0:T(8,128)(2,1)S(1)} collective-permute-done((bf16[1024,128]{1,0:T(8,128)(2,1)S(1)}, bf16[1024,128]{1,0:T(8,128)(2,1)S(1)}, u32[]{:S(2)}, u32[]{:S(2)}) %collective-permute-start.9) | collective-permute-done | bytes 262176 | tf_op jit(solution)/shard_map/ppermute | solution.py:494
  53.1 2.8 %collective-permute-done.7.refs_3_ = bf16[1024,128]{1,0:T(8,128)(2,1)S(1)} collective-permute-done((bf16[1024,128]{1,0:T(8,128)(2,1)S(1)}, bf16[1024,128]{1,0:T(8,128)(2,1)S(1)}, u32[]{:S(2)}, u32[]{:S(2)}) %collective-permute-start.7) | collective-permute-done | bytes 262176 | tf_op jit(solution)/shard_map/ppermute | solution.py:494
  55.9 3.3 %shard_map.124 = (bf16[512,128]{1,0:T(8,128)(2,1)S(1)}, bf16[512,128]{1,0:T(8,128)(2,1)S(1)}, bf16[512,128]{1,0:T(8,128)(2,1)S(1)}, bf16[512,128]{1,0:T(8,128)(2,1)S(1)}) custom-call(s32[971]{0:T(1024)S(1)} %concatenate.46.list_ref, bf16[320,128,128]{2,1,0:T(8,128)(2,1)S(1)} %shard_map.122.hold_ref, bf16[2048,128]{1,0:T(8,128)(2,1)S(1)} %collective-permute-done.3.refs_0_, ...), custom_call_target="tpu_custom_call" | custom-call | flops 5368709120 | bytes 10485760 | tf_op jit(solution)/shard_map/pallas_call | solution.py:302
  59.2 0.8 collective-permute-start.10
  60.0 6.1 %collective-permute-start.11 = (bf16[512,128]{1,0:T(8,128)(2,1)S(1)}, bf16[512,128]{1,0:T(8,128)(2,1)S(1)}, u32[]{:S(2)}, u32[]{:S(2)}) collective-permute-start(bf16[512,128]{1,0:T(8,128)(2,1)S(1)} %get-tuple-element.60), channel_id=1, source_target_pairs={{0,2},{1,3},{2,0},{3,1},{4,6},{5,7},{6,4},{7,5},{8,10},{9,11},{10,... | collective-permute-start | bytes 393224 | tf_op jit(solution)/shard_map/ppermute | solution.py:509
  66.0 0.3 collective-permute-start.12
  66.4 4.7 %shard_map.125.hold_ref = bf16[320,128,128]{2,1,0:T(8,128)(2,1)S(1)} custom-call(s32[9]{0:T(128)S(1)} %pad_add_fusion.place_ref, bf16[640,128,128]{2,1,0:T(8,128)(2,1)} %bitcast.16), custom_call_target="tpu_custom_call" | custom-call | bytes 20971520 | tf_op jit(solution)/shard_map/pallas_call | solution.py:160
  71.1 2.6 %collective-permute-done.12.refs_3_ = bf16[512,128]{1,0:T(8,128)(2,1)S(1)} collective-permute-done((bf16[512,128]{1,0:T(8,128)(2,1)S(1)}, bf16[512,128]{1,0:T(8,128)(2,1)S(1)}, u32[]{:S(2)}, u32[]{:S(2)}) %collective-permute-start.12) | collective-permute-done | bytes 131104 | tf_op jit(solution)/shard_map/ppermute | solution.py:509
  73.6 1.0 shard_map.126
  74.7 1.7 %collective-permute-start.15 = (bf16[768,128]{1,0:T(8,128)(2,1)S(1)}, bf16[768,128]{1,0:T(8,128)(2,1)S(1)}, u32[]{:S(2)}, u32[]{:S(2)}) collective-permute-start(bf16[768,128]{1,0:T(8,128)(2,1)S(1)} %get-tuple-element.69.refs_0_), channel_id=1, source_target_pairs={{0,3},{1,2},{2,1},{3,0},{4,7},{5,6},{6,5},{7,4},{8,11},{9,10},{10,... | collective-permute-start | bytes 589832 | tf_op jit(solution)/shard_map/ppermute | solution.py:509
  76.3 1.6 %collective-permute-start.14 = (bf16[768,128]{1,0:T(8,128)(2,1)S(1)}, bf16[768,128]{1,0:T(8,128)(2,1)S(1)}, u32[]{:S(2)}, u32[]{:S(2)}) collective-permute-start(bf16[768,128]{1,0:T(8,128)(2,1)S(1)} %get-tuple-element.69.refs_0_), channel_id=1, source_target_pairs={{0,2},{1,3},{2,0},{3,1},{4,6},{5,7},{6,4},{7,5},{8,10},{9,11},{10,... | collective-permute-start | bytes 589832 | tf_op jit(solution)/shard_map/ppermute | solution.py:509
  78.0 0.4 collective-permute-start.13
  78.3 4.7 %shard_map.127.hold_ref = bf16[320,128,128]{2,1,0:T(8,128)(2,1)S(1)} custom-call(s32[9]{0:T(128)S(1)} %pad_add_fusion.place_ref, bf16[640,128,128]{2,1,0:T(8,128)(2,1)} %bitcast.17), custom_call_target="tpu_custom_call" | custom-call | bytes 20971520 | tf_op jit(solution)/shard_map/pallas_call | solution.py:160
  83.0 0.4 collective-permute-done.15.refs_3_
  83.4 3.9 %collective-permute-done.14.refs_2_ = bf16[768,128]{1,0:T(8,128)(2,1)S(1)} collective-permute-done((bf16[768,128]{1,0:T(8,128)(2,1)S(1)}, bf16[768,128]{1,0:T(8,128)(2,1)S(1)}, u32[]{:S(2)}, u32[]{:S(2)}) %collective-permute-start.14) | collective-permute-done | bytes 196640 | tf_op jit(solution)/shard_map/ppermute | solution.py:509
  87.3 4.2 %shard_map.128 = (bf16[2304,128]{1,0:T(8,128)(2,1)S(1)}, bf16[4096,128]{1,0:T(8,128)(2,1)S(1)}, bf16[2048,128]{1,0:T(8,128)(2,1)S(1)}) custom-call(s32[1157]{0:T(1024)S(1)} %concatenate.43.list_ref, bf16[320,128,128]{2,1,0:T(8,128)(2,1)S(1)} %shard_map.125.hold_ref, bf16[768,128]{1,0:T(8,128)(2,1)S(1)} %get-tuple-element.69.refs_0_, ...), custom_call_target="tpu_custom_call" | custom-call | flops 5368709120 | bytes 10485760 | tf_op jit(solution)/shard_map/pallas_call | solution.py:415
  91.6 1.1 collective-permute-start.16
  92.7 0.7 collective-permute-start.21
  93.4 3.6 %shard_map.129 = (bf16[2048,128]{1,0:T(8,128)(2,1)S(1)}, bf16[2048,128]{1,0:T(8,128)(2,1)S(1)}, bf16[2048,128]{1,0:T(8,128)(2,1)S(1)}, bf16[2048,128]{1,0:T(8,128)(2,1)S(1)}) custom-call(s32[1157]{0:T(1024)S(1)} %concatenate.43.list_ref, bf16[320,128,128]{2,1,0:T(8,128)(2,1)S(1)} %shard_map.127.hold_ref, bf16[768,128]{1,0:T(8,128)(2,1)S(1)} %get-tuple-element.69.refs_0_, ...), custom_call_target="tpu_custom_call" | custom-call | flops 5368709120 | bytes 10485760 | tf_op jit(solution)/shard_map/pallas_call | solution.py:415
  97.0 4.3 %collective-permute-done.16 = bf16[2304,128]{1,0:T(8,128)(2,1)S(1)} collective-permute-done((bf16[2304,128]{1,0:T(8,128)(2,1)S(1)}, bf16[2304,128]{1,0:T(8,128)(2,1)S(1)}, u32[]{:S(2)}, u32[]{:S(2)}) %collective-permute-start.16) | collective-permute-done | bytes 589856 | tf_op jit(solution)/shard_map/ppermute | solution.py:494
  101.5 0.9 collective-permute-start.18
  102.4 0.7 collective-permute-start.17
  103.1 6.1 %collective-permute-done.18 = bf16[1280,128]{1,0:T(8,128)(2,1)S(1)} collective-permute-done((bf16[1280,128]{1,0:T(8,128)(2,1)S(1)}, bf16[1280,128]{1,0:T(8,128)(2,1)S(1)}, u32[]{:S(2)}, u32[]{:S(2)}) %collective-permute-start.18) | collective-permute-done | bytes 327712 | tf_op jit(solution)/shard_map/ppermute | solution.py:494
  109.2 0.6 collective-permute-done.17
  109.8 2.7 %collective-permute-done.21 = bf16[4096,128]{1,0:T(8,128)(2,1)S(1)} collective-permute-done((bf16[4096,128]{1,0:T(8,128)(2,1)S(1)}, bf16[4096,128]{1,0:T(8,128)(2,1)S(1)}, u32[]{:S(2)}, u32[]{:S(2)}) %collective-permute-start.21) | collective-permute-done | bytes 1048608 | tf_op jit(solution)/shard_map/ppermute | solution.py:494
  112.5 0.3 add_convert_fusion.3
  113.0 2.4 %collective-permute-start.20 = (bf16[2048,128]{1,0:T(8,128)(2,1)S(1)}, bf16[2048,128]{1,0:T(8,128)(2,1)S(1)}, u32[]{:S(2)}, u32[]{:S(2)}) collective-permute-start(bf16[2048,128]{1,0:T(8,128)(2,1)S(1)} %get-tuple-element.77), channel_id=1, source_target_pairs={{0,7},{1,4},{8,15},{9,12},{16,23},{17,20},{24,31},{25,28},{32,39},... | collective-permute-start | bytes 1572872 | tf_op jit(solution)/shard_map/ppermute | solution.py:494
  115.4 2.4 %collective-permute-start.23 = (bf16[2048,128]{1,0:T(8,128)(2,1)S(1)}, bf16[2048,128]{1,0:T(8,128)(2,1)S(1)}, u32[]{:S(2)}, u32[]{:S(2)}) collective-permute-start(bf16[2048,128]{1,0:T(8,128)(2,1)S(1)} %pad_maximum_fusion.2), channel_id=1, source_target_pairs={{0,96},{1,97},{8,104},{9,105},{16,112},{17,113},{24,120},{25,121},... | collective-permute-start | bytes 1572872 | tf_op jit(solution)/shard_map/ppermute | solution.py:494
  117.8 1.2 constant_dynamic-slice_fusion
  119.0 4.5 %collective-permute-start.19 = (s32[1,2048]{1,0:T(1,128)S(1)}, s32[1,2048]{1,0:T(1,128)S(1)}, u32[]{:S(2)}, u32[]{:S(2)}) collective-permute-start(s32[1,2048]{1,0:T(1,128)S(1)} %copy-done.4), channel_id=1, source_target_pairs={{0,0},{23,1},{8,8},{31,9},{16,16},{7,17},{24,24},{15,25},{32,32},{... | collective-permute-start | bytes 24584 | tf_op jit(solution)/shard_map/ppermute | solution.py:494
  123.6 2.5 %collective-permute-done.22 = bf16[2304,128]{1,0:T(8,128)(2,1)S(1)} collective-permute-done((bf16[2304,128]{1,0:T(8,128)(2,1)S(1)}, bf16[2304,128]{1,0:T(8,128)(2,1)S(1)}, u32[]{:S(2)}, u32[]{:S(2)}) %collective-permute-start.22) | collective-permute-done | bytes 589856 | tf_op jit(solution)/shard_map/ppermute | solution.py:494
  126.1 0.8 collective-permute-done.23
  126.8 0.3 add_convert_fusion
  127.2 2.3 %collective-permute-done.19.order_ref = s32[1,2048]{1,0:T(1,128)S(1)} collective-permute-done((s32[1,2048]{1,0:T(1,128)S(1)}, s32[1,2048]{1,0:T(1,128)S(1)}, u32[]{:S(2)}, u32[]{:S(2)}) %collective-permute-start.19) | collective-permute-done | bytes 8224 | tf_op jit(solution)/shard_map/ppermute | solution.py:494
  129.4 3.1 %shard_map.130 = (bf16[768,128]{1,0:T(8,128)(2,1)S(1)}, bf16[768,128]{1,0:T(8,128)(2,1)S(1)}, bf16[768,128]{1,0:T(8,128)(2,1)S(1)}, bf16[768,128]{1,0:T(8,128)(2,1)S(1)}) custom-call(s32[1]{0:T(128)} %bitcast.7.place_ref, s32[1,2048]{1,0:T(1,128)S(1)} %collective-permute-done.19.order_ref, bf16[2304,128]{1,0:T(8,128)(2,1)S(1)} %pad_maximum_fusion.1.home_ref), custom_call_target="tpu_custom_call" | custom-call | tf_op jit(solution)/shard_map/pallas_call | solution.py:457
  132.6 8.2 %collective-permute-start.24 = (bf16[768,128]{1,0:T(8,128)(2,1)S(1)}, bf16[768,128]{1,0:T(8,128)(2,1)S(1)}, u32[]{:S(2)}, u32[]{:S(2)}) collective-permute-start(bf16[768,128]{1,0:T(8,128)(2,1)S(1)} %get-tuple-element.83), channel_id=1, source_target_pairs={{0,0},{1,23},{8,8},{9,31},{16,16},{17,7},{24,24},{25,15},{32,32},{... | collective-permute-start | bytes 589832 | tf_op jit(solution)/shard_map/ppermute | solution.py:494
  140.8 4.7 %collective-permute-start.26 = (bf16[768,128]{1,0:T(8,128)(2,1)S(1)}, bf16[768,128]{1,0:T(8,128)(2,1)S(1)}, u32[]{:S(2)}, u32[]{:S(2)}) collective-permute-start(bf16[768,128]{1,0:T(8,128)(2,1)S(1)} %get-tuple-element.85), channel_id=1, source_target_pairs={{0,2},{1,21},{8,10},{9,29},{16,18},{17,5},{24,26},{25,13},{32,34},... | collective-permute-start | bytes 589832 | tf_op jit(solution)/shard_map/ppermute | solution.py:494
  145.6 6.4 %collective-permute-done.26 = bf16[768,128]{1,0:T(8,128)(2,1)S(1)} collective-permute-done((bf16[768,128]{1,0:T(8,128)(2,1)S(1)}, bf16[768,128]{1,0:T(8,128)(2,1)S(1)}, u32[]{:S(2)}, u32[]{:S(2)}) %collective-permute-start.26) | collective-permute-done | bytes 196640 | tf_op jit(solution)/shard_map/ppermute | solution.py:494
  151.9 2.5 %collective-permute-done.27 = bf16[768,128]{1,0:T(8,128)(2,1)S(1)} collective-permute-done((bf16[768,128]{1,0:T(8,128)(2,1)S(1)}, bf16[768,128]{1,0:T(8,128)(2,1)S(1)}, u32[]{:S(2)}, u32[]{:S(2)}) %collective-permute-start.27) | collective-permute-done | bytes 196640 | tf_op jit(solution)/shard_map/ppermute | solution.py:494
  154.5 0.7 pad_maximum_fusion.5
  155.1 0.7 add_convert_fusion.6
  (84 shorter events, 3.5 us)
Async XLA Ops:
  0.6 1.0 copy-start
  1.7 0.7 copy-start.3
  4.7 15.1 %collective-permute-start = (bf16[2048,128]{1,0:T(8,128)(2,1)S(1)}, bf16[2048,128]{1,0:T(8,128)(2,1)S(1)}, u32[]{:S(2)}, u32[]{:S(2)}) collective-permute-start(bf16[2048,128]{1,0:T(8,128)(2,1)S(1)} %shard_map.121), channel_id=1, source_target_pairs={{0,0},{23,1},{8,8},{31,9},{16,16},{7,17},{24,24},{15,25},{32,32},{... | collective-permute-start | bytes 1572872 | tf_op jit(solution)/shard_map/ppermute | solution.py:494
  19.8 13.1 %collective-permute-start.2 = (bf16[2048,128]{1,0:T(8,128)(2,1)S(1)}, bf16[2048,128]{1,0:T(8,128)(2,1)S(1)}, u32[]{:S(2)}, u32[]{:S(2)}) collective-permute-start(bf16[2048,128]{1,0:T(8,128)(2,1)S(1)} %collective-permute-done.refs_0_), channel_id=1, source_target_pairs={{0,32},{1,33},{8,40},{9,41},{16,48},{17,49},{24,56},{25,57},{32,64... | collective-permute-start | bytes 1572872 | tf_op jit(solution)/shard_map/ppermute | solution.py:494
  21.1 11.8 %collective-permute-start.1 = (bf16[2048,128]{1,0:T(8,128)(2,1)S(1)}, bf16[2048,128]{1,0:T(8,128)(2,1)S(1)}, u32[]{:S(2)}, u32[]{:S(2)}) collective-permute-start(bf16[2048,128]{1,0:T(8,128)(2,1)S(1)} %collective-permute-done.refs_0_), channel_id=1, source_target_pairs={{0,96},{1,97},{8,104},{9,105},{16,112},{17,113},{24,120},{25,121},... | collective-permute-start | bytes 1572872 | tf_op jit(solution)/shard_map/ppermute | solution.py:494
  24.3 8.6 %collective-permute-start.3 = (bf16[2048,128]{1,0:T(8,128)(2,1)S(1)}, bf16[2048,128]{1,0:T(8,128)(2,1)S(1)}, u32[]{:S(2)}, u32[]{:S(2)}) collective-permute-start(bf16[2048,128]{1,0:T(8,128)(2,1)S(1)} %collective-permute-done.refs_0_), channel_id=1, source_target_pairs={{0,7},{1,4},{8,15},{9,12},{16,23},{17,20},{24,31},{25,28},{32,39},... | collective-permute-start | bytes 1572872 | tf_op jit(solution)/shard_map/ppermute | solution.py:494
  33.0 9.3 %collective-permute-start.8 = (bf16[1024,128]{1,0:T(8,128)(2,1)S(1)}, bf16[1024,128]{1,0:T(8,128)(2,1)S(1)}, u32[]{:S(2)}, u32[]{:S(2)}) collective-permute-start(bf16[1024,128]{1,0:T(8,128)(2,1)S(1)} %slice.149), channel_id=1, source_target_pairs={{0,32},{1,33},{8,40},{9,41},{16,48},{17,49},{24,56},{25,57},{32,64... | collective-permute-start | bytes 786440 | tf_op jit(solution)/shard_map/ppermute | solution.py:494
  33.1 9.9 %collective-permute-start.6 = (bf16[1024,128]{1,0:T(8,128)(2,1)S(1)}, bf16[1024,128]{1,0:T(8,128)(2,1)S(1)}, u32[]{:S(2)}, u32[]{:S(2)}) collective-permute-start(bf16[1024,128]{1,0:T(8,128)(2,1)S(1)} %slice.148), channel_id=1, source_target_pairs={{0,96},{1,97},{8,104},{9,105},{16,112},{17,113},{24,120},{25,121},... | collective-permute-start | bytes 786440 | tf_op jit(solution)/shard_map/ppermute | solution.py:494
  35.8 15.0 %collective-permute-start.4 = (bf16[2048,128]{1,0:T(8,128)(2,1)S(1)}, bf16[2048,128]{1,0:T(8,128)(2,1)S(1)}, u32[]{:S(2)}, u32[]{:S(2)}) collective-permute-start(bf16[2048,128]{1,0:T(8,128)(2,1)S(1)} %collective-permute-done.1.refs_1_), channel_id=1, source_target_pairs={{0,7},{1,4},{8,15},{9,12},{16,23},{17,20},{24,31},{25,28},{32,39},... | collective-permute-start | bytes 1572872 | tf_op jit(solution)/shard_map/ppermute | solution.py:494
  36.4 14.4 %collective-permute-start.5 = (bf16[2048,128]{1,0:T(8,128)(2,1)S(1)}, bf16[2048,128]{1,0:T(8,128)(2,1)S(1)}, u32[]{:S(2)}, u32[]{:S(2)}) collective-permute-start(bf16[2048,128]{1,0:T(8,128)(2,1)S(1)} %collective-permute-done.2.refs_2_), channel_id=1, source_target_pairs={{0,7},{1,4},{8,15},{9,12},{16,23},{17,20},{24,31},{25,28},{32,39},... | collective-permute-start | bytes 1572872 | tf_op jit(solution)/shard_map/ppermute | solution.py:494
  42.3 10.8 %collective-permute-start.9 = (bf16[1024,128]{1,0:T(8,128)(2,1)S(1)}, bf16[1024,128]{1,0:T(8,128)(2,1)S(1)}, u32[]{:S(2)}, u32[]{:S(2)}) collective-permute-start(bf16[1024,128]{1,0:T(8,128)(2,1)S(1)} %collective-permute-done.8.refs_4_), channel_id=1, source_target_pairs={{0,7},{1,4},{8,15},{9,12},{16,23},{17,20},{24,31},{25,28},{32,39},... | collective-permute-start | bytes 786440 | tf_op jit(solution)/shard_map/ppermute | solution.py:494
  42.9 13.0 %collective-permute-start.7 = (bf16[1024,128]{1,0:T(8,128)(2,1)S(1)}, bf16[1024,128]{1,0:T(8,128)(2,1)S(1)}, u32[]{:S(2)}, u32[]{:S(2)}) collective-permute-start(bf16[1024,128]{1,0:T(8,128)(2,1)S(1)} %collective-permute-done.6.refs_3_), channel_id=1, source_target_pairs={{0,7},{1,4},{8,15},{9,12},{16,23},{17,20},{24,31},{25,28},{32,39},... | collective-permute-start | bytes 786440 | tf_op jit(solution)/shard_map/ppermute | solution.py:494
  59.2 11.9 %collective-permute-start.10 = (bf16[512,128]{1,0:T(8,128)(2,1)S(1)}, bf16[512,128]{1,0:T(8,128)(2,1)S(1)}, u32[]{:S(2)}, u32[]{:S(2)}) collective-permute-start(bf16[512,128]{1,0:T(8,128)(2,1)S(1)} %get-tuple-element.57), channel_id=1, source_target_pairs={{0,1},{1,0},{2,3},{3,2},{4,5},{5,4},{6,7},{7,6},{8,9},{9,8},{10,11... | collective-permute-start | bytes 393224 | tf_op jit(solution)/shard_map/ppermute | solution.py:509
  60.0 11.1 %collective-permute-start.11 = (bf16[512,128]{1,0:T(8,128)(2,1)S(1)}, bf16[512,128]{1,0:T(8,128)(2,1)S(1)}, u32[]{:S(2)}, u32[]{:S(2)}) collective-permute-start(bf16[512,128]{1,0:T(8,128)(2,1)S(1)} %get-tuple-element.60), channel_id=1, source_target_pairs={{0,2},{1,3},{2,0},{3,1},{4,6},{5,7},{6,4},{7,5},{8,10},{9,11},{10,... | collective-permute-start | bytes 393224 | tf_op jit(solution)/shard_map/ppermute | solution.py:509
  66.0 7.6 %collective-permute-start.12 = (bf16[512,128]{1,0:T(8,128)(2,1)S(1)}, bf16[512,128]{1,0:T(8,128)(2,1)S(1)}, u32[]{:S(2)}, u32[]{:S(2)}) collective-permute-start(bf16[512,128]{1,0:T(8,128)(2,1)S(1)} %get-tuple-element.61), channel_id=1, source_target_pairs={{0,3},{1,2},{2,1},{3,0},{4,7},{5,6},{6,5},{7,4},{8,11},{9,10},{10,... | collective-permute-start | bytes 393224 | tf_op jit(solution)/shard_map/ppermute | solution.py:509
  66.4 7.3 %copy-start.1 = (bf16[512,256]{1,0:T(8,128)(2,1)S(1)}, bf16[512,256]{1,0:T(8,128)(2,1)}, u32[]{:S(2)}) copy-start(bf16[512,256]{1,0:T(8,128)(2,1)} %refs_5_.1) | copy-start | bytes 786436
  66.4 7.3 %copy-start.2 = (bf16[128,256]{1,0:T(8,128)(2,1)S(1)}, bf16[128,256]{1,0:T(8,128)(2,1)}, u32[]{:S(2)}) copy-start(bf16[128,256]{1,0:T(8,128)(2,1)} %refs_4_.1) | copy-start | bytes 196612
  74.7 8.7 %collective-permute-start.15 = (bf16[768,128]{1,0:T(8,128)(2,1)S(1)}, bf16[768,128]{1,0:T(8,128)(2,1)S(1)}, u32[]{:S(2)}, u32[]{:S(2)}) collective-permute-start(bf16[768,128]{1,0:T(8,128)(2,1)S(1)} %get-tuple-element.69.refs_0_), channel_id=1, source_target_pairs={{0,3},{1,2},{2,1},{3,0},{4,7},{5,6},{6,5},{7,4},{8,11},{9,10},{10,... | collective-permute-start | bytes 589832 | tf_op jit(solution)/shard_map/ppermute | solution.py:509
  76.3 11.0 %collective-permute-start.14 = (bf16[768,128]{1,0:T(8,128)(2,1)S(1)}, bf16[768,128]{1,0:T(8,128)(2,1)S(1)}, u32[]{:S(2)}, u32[]{:S(2)}) collective-permute-start(bf16[768,128]{1,0:T(8,128)(2,1)S(1)} %get-tuple-element.69.refs_0_), channel_id=1, source_target_pairs={{0,2},{1,3},{2,0},{3,1},{4,6},{5,7},{6,4},{7,5},{8,10},{9,11},{10,... | collective-permute-start | bytes 589832 | tf_op jit(solution)/shard_map/ppermute | solution.py:509
  78.0 9.4 %collective-permute-start.13 = (bf16[768,128]{1,0:T(8,128)(2,1)S(1)}, bf16[768,128]{1,0:T(8,128)(2,1)S(1)}, u32[]{:S(2)}, u32[]{:S(2)}) collective-permute-start(bf16[768,128]{1,0:T(8,128)(2,1)S(1)} %get-tuple-element.69.refs_0_), channel_id=1, source_target_pairs={{0,1},{1,0},{2,3},{3,2},{4,5},{5,4},{6,7},{7,6},{8,9},{9,8},{10,11... | collective-permute-start | bytes 589832 | tf_op jit(solution)/shard_map/ppermute | solution.py:509
  91.6 9.7 %collective-permute-start.16 = (bf16[2304,128]{1,0:T(8,128)(2,1)S(1)}, bf16[2304,128]{1,0:T(8,128)(2,1)S(1)}, u32[]{:S(2)}, u32[]{:S(2)}) collective-permute-start(bf16[2304,128]{1,0:T(8,128)(2,1)S(1)} %get-tuple-element.74), channel_id=1, source_target_pairs={{0,7},{1,4},{8,15},{9,12},{16,23},{17,20},{24,31},{25,28},{32,39},... | collective-permute-start | bytes 1769480 | tf_op jit(solution)/shard_map/ppermute | solution.py:494
  92.7 19.8 %collective-permute-start.21 = (bf16[4096,128]{1,0:T(8,128)(2,1)S(1)}, bf16[4096,128]{1,0:T(8,128)(2,1)S(1)}, u32[]{:S(2)}, u32[]{:S(2)}) collective-permute-start(bf16[4096,128]{1,0:T(8,128)(2,1)S(1)} %get-tuple-element.79), channel_id=1, source_target_pairs={{0,7},{1,4},{8,15},{9,12},{16,23},{17,20},{24,31},{25,28},{32,39},... | collective-permute-start | bytes 3145736 | tf_op jit(solution)/shard_map/ppermute | solution.py:494
  101.5 7.7 %collective-permute-start.18 = (bf16[1280,128]{1,0:T(8,128)(2,1)S(1)}, bf16[1280,128]{1,0:T(8,128)(2,1)S(1)}, u32[]{:S(2)}, u32[]{:S(2)}) collective-permute-start(bf16[1280,128]{1,0:T(8,128)(2,1)S(1)} %get-tuple-element.101), channel_id=1, source_target_pairs={{0,96},{1,97},{8,104},{9,105},{16,112},{17,113},{24,120},{25,121},... | collective-permute-start | bytes 983048 | tf_op jit(solution)/shard_map/ppermute | solution.py:494
  102.4 7.4 %collective-permute-start.17 = (bf16[1280,128]{1,0:T(8,128)(2,1)S(1)}, bf16[1280,128]{1,0:T(8,128)(2,1)S(1)}, u32[]{:S(2)}, u32[]{:S(2)}) collective-permute-start(bf16[1280,128]{1,0:T(8,128)(2,1)S(1)} %get-tuple-element.102), channel_id=1, source_target_pairs={{0,32},{1,33},{8,40},{9,41},{16,48},{17,49},{24,56},{25,57},{32,64... | collective-permute-start | bytes 983048 | tf_op jit(solution)/shard_map/ppermute | solution.py:494
  112.8 6.2 %copy-start.4 = (s32[1,2048]{1,0:T(1,128)S(1)}, s32[1,2048]{1,0:T(1,128)}, u32[]{:S(2)}) copy-start(s32[1,2048]{1,0:T(1,128)} %order_ref.1) | copy-start | bytes 24580
  112.9 13.1 %collective-permute-start.22 = (bf16[2304,128]{1,0:T(8,128)(2,1)S(1)}, bf16[2304,128]{1,0:T(8,128)(2,1)S(1)}, u32[]{:S(2)}, u32[]{:S(2)}) collective-permute-start(bf16[2304,128]{1,0:T(8,128)(2,1)S(1)} %pad_maximum_fusion), channel_id=1, source_target_pairs={{0,32},{1,33},{8,40},{9,41},{16,48},{17,49},{24,56},{25,57},{32,64... | collective-permute-start | bytes 1769480 | tf_op jit(solution)/shard_map/ppermute | solution.py:494
  113.0 13.1 %collective-permute-start.20 = (bf16[2048,128]{1,0:T(8,128)(2,1)S(1)}, bf16[2048,128]{1,0:T(8,128)(2,1)S(1)}, u32[]{:S(2)}, u32[]{:S(2)}) collective-permute-start(bf16[2048,128]{1,0:T(8,128)(2,1)S(1)} %get-tuple-element.77), channel_id=1, source_target_pairs={{0,7},{1,4},{8,15},{9,12},{16,23},{17,20},{24,31},{25,28},{32,39},... | collective-permute-start | bytes 1572872 | tf_op jit(solution)/shard_map/ppermute | solution.py:494
  115.4 11.4 %collective-permute-start.23 = (bf16[2048,128]{1,0:T(8,128)(2,1)S(1)}, bf16[2048,128]{1,0:T(8,128)(2,1)S(1)}, u32[]{:S(2)}, u32[]{:S(2)}) collective-permute-start(bf16[2048,128]{1,0:T(8,128)(2,1)S(1)} %pad_maximum_fusion.2), channel_id=1, source_target_pairs={{0,96},{1,97},{8,104},{9,105},{16,112},{17,113},{24,120},{25,121},... | collective-permute-start | bytes 1572872 | tf_op jit(solution)/shard_map/ppermute | solution.py:494
  119.0 10.4 %collective-permute-start.19 = (s32[1,2048]{1,0:T(1,128)S(1)}, s32[1,2048]{1,0:T(1,128)S(1)}, u32[]{:S(2)}, u32[]{:S(2)}) collective-permute-start(s32[1,2048]{1,0:T(1,128)S(1)} %copy-done.4), channel_id=1, source_target_pairs={{0,0},{23,1},{8,8},{31,9},{16,16},{7,17},{24,24},{15,25},{32,32},{... | collective-permute-start | bytes 24584 | tf_op jit(solution)/shard_map/ppermute | solution.py:494
  132.6 13.0 %collective-permute-start.24 = (bf16[768,128]{1,0:T(8,128)(2,1)S(1)}, bf16[768,128]{1,0:T(8,128)(2,1)S(1)}, u32[]{:S(2)}, u32[]{:S(2)}) collective-permute-start(bf16[768,128]{1,0:T(8,128)(2,1)S(1)} %get-tuple-element.83), channel_id=1, source_target_pairs={{0,0},{1,23},{8,8},{9,31},{16,16},{17,7},{24,24},{25,15},{32,32},{... | collective-permute-start | bytes 589832 | tf_op jit(solution)/shard_map/ppermute | solution.py:494
  140.8 4.8 %collective-permute-start.25 = (bf16[768,128]{1,0:T(8,128)(2,1)S(1)}, bf16[768,128]{1,0:T(8,128)(2,1)S(1)}, u32[]{:S(2)}, u32[]{:S(2)}) collective-permute-start(bf16[768,128]{1,0:T(8,128)(2,1)S(1)} %get-tuple-element.84), channel_id=1, source_target_pairs={{0,1},{1,20},{8,9},{9,28},{16,17},{17,4},{24,25},{25,12},{32,33},{... | collective-permute-start | bytes 589832 | tf_op jit(solution)/shard_map/ppermute | solution.py:494
  140.8 11.1 %collective-permute-start.26 = (bf16[768,128]{1,0:T(8,128)(2,1)S(1)}, bf16[768,128]{1,0:T(8,128)(2,1)S(1)}, u32[]{:S(2)}, u32[]{:S(2)}) collective-permute-start(bf16[768,128]{1,0:T(8,128)(2,1)S(1)} %get-tuple-element.85), channel_id=1, source_target_pairs={{0,2},{1,21},{8,10},{9,29},{16,18},{17,5},{24,26},{25,13},{32,34},... | collective-permute-start | bytes 589832 | tf_op jit(solution)/shard_map/ppermute | solution.py:494
  145.5 8.9 %collective-permute-start.27 = (bf16[768,128]{1,0:T(8,128)(2,1)S(1)}, bf16[768,128]{1,0:T(8,128)(2,1)S(1)}, u32[]{:S(2)}, u32[]{:S(2)}) collective-permute-start(bf16[768,128]{1,0:T(8,128)(2,1)S(1)} %get-tuple-element.86), channel_id=1, source_target_pairs={{0,3},{1,22},{8,11},{9,30},{16,19},{17,6},{24,27},{25,14},{32,35},... | collective-permute-start | bytes 589832 | tf_op jit(solution)/shard_map/ppermute | solution.py:494
